TPU v7x, 256 devices: a whole 4x4x8 slice. The times are simulated.
256 devices in a mesh: ctx: 64 (over z, y, x_lo), head: 2 (over core), conv: 2 (over x_hi).
Axes of the slice: x: 4 (x_hi: 2, x_lo: 2; x = x_hi * 2 + x_lo), y: 4, z: 8, core: 2. Of those that a mesh axis runs over, the one named last changes fastest.
Arguments:
- queries: bfloat16 [4, 512, 8192], P('conv', 'ctx', 'head'), parts along dimension 0, may hold values from -100 to 100
- new_keys: bfloat16 [4, 512, 1024], P('conv', 'ctx', 'head'), parts along dimension 0, may hold values from -5.5 to 5.5
- incoming_values: bfloat16 [4, 512, 1024], P('conv', 'ctx', 'head'), parts along dimension 0, may hold values from -6 to 6
- slotted_cache_keys: bfloat16 [4, 256, 128, 1024], P('conv', 'ctx', None, 'head'), parts along dimension 0, may hold values from -6 to 6
- slotted_cache_values: bfloat16 [4, 256, 128, 1024], P('conv', 'ctx', None, 'head'), parts along dimension 0, may hold values from -6 to 6
- lengths: int32 [4], P('conv'), parts along dimension 0, may hold values from 8064 to 32256, as said below
- span_slots: int32 [4, 256], P('conv'), parts along dimension 0, may hold values from 0 to 255, as said below
Outputs:
- attended: bfloat16 [4, 512, 8192], P('conv', 'ctx', 'head'), parts along dimension 0
- cache_keys_out: bfloat16 [4, 256, 128, 1024], P('conv', 'ctx', None, 'head'), parts along dimension 0
- cache_values_out: bfloat16 [4, 256, 128, 1024], P('conv', 'ctx', None, 'head'), parts along dimension 0
There are 2 independent parts, one for each index of `conv`. A program takes and returns all parts, laid end to end along the dimension named above; each array names one. Nothing has to cross between parts.
Inputs may be any that keep to these rules, and one draw needn't show every extreme that they name: `lengths`: in every part one conversation has exactly 32256 cached tokens. `span_slots`: each row is a permutation of the slots. Slot s lies on cycle member s // 4. Span j of a conversation lies on cycle member (j + r) mod (64) in its local slot j // 64, for a rotation r of that conversation.
All inputs are finite; a program needn't handle non-finite values.
Results may differ from a plain program's by a relative error of at most 0.013.
Values may be sent and summed in bfloat16 or wider, within the bound.
No kernel may reach another device: no remote copies, remote signals or barrier semaphores. Data moves between devices by JAX's collectives and lax.ppermute only.
A program may use at most 128 MiB of HBM per device.

v0:
```python
import math

import jax
import jax.numpy as jnp
from jax import lax
from jax.sharding import PartitionSpec as P

HEAD_SIZE = 128


NEG_LARGE = -1e30


def local_softmax(arguments):
    rows_of_queries, keys_head, values_head, limit_rows, places = arguments
    scores = jnp.einsum(
        "rd,sd->rs", rows_of_queries, keys_head, preferred_element_type=jnp.float32
    ) * (1.0 / math.sqrt(rows_of_queries.shape[-1]))
    allowed = places[None, :] <= limit_rows[:, None]
    row_top = jnp.max(jnp.where(allowed, scores, NEG_LARGE), axis=1)
    weights = jnp.where(allowed, jnp.exp(scores - row_top[:, None]), 0.0)
    totals = jnp.sum(weights, axis=1)
    numerator = jnp.dot(
        weights.astype(jnp.bfloat16), values_head, preferred_element_type=jnp.float32
    )
    return (numerator, row_top, totals)


def head_major(rows, kv_local):
    conv_count, row_count, width = rows.shape
    return (
        rows.reshape(conv_count, row_count, kv_local, HEAD_SIZE)
        .transpose(0, 2, 1, 3)
        .reshape(conv_count * kv_local, row_count, HEAD_SIZE)
    )


def attend(rows_of_queries, keys_heads, values_heads, place_heads, limits, kv_local):
    conv_count, row_count, query_width = rows_of_queries.shape
    query_group_size = query_width // (kv_local * HEAD_SIZE)
    stacked = (
        rows_of_queries.reshape(conv_count, row_count, kv_local, query_group_size, HEAD_SIZE)
        .transpose(0, 2, 1, 3, 4)
        .reshape(conv_count * kv_local, row_count * query_group_size, HEAD_SIZE)
    )
    limit_heads = jnp.broadcast_to(
        limits[:, None, :, None], (conv_count, kv_local, row_count, query_group_size)
    ).reshape(conv_count * kv_local, row_count * query_group_size)
    numerator, row_top, totals = lax.map(
        local_softmax, (stacked, keys_heads, values_heads, limit_heads, place_heads)
    )
    numerator = (
        numerator.reshape(conv_count, kv_local, row_count, query_group_size, HEAD_SIZE)
        .transpose(0, 2, 1, 3, 4)
        .reshape(conv_count, row_count, query_width)
    )
    row_top = (
        row_top.reshape(conv_count, kv_local, row_count, query_group_size)
        .transpose(0, 2, 1, 3)
        .reshape(conv_count, row_count, kv_local * query_group_size)
    )
    totals = (
        totals.reshape(conv_count, kv_local, row_count, query_group_size)
        .transpose(0, 2, 1, 3)
        .reshape(conv_count, row_count, kv_local * query_group_size)
    )
    return (numerator, row_top, totals)


def merge_sources(sources):
    numer_parts, top_parts, total_parts = sources
    highest = jnp.max(top_parts, axis=0)
    factor = jnp.exp(top_parts - highest[None])
    denominator = jnp.sum(factor * total_parts, axis=0)
    numer_shape = numer_parts.shape
    scaled = (
        numer_parts.reshape(numer_shape[:-1] + (factor.shape[-1], HEAD_SIZE)) * factor[..., None]
    )
    numerator = jnp.sum(scaled, axis=0).reshape(numer_shape[1:])
    return (numerator, highest, denominator)


def on_device(
    queries,
    new_keys,
    incoming_values,
    slotted_cache_keys,
    slotted_cache_values,
    lengths,
    span_slots,
):
    conv_count, local_rows, query_width = queries.shape
    key_width = new_keys.shape[2]
    per_device = slotted_cache_keys.shape[1]
    span_rows = slotted_cache_keys.shape[2]
    kv_local = key_width // HEAD_SIZE
    query_local = query_width // HEAD_SIZE
    cycle_size = lax.axis_size("ctx")
    member = lax.axis_index("ctx")
    turn_rows = local_rows * cycle_size
    slot_rows = per_device * span_rows
    span_total = span_slots.shape[1]
    turn_keys, turn_values = (
        lax.all_gather(new_keys, "ctx", axis=1, tiled=True),
        lax.all_gather(incoming_values, "ctx", axis=1, tiled=True),
    )
    own_slots = member * per_device + jnp.arange(per_device, dtype=jnp.int32)
    matches = span_slots[:, :, None] == own_slots[None, None, :]
    span_index = jnp.sum(
        jnp.where(matches, jnp.arange(span_total, dtype=jnp.int32)[None, :, None], 0), axis=1
    )
    places = (
        span_index[:, :, None] * span_rows + jnp.arange(span_rows, dtype=jnp.int32)[None, None, :]
    ).reshape(conv_count, slot_rows)
    turn_offset = places - lengths[:, None]
    fresh = (turn_offset >= 0) & (turn_offset < turn_rows)
    source_rows = jnp.clip(turn_offset, 0, turn_rows - 1)[:, :, None]
    keys_now = jnp.where(
        fresh[:, :, None],
        jnp.take_along_axis(turn_keys, source_rows, axis=1),
        slotted_cache_keys.reshape(conv_count, slot_rows, key_width),
    )
    values_now = jnp.where(
        fresh[:, :, None],
        jnp.take_along_axis(turn_values, source_rows, axis=1),
        slotted_cache_values.reshape(conv_count, slot_rows, key_width),
    )
    keys_heads = head_major(keys_now, kv_local)
    values_heads = head_major(values_now, kv_local)
    place_heads = jnp.broadcast_to(places[:, None, :], (conv_count, kv_local, slot_rows)).reshape(
        conv_count * kv_local, slot_rows
    )
    pieces = lax.all_gather(queries, "ctx", axis=1, tiled=True)
    row_count = pieces.shape[1]
    numerator, row_top, totals = attend(
        pieces,
        keys_heads,
        values_heads,
        place_heads,
        lengths[:, None] + jnp.arange(row_count, dtype=jnp.int32)[None, :],
        kv_local,
    )
    numer_all = numerator
    numerator, highest, denominator = merge_sources(
        (
            lax.all_to_all(numer_all[None], "ctx", split_axis=2, concat_axis=0, tiled=True),
            lax.all_to_all(row_top[None], "ctx", split_axis=2, concat_axis=0, tiled=True),
            lax.all_to_all(totals[None], "ctx", split_axis=2, concat_axis=0, tiled=True),
        )
    )
    attended = (
        (numerator.reshape(conv_count, local_rows, query_local, HEAD_SIZE) / denominator[..., None])
        .reshape(conv_count, local_rows, query_width)
        .astype(jnp.bfloat16)
    )
    return (
        attended,
        keys_now.reshape(slotted_cache_keys.shape),
        values_now.reshape(slotted_cache_values.shape),
    )


def solution(mesh):
    in_specs = (
        P("conv", "ctx", "head"),
        P("conv", "ctx", "head"),
        P("conv", "ctx", "head"),
        P("conv", "ctx", None, "head"),
        P("conv", "ctx", None, "head"),
        P("conv"),
        P("conv", None),
    )
    out_specs = (
        P("conv", "ctx", "head"),
        P("conv", "ctx", None, "head"),
        P("conv", "ctx", None, "head"),
    )
    return jax.shard_map(
        on_device, mesh=mesh, in_specs=in_specs, out_specs=out_specs, check_vma=False
    )
```

profile of v0, /device:TPU:4, one launch (start us, length us, event | category | flops | bytes accessed | tf_op | source)
XLA Modules:
  0.0 1439.5 jit_solution(18266960727463212460)
XLA Ops:
  7.9 0.7 all-gather.8.cloned.1.call-update
  9.4 0.9 select_reduce_fusion
  10.4 0.7 and_bitcast_fusion
  11.2 0.7 compare_and_fusion
  12.6 0.7 iota_add_fusion
  13.5 1.2 reshape.212
  14.7 294.6 %all-gather.6.cloned.1.call-done = bf16[2,512,512]{2,1,0:T(8,128)(2,1)} async-done(((bf16[2,8,512]{2,1,0:T(8,128)(2,1)}), bf16[2,512,512]{2,1,0:T(8,128)(2,1)}) %all-gather.6.cloned.1.call-update) | async-done | bytes 1048592 | tf_op jit(solution)/shard_map/all_gather | solution.py:104
  309.3 41.1 %gather_fusion = bf16[1024,512]{1,0:T(8,128)(2,1)S(1)} fusion(bf16[2,512,512]{2,1,0:T(8,128)(2,1)} %all-gather.6.cloned.1.call-done, s32[1024]{0:T(1024)S(1)} %bitcast.112), kind=kCustom, calls=%fused_computation.clone | custom fusion | bytes 2105344 | tf_op jit(solution)/shard_map/jit(take_along_axis)/gather | solution.py:120
  350.4 255.2 %all-gather.8.cloned.1.call-done = bf16[2,512,512]{2,1,0:T(8,128)(2,1)} async-done(((bf16[2,8,512]{2,1,0:T(8,128)(2,1)}), bf16[2,512,512]{2,1,0:T(8,128)(2,1)}) %all-gather.8.cloned.1.call-update) | async-done | bytes 1048592 | tf_op jit(solution)/shard_map/all_gather | solution.py:105
  605.6 41.0 %gather_fusion.1 = bf16[1024,512]{1,0:T(8,128)(2,1)S(1)} fusion(bf16[2,512,512]{2,1,0:T(8,128)(2,1)} %all-gather.8.cloned.1.call-done, s32[1024]{0:T(1024)S(1)} %bitcast.113), kind=kCustom, calls=%fused_computation.1.clone | custom fusion | bytes 2105344 | tf_op jit(solution)/shard_map/jit(take_along_axis)/gather | solution.py:125
  646.6 1.8 bitcast_select_fusion
  648.5 0.9 copy-done.1
  649.9 1.1 pad_maximum_fusion
  650.9 268.0 %all-gather.4.cloned.1.call-done = bf16[2,512,4096]{2,1,0:T(8,128)(2,1)} async-done(((bf16[2,8,4096]{2,1,0:T(8,128)(2,1)}), bf16[2,512,4096]{2,1,0:T(8,128)(2,1)}) %all-gather.4.cloned.1.call-update) | async-done | bytes 8388624 | tf_op jit(solution)/shard_map/all_gather | solution.py:133
  919.0 9.4 copy.50
  928.4 8.1 copy.37
  936.5 78.8 %while.14 = (s32[]{:T(128)}, f32[8,4096,128]{2,1,0:T(8,128)}, f32[8,4096]{1,0:T(8,128)S(1)}, f32[8,4096]{1,0:T(8,128)S(1)}, s32[8,512]{1,0:T(8,128)}, /*index=5*...) while((s32[]{:T(128)}, f32[8,4096,128]{2,1,0:T(8,128)}, ...), condition=%wide.region_4.6_spmd, body=%wide.region_1.5_spmd.sunk | while | flops 1103093760 | bytes 28799100 | solution.py:49
  936.5 0.7 constant_dynamic-slice_fusion.5
  937.3 2.5 fusion.34
  939.8 3.5 fusion.35
  943.4 2.2 fusion.36
  946.4 0.7 constant_dynamic-slice_fusion.5
  947.1 2.5 fusion.34
  949.7 3.5 fusion.35
  953.2 2.2 fusion.36
  956.2 0.7 constant_dynamic-slice_fusion.5
  956.9 2.6 fusion.34
  959.5 3.5 fusion.35
  963.0 2.2 fusion.36
  966.0 0.7 constant_dynamic-slice_fusion.5
  966.7 2.6 fusion.34
  969.3 3.5 fusion.35
  972.8 2.2 fusion.36
  975.8 0.7 constant_dynamic-slice_fusion.5
  976.6 2.6 fusion.34
  979.1 3.6 fusion.35
  982.7 2.2 fusion.36
  985.7 0.7 constant_dynamic-slice_fusion.5
  986.5 2.6 fusion.34
  989.0 3.5 fusion.35
  992.5 2.2 fusion.36
  995.5 0.7 constant_dynamic-slice_fusion.5
  996.3 2.5 fusion.34
  998.8 3.5 fusion.35
  1002.4 2.2 fusion.36
  1005.4 0.7 constant_dynamic-slice_fusion.5
  1006.1 2.6 fusion.34
  1008.7 3.5 fusion.35
  1012.2 2.2 fusion.36
  1015.3 1.1 reshape.220
  1017.3 1.2 reshape.244
  1018.5 6.9 all-to-all-start.1
  1025.4 1.1 reshape.221
  1027.3 1.2 reshape.246
  1028.5 7.8 all-to-all-done.1
  1036.3 4.6 all-to-all-start.2
  1040.9 19.3 %copy.38 = f32[2,512,4,8,128]{1,4,3,2,0:T(8,128)} copy(f32[2,512,4,8,128]{4,3,1,2,0:T(8,128)} %bitcast.116) | data formatting | bytes 33554432 | tf_op jit(solution)/shard_map/transpose | solution.py:54
  1060.2 25.4 %copy.39 = f32[1,2,512,4096]{3,1,0,2:T(2,128)} copy(f32[1,2,512,4096]{2,3,1,0:T(8,128)} %bitcast.114) | data formatting | bytes 33554432 | tf_op jit(solution)/shard_map/broadcast_in_dim;reshape | solution.py:146
  1085.6 11.5 all-to-all-start
  1097.6 0.9 reduce.3
  1099.0 1.0 reduce.2
  1101.3 320.2 %all-to-all-done = f32[1,2,512,4096]{3,1,0,2:T(2,128)} async-done(((f32[1,2,512,4096]{3,1,0,2:T(2,128)}), f32[1,2,512,4096]{3,1,0,2:T(2,128)}, u32[]{:S(2)}, u32[]{:S(2)}) %all-to-all-start) | async-done | bytes 16777248 | tf_op jit(solution)/shard_map/all_to_all | solution.py:146
  1421.5 10.7 fusion.20
  1432.2 0.8 fusion.23
  (60 shorter events, 13.2 us)
Async XLA Ops:
  7.2 302.1 %all-gather.6.cloned.1.call-start = ((), (), s32[]{:S(2)}) async-start(), calls=%async_computation.4 | async-start | bytes 1064960 | tf_op jit(solution)/shard_map/all_gather | solution.py:104
  7.9 597.7 %all-gather.8.cloned.1.call-start = ((), (), s32[]{:S(2)}) async-start(), calls=%async_computation.5 | async-start | bytes 1064960 | tf_op jit(solution)/shard_map/all_gather | solution.py:105
  8.6 910.3 %all-gather.4.cloned.1.call-start = ((), (), s32[]{:S(2)}) async-start(), calls=%async_computation.3 | async-start | bytes 8519680 | tf_op jit(solution)/shard_map/all_gather | solution.py:133
  648.5 1.0 copy-start.1
  648.5 279.9 %copy-start = (bf16[2,512,512]{2,1,0:T(8,128)(2,1)}, bf16[2,512,512]{2,1,0:T(8,128)(2,1)S(1)}, u32[]{:S(2)}) copy-start(bf16[2,512,512]{2,1,0:T(8,128)(2,1)S(1)} %get-tuple-element.90) | copy-start | bytes 3145732
  1018.5 17.8 %all-to-all-start.1 = ((f32[64,1,512]{2,1,0:T(1,128)}), f32[64,1,512]{2,1,0:T(1,128)S(1)}, u32[]{:S(2)}, u32[]{:S(2)}) async-start(f32[64,1,512]{2,1,0:T(1,128)} %reshape.244), calls=%async_computation.1 | async-start | bytes 262144 | tf_op jit(solution)/shard_map/all_to_all | solution.py:147
  1036.3 49.3 %all-to-all-start.2 = ((f32[64,1,512]{2,1,0:T(1,128)}), f32[64,1,512]{2,1,0:T(1,128)S(1)}, u32[]{:S(2)}, u32[]{:S(2)}) async-start(f32[64,1,512]{2,1,0:T(1,128)} %reshape.246), calls=%async_computation.2 | async-start | bytes 262144 | tf_op jit(solution)/shard_map/all_to_all | solution.py:148
  1085.6 335.9 %all-to-all-start = ((f32[1,2,512,4096]{3,1,0,2:T(2,128)}), f32[1,2,512,4096]{3,1,0,2:T(2,128)}, u32[]{:S(2)}, u32[]{:S(2)}) async-start(f32[1,2,512,4096]{3,1,0,2:T(2,128)} %copy.39), calls=%async_computation | async-start | bytes 33554432 | tf_op jit(solution)/shard_map/all_to_all | solution.py:146
Sparse Core Ops, SparseCore 0:
  9.8 299.4 all-gather.5
  311.1 294.4 all-gather.7
  607.4 311.5 all-gather.3
where the time goes:
time: 1450 us; the launch traced here: 1440 us
  waiting for transfers between devices  1150 us (79%)
  local copies, waits for them, and re-layouts  168 us (12%)
  matrix products  48.7 us (3%)
  other arithmetic  36.8 us (3%)
  starting transfers between devices  23.1 us (2%)
    all_to_all x1, waiting for transfers between devices, on_device(): lax.all_to_all(numer_all[None], 'ctx', split_axis=2, concat_axis=0, tiled...  320 us
    all_gather x1, waiting for transfers between devices, on_device(): lax.all_gather(new_keys, 'ctx', axis=1, tiled=True)  295 us
    all_gather x1, waiting for transfers between devices, on_device(): pieces = lax.all_gather(queries, 'ctx', axis=1, tiled=True)  268 us
    all_gather x1, waiting for transfers between devices, on_device(): lax.all_gather(incoming_values, 'ctx', axis=1, tiled=True)  255 us
    gather x1, local copies, waits for them, and re-layouts, on_device(): jnp.take_along_axis(turn_keys, source_rows, axis=1)  41.1 us
    gather x1, local copies, waits for them, and re-layouts, on_device(): jnp.take_along_axis(turn_values, source_rows, axis=1)  41 us
  transfers between devices with their start and end apart: 6, of which 5 were waited for; matrix products, arithmetic and copies ran while one was open for 10% of the time, Pallas kernels for 0%

commit v1 on v0

v1 whole, which is shorter than its diff:
```python
import functools
import math

import jax
import jax.numpy as jnp
from jax import lax
from jax.experimental import pallas as pl
from jax.experimental.pallas import tpu as pltpu
from jax.sharding import Mesh, PartitionSpec as P

HEAD_SIZE = 128
NEG_LARGE = -1e30
SCALE = math.log2(math.e) / math.sqrt(HEAD_SIZE)
F32, BF16 = jnp.float32, jnp.bfloat16
MIB = 2**20
SUM_ROWS = 16


def dot(a, b):
    return jnp.dot(a, b, preferred_element_type=F32)


def pack_kernel(keys_ref, values_ref, out_ref):
    for head in range(out_ref.shape[0]):
        lanes = slice(head * HEAD_SIZE, (head + 1) * HEAD_SIZE)
        out_ref[head, 0, 0] = keys_ref[0, 0, :, lanes]
        out_ref[head, 1, 0] = values_ref[0, 0, :, lanes].T


def pack(cache_keys, cache_values):
    conv_count, slots, span, width = cache_keys.shape
    heads = width // HEAD_SIZE
    spec = pl.BlockSpec((1, 1, span, width), lambda c, s: (c, s, 0, 0))
    return pl.pallas_call(
        pack_kernel,
        grid=(conv_count, slots),
        in_specs=[spec, spec],
        out_specs=pl.BlockSpec((heads, 2, 1, span, HEAD_SIZE), lambda c, s: (c, 0, s, 0, 0)),
        out_shape=jax.ShapeDtypeStruct((conv_count * heads, 2, slots, span, HEAD_SIZE), BF16),
        name="pack",
    )(cache_keys, cache_values)


def attend_kernel(group, turn_part, scalars, q_ref, kv_ref, new_ref, o_ref, keys, sums):
    step = pl.program_id(0)
    sources, _, slots, span, _ = kv_ref.shape
    blocks = sources * slots
    cached = blocks * span
    length, me, good = scalars[blocks], scalars[blocks + 1], scalars[blocks + 2]

    @pl.when(step == 0)
    def _():
        filler = kv_ref[good, 0, 0, 0:16, :].astype(F32)[0:1]
        for s in range(sources):
            for j in range(slots):
                n = s * slots + j
                base = scalars[n]
                at = slice(n * span, (n + 1) * span)
                rows = lax.broadcasted_iota(jnp.int32, (span, HEAD_SIZE), 0) + base < length
                cols = lax.broadcasted_iota(jnp.int32, (HEAD_SIZE, span), 1) + base < length
                keys[at, :] = jnp.where(rows, kv_ref[s, 0, j].astype(F32), filler).astype(BF16)
                sums[0:HEAD_SIZE, at] = jnp.where(cols, kv_ref[s, 1, j].astype(F32), 0.0).astype(BF16)
                sums[HEAD_SIZE:, at] = jnp.where(cols[:SUM_ROWS], 1.0, 0.0).astype(BF16)
        keys[cached:, :] = new_ref[0:turn_part, :]
        sums[0:HEAD_SIZE, cached:] = new_ref[turn_part:, :].T
        sums[HEAD_SIZE:, cached:] = jnp.ones((SUM_ROWS, turn_part), BF16)

    chunks, _, width = q_ref.shape
    columns = chunks * width
    q = jnp.concatenate([q_ref[c] for c in range(chunks)], axis=1)
    top = jnp.full((1, columns), NEG_LARGE, F32)
    total = jnp.zeros((HEAD_SIZE + SUM_ROWS, columns), F32)
    tile = 512
    for j in range(0, cached + 1, tile):
        if j < cached:
            at = slice(j, j + tile)
            scores = dot(keys[at, :], q) * SCALE
        else:
            at = slice(cached, cached + turn_part)
            scores = dot(keys[at, :], q) * SCALE
            shape = scores.shape
            lane = lax.broadcasted_iota(jnp.int32, shape, 1)
            chunk = lane // width
            part = lax.rem(me + step * chunks + chunk, group)
            token = part * turn_part + (lane - chunk * width) // (width // turn_part)
            place = me * turn_part + lax.broadcasted_iota(jnp.int32, shape, 0)
            scores = jnp.where(place <= token, scores, NEG_LARGE)
        higher = jnp.maximum(top, jnp.max(scores, axis=0, keepdims=True))
        weights = jnp.exp2(scores - higher).astype(BF16)
        total = total * jnp.exp2(top - higher) + dot(sums[:, at], weights)
        top = higher
    denominator = total[HEAD_SIZE : HEAD_SIZE + 1]
    out = (total[:HEAD_SIZE] * (1.0 / denominator)).astype(BF16)
    level = top + jnp.log2(denominator)
    first = level.astype(BF16)
    rest = level - first.astype(F32)
    second = rest.astype(BF16)
    third = (rest - second.astype(F32)).astype(BF16)
    row = lax.broadcasted_iota(jnp.int32, (SUM_ROWS, columns), 0)
    coded = jnp.where(
        row == 0, first.astype(F32), jnp.where(row == 1, second.astype(F32), third.astype(F32))
    ).astype(BF16)
    for c in range(chunks):
        o_ref[c, 0:HEAD_SIZE] = out[:, c * width : (c + 1) * width]
        o_ref[c, HEAD_SIZE:] = coded[:, c * width : (c + 1) * width]


def attend(scalars, chunks, kv, new, group, turn_part):
    count, _, width = chunks.shape
    width = width - 128
    per_step = 2
    cached = kv.shape[0] * kv.shape[2] * kv.shape[3]
    whole = lambda i, s: (0, 0, 0, 0, 0)
    return pl.pallas_call(
        functools.partial(attend_kernel, group, turn_part),
        grid_spec=pltpu.PrefetchScalarGridSpec(
            num_scalar_prefetch=1,
            grid=(count // per_step,),
            in_specs=[
                pl.BlockSpec((per_step, HEAD_SIZE, width), lambda i, s: (i, 0, 0)),
                pl.BlockSpec(kv.shape, whole),
                pl.BlockSpec(new.shape, lambda i, s: (0, 0)),
            ],
            out_specs=pl.BlockSpec(
                (per_step, HEAD_SIZE + SUM_ROWS, width), lambda i, s: (i, 0, 0)
            ),
            scratch_shapes=[
                pltpu.VMEM((cached + turn_part, HEAD_SIZE), BF16),
                pltpu.VMEM((HEAD_SIZE + SUM_ROWS, cached + turn_part), BF16),
            ],
        ),
        out_shape=jax.ShapeDtypeStruct((count, HEAD_SIZE + SUM_ROWS, width), BF16),
        compiler_params=pltpu.CompilerParams(vmem_limit_bytes=40 * MIB),
        cost_estimate=pl.CostEstimate(
            flops=4 * HEAD_SIZE * count * width * cached,
            bytes_accessed=5 * MIB,
            transcendentals=count * width * cached,
        ),
        name="attend",
    )(scalars, chunks, kv, new)


def merge_kernel(*refs):
    parts, out_ref = refs[:-1], refs[-1]
    levels = []
    for part in parts:
        coded = part[HEAD_SIZE:].astype(F32)
        levels.append(coded[0:1] + coded[1:2] + coded[2:3])
    top = functools.reduce(jnp.maximum, levels)
    shares = [jnp.exp2(level - top) for level in levels]
    over = 1.0 / functools.reduce(jnp.add, shares)
    out = functools.reduce(
        jnp.add,
        [part[:HEAD_SIZE].astype(F32) * (share * over) for part, share in zip(parts, shares)],
    )
    out_ref[...] = out.T.astype(BF16)


def merge(parts):
    width = parts[0].shape[1]
    return pl.pallas_call(
        merge_kernel,
        out_shape=jax.ShapeDtypeStruct((width, HEAD_SIZE), BF16),
        name="merge",
    )(*parts)


def shift(x, axis, size, by):
    return lax.ppermute(x, axis, [(i, (i + by) % size) for i in range(size)])


def gather_ring(x, axis, size):
    held = {0: x}
    for step in range(1, size // 2):
        held[size - step] = shift(held[(size - step + 1) % size], axis, size, 1)
        held[step] = shift(held[step - 1], axis, size, -1)
    half = x.shape[0] // 2
    below = shift(held[size // 2 + 1][:half], axis, size, 1)
    above = shift(held[size // 2 - 1][half:], axis, size, -1)
    held[size // 2] = jnp.concatenate([below, above], axis=0)
    return jnp.stack([held[i] for i in range(size)])


def on_device(rows, columns, queries, new_keys, new_values, cache_keys, cache_values, lengths, span_slots):
    convs, tokens, query_width = queries.shape
    heads = new_keys.shape[2] // HEAD_SIZE
    per_head = query_width // (heads * HEAD_SIZE)
    slots, span = cache_keys.shape[1:3]
    pairs = convs * heads
    cycle = rows * columns
    turn_part = columns * tokens
    turn = rows * turn_part
    z, b = lax.axis_index("z"), lax.axis_index("b")

    kv = lax.all_to_all(pack(cache_keys, cache_values), "b", 0, 0, tiled=True)

    def by_pair(x, inner):
        return (
            x.reshape(convs, tokens, heads, inner, HEAD_SIZE)
            .transpose(0, 2, 1, 3, 4)
            .reshape(pairs, tokens * inner, HEAD_SIZE)
        )

    turn_rows = jnp.concatenate(
        [by_pair(queries, per_head), by_pair(new_keys, 1), by_pair(new_values, 1)], axis=1
    )
    turn_rows = lax.all_to_all(turn_rows, "b", 0, 0, tiled=True)
    q_rows = tokens * per_head
    own_q = turn_rows[:, :q_rows].reshape(columns * q_rows, HEAD_SIZE)
    own_new = turn_rows[:, q_rows:].reshape(columns, 2, tokens, HEAD_SIZE)
    own_new = own_new.transpose(1, 0, 2, 3).reshape(2 * turn_part, HEAD_SIZE)
    chunks = gather_ring(jnp.concatenate([own_q.T, own_new], axis=1), "z", rows)

    rotation = span_slots[:, 0] // slots
    conv = b // heads
    length = lengths[conv]
    member = z * columns + jnp.arange(columns, dtype=jnp.int32)
    first_span = jnp.mod(member - rotation[conv], cycle)
    bases = (first_span[:, None] + cycle * jnp.arange(slots, dtype=jnp.int32)) * span
    good = jnp.where(bases[0, 0] < length, 0, 1)
    scalars = jnp.concatenate([bases.reshape(-1), jnp.stack([length, z, good])]).astype(jnp.int32)

    parts = attend(scalars, chunks, kv, own_new, rows, turn_part)

    def turn_slot(members, conv_length, conv_rotation):
        spans = jnp.mod(members - conv_rotation, cycle)
        at = (conv_length // span - spans + cycle - 1) // cycle
        at = jnp.clip(at, 0, slots - 1)
        return at, (spans + at * cycle) * span - conv_length

    all_new = jnp.roll(chunks[:, :, q_rows * columns :], z, axis=0)
    all_new = all_new.reshape(rows, 2, turn_part, HEAD_SIZE)
    all_new = all_new.transpose(0, 2, 1, 3).reshape(turn, 2 * HEAD_SIZE)
    padded = jnp.pad(all_new, ((span, span), (0, 0)))
    _, starts = turn_slot(member, length, rotation[conv])
    starts = jnp.clip(starts + span, 0, turn + span)
    windows = jnp.stack(
        [lax.dynamic_slice(padded, (starts[i], 0), (span, 2 * HEAD_SIZE)) for i in range(columns)]
    )
    windows = lax.all_to_all(windows, "b", 0, 0, tiled=True)
    windows = windows.reshape(convs, heads, span, 2, HEAD_SIZE).transpose(3, 0, 2, 1, 4)
    windows = windows.reshape(2, convs, 1, span, heads * HEAD_SIZE)
    slot, start = turn_slot(z * columns + b, lengths, rotation)
    token = start[:, None] + jnp.arange(span, dtype=jnp.int32)
    fresh = (token >= 0) & (token < turn)
    here = jnp.arange(slots, dtype=jnp.int32)[None, :] == slot[:, None]
    fresh = (fresh[:, None, :] & here[:, :, None])[..., None]
    keys_out = jnp.where(fresh, windows[0], cache_keys)
    values_out = jnp.where(fresh, windows[1], cache_values)

    received = [parts[0]] + [shift(parts[i], "z", rows, i) for i in range(1, rows)]
    done = merge(received).reshape(columns, q_rows, HEAD_SIZE)
    done = lax.all_to_all(done, "b", 0, 0, tiled=True)
    attended = (
        done.reshape(convs, heads, tokens, per_head, HEAD_SIZE)
        .transpose(0, 2, 1, 3, 4)
        .reshape(convs, tokens, query_width)
    )
    return attended, keys_out, values_out


def solution(mesh):
    members, heads, convs = mesh.devices.shape
    columns = 8
    rows = members // columns
    grid = Mesh(mesh.devices.reshape(rows, columns, heads, convs), ("z", "b", "head", "conv"))
    ctx = ("z", "b")
    turn = P("conv", ctx, "head")
    cache = P("conv", ctx, None, "head")
    return jax.shard_map(
        functools.partial(on_device, rows, columns),
        mesh=grid,
        in_specs=(turn, turn, turn, cache, cache, P("conv"), P("conv", None)),
        out_specs=(turn, cache, cache),
        check_vma=False,
    )
```

time: 1450 us -> 163 us (0.11)
  waiting for transfers between devices: 1150 us -> 32.6 us
  local copies, waits for them, and re-layouts: 168 us -> 16.2 us
  matrix products: 48.7 us -> 0 us
  Pallas kernels: 0 us -> 35.3 us
  other arithmetic: 36.8 us -> 7.82 us
  starting transfers between devices: 23.1 us -> 49.6 us
    all_gather x3 -> x0, waiting for transfers between devices: 818 us -> none  [the longest x1 295 us: on_device(): lax.all_gather(new_keys, 'ctx', axis=1, tiled=True)]
    all_to_all x3 -> x4, waiting for transfers between devices: 328 us -> 5.09 us  [the longest x1 5.08 us: on_device(): done = lax.all_to_all(done, 'b', 0, 0, tiled=True)]
    gather x2 -> x0, local copies, waits for them, and re-layouts: 82.1 us -> none  [the longest x1 41.1 us: on_device(): jnp.take_along_axis(turn_keys, source_rows, axis=1)]
    dot_general x16 -> x0, matrix products: 48.7 us -> none  [the longest x8 28.3 us: local_softmax(): jnp.dot(weights.astype(jnp.bfloat16), values_head, preferred_element_type...]
    pallas_call x0 -> x3, Pallas kernels: none -> 35.3 us  [the longest x1 26.8 us: attend(): pl.pallas_call(functools.partial(attend_kernel, group, turn_part), grid_s...]
    reduce_sum x11 -> x0, other arithmetic: 28.9 us -> none  [the longest x8 17.3 us: local_softmax(): totals = jnp.sum(weights, axis=1)]
    ppermute x0 -> x15, waiting for transfers between devices: none -> 27.5 us  [shift(): return lax.ppermute(x, axis, [(i, (i + by) % size) for i in range(size)])]
    ppermute x0 -> x15, starting transfers between devices: none -> 27.4 us  [shift(): return lax.ppermute(x, axis, [(i, (i + by) % size) for i in range(size)])]
  transfers between devices with their start and end apart: 6 -> 19, of which waited for: 5 -> 10; matrix products, arithmetic and copies ran while one was open for 10% -> 13% of each run, Pallas kernels for 0% -> 20%
where the time goes in v1:
time: 163 us; the launch traced here: 161 us
  starting transfers between devices  49.6 us (30%)
  Pallas kernels  35.3 us (22%)
  waiting for transfers between devices  32.6 us (20%)
  between operations  20 us (12%)
  local copies, waits for them, and re-layouts  16.2 us (10%)
  other arithmetic  7.82 us (5%)
    ppermute x15, waiting for transfers between devices, shift(): return lax.ppermute(x, axis, [(i, (i + by) % size) for i in range(size)])  27.5 us
    ppermute x15, starting transfers between devices, shift(): return lax.ppermute(x, axis, [(i, (i + by) % size) for i in range(size)])  27.4 us
    pallas_call x1, Pallas kernels, attend(): pl.pallas_call(functools.partial(attend_kernel, group, turn_part), grid_s...  26.8 us
    unnamed x24, local copies, waits for them, and re-layouts  6.98 us
    pallas_call x1, Pallas kernels, pack(): pl.pallas_call(pack_kernel, grid=(conv_count, slots), in_specs=[spec, spe...  6.16 us
    all_to_all x1, starting transfers between devices, on_device(): windows = lax.all_to_all(windows, 'b', 0, 0, tiled=True)  6 us
    all_to_all x1, starting transfers between devices, on_device(): kv = lax.all_to_all(pack(cache_keys, cache_values), 'b', 0, 0, tiled=True)  5.67 us
    all_to_all x1, starting transfers between devices, on_device(): done = lax.all_to_all(done, 'b', 0, 0, tiled=True)  5.42 us
  transfers between devices with their start and end apart: 19, of which 10 were waited for; matrix products, arithmetic and copies ran while one was open for 13% of the time, Pallas kernels for 20%

profile of v1, /device:TPU:4, one launch (start us, length us, event | category | flops | bytes accessed | tf_op | source)
XLA Modules:
  0.0 161.5 jit_solution(17658796405935255659)
XLA Ops:
  0.6 0.9 copy.32
  1.6 1.4 pad_maximum_fusion
  3.0 5.1 %all-to-all-start = ((bf16[8,80,128]{2,1,0:T(8,128)(2,1)}), bf16[8,80,128]{2,1,0:T(8,128)(2,1)S(1)}, u32[]{:S(2)}, u32[]{:S(2)}) async-start(bf16[8,80,128]{2,1,0:T(8,128)(2,1)} %pad_maximum_fusion), calls=%async_computation | async-start | bytes 327680 | tf_op jit(solution)/shard_map/all_to_all | solution.py:207
  8.1 1.2 dynamic_slice.36
  12.0 0.8 slice_reduce_fusion
  12.8 0.6 dynamic_slice.35
  13.4 0.7 multiply_subtract_fusion
  14.1 0.1 iota_compare_fusion
  14.2 1.3 add_clamp_fusion
  15.5 0.1 add_multiply_fusion
  15.5 0.1 compare_and_fusion
  15.6 0.5 slice.78
  16.1 0.1 mul.37
  17.5 6.2 %pack.1 = bf16[8,2,4,128,128]{4,3,2,1,0:T(8,128)(2,1)} custom-call(bf16[2,4,128,512]{3,2,1,0:T(8,128)(2,1)} %keys_ref.1, bf16[2,4,128,512]{3,2,1,0:T(8,128)(2,1)} %values_ref.1), custom_call_target="tpu_custom_call" | custom-call | tf_op jit(solution)/shard_map/pack/pallas_call | solution.py:34
  23.7 0.7 fusion.23
  24.4 5.7 %all-to-all-start.1 = ((bf16[8,2,4,128,128]{4,3,2,1,0:T(8,128)(2,1)}), bf16[8,2,4,128,128]{4,3,2,1,0:T(8,128)(2,1)S(1)}, u32[]{:S(2)}, u32[]{:S(2)}) async-start(bf16[8,2,4,128,128]{4,3,2,1,0:T(8,128)(2,1)} %pack.1), calls=%async_computation.1 | async-start | bytes 4194304 | tf_op jit(solution)/shard_map/all_to_all | solution.py:195
  30.1 0.1 copy.20
  30.2 0.0 copy-start.2
  30.2 0.7 pad_maximum_fusion.1
  30.9 5.9 %collective-permute-start = (bf16[128,640]{1,0:T(8,128)(2,1)}, bf16[128,640]{1,0:T(8,128)(2,1)}, u32[]{:S(2)}, u32[]{:S(2)}) collective-permute-start(bf16[128,640]{1,0:T(8,128)(2,1)} %pad_maximum_fusion.1), channel_id=1, source_target_pairs={{0,224},{32,0},{64,32},{96,64},{128,96},{160,128},{192,160},{224,1... | collective-permute-start | bytes 491528 | tf_op jit(solution)/shard_map/ppermute | solution.py:169
  36.8 0.7 pad_add_fusion.scalars
  52.6 0.9 bitcast_dynamic-update-slice_fusion.6
  53.6 3.3 %collective-permute-start.1 = (bf16[128,640]{1,0:T(8,128)(2,1)}, bf16[128,640]{1,0:T(8,128)(2,1)S(1)}, u32[]{:S(2)}, u32[]{:S(2)}) collective-permute-start(bf16[128,640]{1,0:T(8,128)(2,1)} %collective-permute-done), channel_id=1, source_target_pairs={{0,224},{32,0},{64,32},{96,64},{128,96},{160,128},{192,160},{224,1... | collective-permute-start | bytes 491528 | tf_op jit(solution)/shard_map/ppermute | solution.py:169
  56.9 1.0 bitcast_dynamic-update-slice_fusion.5
  57.9 2.2 %collective-permute-done.1 = bf16[128,640]{1,0:T(8,128)(2,1)S(1)} collective-permute-done((bf16[128,640]{1,0:T(8,128)(2,1)}, bf16[128,640]{1,0:T(8,128)(2,1)S(1)}, u32[]{:S(2)}, u32[]{:S(2)}) %collective-permute-start.1) | collective-permute-done | bytes 163872 | tf_op jit(solution)/shard_map/ppermute | solution.py:169
  60.0 3.6 %collective-permute-start.2 = (bf16[128,640]{1,0:T(8,128)(2,1)S(1)}, bf16[128,640]{1,0:T(8,128)(2,1)S(1)}, u32[]{:S(2)}, u32[]{:S(2)}) collective-permute-start(bf16[128,640]{1,0:T(8,128)(2,1)S(1)} %collective-permute-done.1), channel_id=1, source_target_pairs={{0,224},{32,0},{64,32},{96,64},{128,96},{160,128},{192,160},{224,1... | collective-permute-start | bytes 491528 | tf_op jit(solution)/shard_map/ppermute | solution.py:169
  63.7 2.8 %collective-permute-done.2 = bf16[128,640]{1,0:T(8,128)(2,1)S(1)} collective-permute-done((bf16[128,640]{1,0:T(8,128)(2,1)S(1)}, bf16[128,640]{1,0:T(8,128)(2,1)S(1)}, u32[]{:S(2)}, u32[]{:S(2)}) %collective-permute-start.2) | collective-permute-done | bytes 163872 | tf_op jit(solution)/shard_map/ppermute | solution.py:169
  66.5 3.8 %collective-permute-start.7 = (bf16[64,640]{1,0:T(8,128)(2,1)S(1)}, bf16[64,640]{1,0:T(8,128)(2,1)S(1)}, u32[]{:S(2)}, u32[]{:S(2)}) collective-permute-start(bf16[64,640]{1,0:T(8,128)(2,1)S(1)} %slice.105), channel_id=1, source_target_pairs={{0,224},{32,0},{64,32},{96,64},{128,96},{160,128},{192,160},{224,1... | collective-permute-start | bytes 245768 | tf_op jit(solution)/shard_map/ppermute | solution.py:169
  70.3 0.1 collective-permute-start.6
  70.4 1.9 %collective-permute-done.7 = bf16[64,640]{1,0:T(8,128)(2,1)S(1)} collective-permute-done((bf16[64,640]{1,0:T(8,128)(2,1)S(1)}, bf16[64,640]{1,0:T(8,128)(2,1)S(1)}, u32[]{:S(2)}, u32[]{:S(2)}) %collective-permute-start.7) | collective-permute-done | bytes 81952 | tf_op jit(solution)/shard_map/ppermute | solution.py:169
  72.3 3.7 %collective-permute-done.6 = bf16[64,640]{1,0:T(8,128)(2,1)S(1)} collective-permute-done((bf16[64,640]{1,0:T(8,128)(2,1)S(1)}, bf16[64,640]{1,0:T(8,128)(2,1)S(1)}, u32[]{:S(2)}, u32[]{:S(2)}) %collective-permute-start.6) | collective-permute-done | bytes 81952 | tf_op jit(solution)/shard_map/ppermute | solution.py:169
  76.1 0.9 bitcast_dynamic-update-slice_fusion.q_ref
  77.1 0.1 fusion
  77.2 0.3 copy.23
  77.5 0.7 fusion.3
  78.2 0.7 fusion.5
  78.9 0.7 fusion.7
  79.6 0.7 fusion.9
  80.4 0.7 fusion.11
  81.1 0.7 fusion.13
  81.8 0.7 fusion.15
  82.5 0.7 fusion.17
  83.2 6.0 %all-to-all-start.3 = ((bf16[8,128,256]{2,1,0:T(8,128)(2,1)}), bf16[8,128,256]{2,1,0:T(8,128)(2,1)}, u32[]{:S(2)}, u32[]{:S(2)}) async-start(bf16[8,128,256]{2,1,0:T(8,128)(2,1)} %fusion.17), calls=%async_computation.3 | async-start | bytes 1048576 | tf_op jit(solution)/shard_map/all_to_all | solution.py:240
  89.2 26.8 %attend.1 = bf16[8,144,512]{2,1,0:T(8,128)(2,1)S(1)} custom-call(s32[35]{0:T(128)S(1)} %pad_add_fusion.scalars, bf16[8,128,640]{2,1,0:T(8,128)(2,1)S(1)} %bitcast_dynamic-update-slice_fusion.q_ref, bf16[8,2,4,128,128]{4,3,2,1,0:T(8,128)(2,1)S(1)} %all-to-all-done.1.kv_ref, bf16[128,128]{1,0:T(8,128)(2,1)S(1)} %bitcast.126), custom_call_target="tpu_custom_call" | custom-call | flops 8589934592 | bytes 5242880 | tf_op jit(solution)/shard_map/attend/pallas_call | solution.py:114
  116.0 0.9 slice_bitcast_fusion
  116.9 0.1 broadcast_and_fusion
  117.0 1.3 copy.24
  118.3 1.9 %collective-permute-start.10 = (bf16[144,512]{1,0:T(8,128)(2,1)}, bf16[144,512]{1,0:T(8,128)(2,1)}, u32[]{:S(2)}, u32[]{:S(2)}) collective-permute-start(bf16[144,512]{1,0:T(8,128)(2,1)} %get-tuple-element.13), channel_id=1, source_target_pairs={{0,96},{32,128},{64,160},{96,192},{128,224},{160,0},{192,32},{224,... | collective-permute-start | bytes 442376 | tf_op jit(solution)/shard_map/ppermute | solution.py:169
  120.2 4.7 %collective-permute-start.11 = (bf16[144,512]{1,0:T(8,128)(2,1)}, bf16[144,512]{1,0:T(8,128)(2,1)}, u32[]{:S(2)}, u32[]{:S(2)}) collective-permute-start(bf16[144,512]{1,0:T(8,128)(2,1)} %get-tuple-element.12), channel_id=1, source_target_pairs={{0,128},{32,160},{64,192},{96,224},{128,0},{160,32},{192,64},{224,... | collective-permute-start | bytes 442376 | tf_op jit(solution)/shard_map/ppermute | solution.py:169
  124.8 2.2 %collective-permute-start.12 = (bf16[144,512]{1,0:T(8,128)(2,1)}, bf16[144,512]{1,0:T(8,128)(2,1)}, u32[]{:S(2)}, u32[]{:S(2)}) collective-permute-start(bf16[144,512]{1,0:T(8,128)(2,1)} %get-tuple-element.11), channel_id=1, source_target_pairs={{0,160},{32,192},{64,224},{96,0},{128,32},{160,64},{192,96},{224,1... | collective-permute-start | bytes 442376 | tf_op jit(solution)/shard_map/ppermute | solution.py:169
  127.0 2.1 %collective-permute-start.13 = (bf16[144,512]{1,0:T(8,128)(2,1)S(1)}, bf16[144,512]{1,0:T(8,128)(2,1)}, u32[]{:S(2)}, u32[]{:S(2)}) collective-permute-start(bf16[144,512]{1,0:T(8,128)(2,1)S(1)} %get-tuple-element.10), channel_id=1, source_target_pairs={{0,192},{32,224},{64,0},{96,32},{128,64},{160,96},{192,128},{224,1... | collective-permute-start | bytes 442376 | tf_op jit(solution)/shard_map/ppermute | solution.py:169
  129.1 7.1 %collective-permute-done.9.refs_2_ = bf16[144,512]{1,0:T(8,128)(2,1)S(1)} collective-permute-done((bf16[144,512]{1,0:T(8,128)(2,1)S(1)}, bf16[144,512]{1,0:T(8,128)(2,1)S(1)}, u32[]{:S(2)}, u32[]{:S(2)}) %collective-permute-start.9) | collective-permute-done | bytes 147488 | tf_op jit(solution)/shard_map/ppermute | solution.py:169
  136.2 0.0 copy-start
  136.2 0.1 copy.26
  136.4 0.1 copy.25
  136.5 1.7 %collective-permute-done.11.refs_4_ = bf16[144,512]{1,0:T(8,128)(2,1)} collective-permute-done((bf16[144,512]{1,0:T(8,128)(2,1)}, bf16[144,512]{1,0:T(8,128)(2,1)}, u32[]{:S(2)}, u32[]{:S(2)}) %collective-permute-start.11) | collective-permute-done | bytes 147488 | tf_op jit(solution)/shard_map/ppermute | solution.py:169
  138.2 2.9 %collective-permute-done.12.refs_5_ = bf16[144,512]{1,0:T(8,128)(2,1)} collective-permute-done((bf16[144,512]{1,0:T(8,128)(2,1)}, bf16[144,512]{1,0:T(8,128)(2,1)}, u32[]{:S(2)}, u32[]{:S(2)}) %collective-permute-start.12) | collective-permute-done | bytes 147488 | tf_op jit(solution)/shard_map/ppermute | solution.py:169
  141.1 3.5 %collective-permute-done.13.refs_6_ = bf16[144,512]{1,0:T(8,128)(2,1)} collective-permute-done((bf16[144,512]{1,0:T(8,128)(2,1)S(1)}, bf16[144,512]{1,0:T(8,128)(2,1)}, u32[]{:S(2)}, u32[]{:S(2)}) %collective-permute-start.13) | collective-permute-done | bytes 147488 | tf_op jit(solution)/shard_map/ppermute | solution.py:169
  144.6 1.7 %collective-permute-done.14.refs_7_ = bf16[144,512]{1,0:T(8,128)(2,1)} collective-permute-done((bf16[144,512]{1,0:T(8,128)(2,1)S(1)}, bf16[144,512]{1,0:T(8,128)(2,1)}, u32[]{:S(2)}, u32[]{:S(2)}) %collective-permute-start.14) | collective-permute-done | bytes 147488 | tf_op jit(solution)/shard_map/ppermute | solution.py:169
  146.3 2.3 %merge.1 = bf16[512,128]{1,0:T(8,128)(2,1)} custom-call(bf16[144,512]{1,0:T(8,128)(2,1)} %get-tuple-element.16.refs_0_, bf16[144,512]{1,0:T(8,128)(2,1)} %copy-done.3, bf16[144,512]{1,0:T(8,128)(2,1)} %copy-done.4, bf16[144,512]{1,0:T(8,128)(2,1)} %collective-permute-done.10.refs_3_, bf16[144,512]{1,0:T(8,128)(2,1)} %collective-permute-done.11.refs_4_, ...), custom_call_target="tpu_custom_call" | custom-call | tf_op jit(solution)/shard_map/merge/pallas_call | solution.py:161
  148.7 5.4 %all-to-all-start.2 = ((bf16[8,64,128]{2,1,0:T(8,128)(2,1)}), bf16[8,64,128]{2,1,0:T(8,128)(2,1)S(1)}, u32[]{:S(2)}, u32[]{:S(2)}) async-start(bf16[8,64,128]{2,1,0:T(8,128)(2,1)} %bitcast.142), calls=%async_computation.2 | async-start | bytes 262144 | tf_op jit(solution)/shard_map/all_to_all | solution.py:253
  154.1 1.6 broadcast_select_fusion
  155.7 5.1 %all-to-all-done.2 = bf16[8,64,128]{2,1,0:T(8,128)(2,1)S(1)} async-done(((bf16[8,64,128]{2,1,0:T(8,128)(2,1)}), bf16[8,64,128]{2,1,0:T(8,128)(2,1)S(1)}, u32[]{:S(2)}, u32[]{:S(2)}) %all-to-all-start.2) | async-done | bytes 131104 | tf_op jit(solution)/shard_map/all_to_all | solution.py:253
  160.8 0.7 copy.22
  (39 shorter events, 0.4 us)
Async XLA Ops:
  3.0 21.4 %all-to-all-start = ((bf16[8,80,128]{2,1,0:T(8,128)(2,1)}), bf16[8,80,128]{2,1,0:T(8,128)(2,1)S(1)}, u32[]{:S(2)}, u32[]{:S(2)}) async-start(bf16[8,80,128]{2,1,0:T(8,128)(2,1)} %pad_maximum_fusion), calls=%async_computation | async-start | bytes 327680 | tf_op jit(solution)/shard_map/all_to_all | solution.py:207
  24.4 58.8 %all-to-all-start.1 = ((bf16[8,2,4,128,128]{4,3,2,1,0:T(8,128)(2,1)}), bf16[8,2,4,128,128]{4,3,2,1,0:T(8,128)(2,1)S(1)}, u32[]{:S(2)}, u32[]{:S(2)}) async-start(bf16[8,2,4,128,128]{4,3,2,1,0:T(8,128)(2,1)} %pack.1), calls=%async_computation.1 | async-start | bytes 4194304 | tf_op jit(solution)/shard_map/all_to_all | solution.py:195
  30.2 6.6 %copy-start.2 = (bf16[512,128]{0,1:T(8,128)(2,1)}, bf16[512,128]{0,1:T(8,128)(2,1)S(1)}, u32[]{:S(2)}) copy-start(bf16[512,128]{0,1:T(8,128)(2,1)S(1)} %copy.20) | copy-start | bytes 393220
  30.9 22.7 %collective-permute-start = (bf16[128,640]{1,0:T(8,128)(2,1)}, bf16[128,640]{1,0:T(8,128)(2,1)}, u32[]{:S(2)}, u32[]{:S(2)}) collective-permute-start(bf16[128,640]{1,0:T(8,128)(2,1)} %pad_maximum_fusion.1), channel_id=1, source_target_pairs={{0,224},{32,0},{64,32},{96,64},{128,96},{160,128},{192,160},{224,1... | collective-permute-start | bytes 491528 | tf_op jit(solution)/shard_map/ppermute | solution.py:169
  36.8 20.1 %collective-permute-start.3 = (bf16[128,640]{1,0:T(8,128)(2,1)}, bf16[128,640]{1,0:T(8,128)(2,1)}, u32[]{:S(2)}, u32[]{:S(2)}) collective-permute-start(bf16[128,640]{1,0:T(8,128)(2,1)} %pad_maximum_fusion.1), channel_id=1, source_target_pairs={{0,32},{32,64},{64,96},{96,128},{128,160},{160,192},{192,224},{224... | collective-permute-start | bytes 491528 | tf_op jit(solution)/shard_map/ppermute | solution.py:169
  53.6 6.5 %collective-permute-start.1 = (bf16[128,640]{1,0:T(8,128)(2,1)}, bf16[128,640]{1,0:T(8,128)(2,1)S(1)}, u32[]{:S(2)}, u32[]{:S(2)}) collective-permute-start(bf16[128,640]{1,0:T(8,128)(2,1)} %collective-permute-done), channel_id=1, source_target_pairs={{0,224},{32,0},{64,32},{96,64},{128,96},{160,128},{192,160},{224,1... | collective-permute-start | bytes 491528 | tf_op jit(solution)/shard_map/ppermute | solution.py:169
  56.9 6.7 %collective-permute-start.4 = (bf16[128,640]{1,0:T(8,128)(2,1)}, bf16[128,640]{1,0:T(8,128)(2,1)S(1)}, u32[]{:S(2)}, u32[]{:S(2)}) collective-permute-start(bf16[128,640]{1,0:T(8,128)(2,1)} %collective-permute-done.3), channel_id=1, source_target_pairs={{0,32},{32,64},{64,96},{96,128},{128,160},{160,192},{192,224},{224... | collective-permute-start | bytes 491528 | tf_op jit(solution)/shard_map/ppermute | solution.py:169
  60.0 6.4 %collective-permute-start.2 = (bf16[128,640]{1,0:T(8,128)(2,1)S(1)}, bf16[128,640]{1,0:T(8,128)(2,1)S(1)}, u32[]{:S(2)}, u32[]{:S(2)}) collective-permute-start(bf16[128,640]{1,0:T(8,128)(2,1)S(1)} %collective-permute-done.1), channel_id=1, source_target_pairs={{0,224},{32,0},{64,32},{96,64},{128,96},{160,128},{192,160},{224,1... | collective-permute-start | bytes 491528 | tf_op jit(solution)/shard_map/ppermute | solution.py:169
  63.6 6.6 %collective-permute-start.5 = (bf16[128,640]{1,0:T(8,128)(2,1)S(1)}, bf16[128,640]{1,0:T(8,128)(2,1)S(1)}, u32[]{:S(2)}, u32[]{:S(2)}) collective-permute-start(bf16[128,640]{1,0:T(8,128)(2,1)S(1)} %collective-permute-done.4), channel_id=1, source_target_pairs={{0,32},{32,64},{64,96},{96,128},{128,160},{160,192},{192,224},{224... | collective-permute-start | bytes 491528 | tf_op jit(solution)/shard_map/ppermute | solution.py:169
  66.5 5.8 %collective-permute-start.7 = (bf16[64,640]{1,0:T(8,128)(2,1)S(1)}, bf16[64,640]{1,0:T(8,128)(2,1)S(1)}, u32[]{:S(2)}, u32[]{:S(2)}) collective-permute-start(bf16[64,640]{1,0:T(8,128)(2,1)S(1)} %slice.105), channel_id=1, source_target_pairs={{0,224},{32,0},{64,32},{96,64},{128,96},{160,128},{192,160},{224,1... | collective-permute-start | bytes 245768 | tf_op jit(solution)/shard_map/ppermute | solution.py:169
  70.3 5.7 %collective-permute-start.6 = (bf16[64,640]{1,0:T(8,128)(2,1)S(1)}, bf16[64,640]{1,0:T(8,128)(2,1)S(1)}, u32[]{:S(2)}, u32[]{:S(2)}) collective-permute-start(bf16[64,640]{1,0:T(8,128)(2,1)S(1)} %slice.104), channel_id=1, source_target_pairs={{0,32},{32,64},{64,96},{96,128},{128,160},{160,192},{192,224},{224... | collective-permute-start | bytes 245768 | tf_op jit(solution)/shard_map/ppermute | solution.py:169
  83.2 33.8 %all-to-all-start.3 = ((bf16[8,128,256]{2,1,0:T(8,128)(2,1)}), bf16[8,128,256]{2,1,0:T(8,128)(2,1)}, u32[]{:S(2)}, u32[]{:S(2)}) async-start(bf16[8,128,256]{2,1,0:T(8,128)(2,1)} %fusion.17), calls=%async_computation.3 | async-start | bytes 1048576 | tf_op jit(solution)/shard_map/all_to_all | solution.py:240
  116.9 10.1 %collective-permute-start.8 = (bf16[144,512]{1,0:T(8,128)(2,1)S(1)}, bf16[144,512]{1,0:T(8,128)(2,1)S(1)}, u32[]{:S(2)}, u32[]{:S(2)}) collective-permute-start(bf16[144,512]{1,0:T(8,128)(2,1)S(1)} %get-tuple-element.15), channel_id=1, source_target_pairs={{0,32},{32,64},{64,96},{96,128},{128,160},{160,192},{192,224},{224... | collective-permute-start | bytes 442376 | tf_op jit(solution)/shard_map/ppermute | solution.py:169
  116.9 19.3 %collective-permute-start.9 = (bf16[144,512]{1,0:T(8,128)(2,1)S(1)}, bf16[144,512]{1,0:T(8,128)(2,1)S(1)}, u32[]{:S(2)}, u32[]{:S(2)}) collective-permute-start(bf16[144,512]{1,0:T(8,128)(2,1)S(1)} %get-tuple-element.14), channel_id=1, source_target_pairs={{0,64},{32,96},{64,128},{96,160},{128,192},{160,224},{192,0},{224,... | collective-permute-start | bytes 442376 | tf_op jit(solution)/shard_map/ppermute | solution.py:169
  118.3 18.2 %collective-permute-start.10 = (bf16[144,512]{1,0:T(8,128)(2,1)}, bf16[144,512]{1,0:T(8,128)(2,1)}, u32[]{:S(2)}, u32[]{:S(2)}) collective-permute-start(bf16[144,512]{1,0:T(8,128)(2,1)} %get-tuple-element.13), channel_id=1, source_target_pairs={{0,96},{32,128},{64,160},{96,192},{128,224},{160,0},{192,32},{224,... | collective-permute-start | bytes 442376 | tf_op jit(solution)/shard_map/ppermute | solution.py:169
  120.2 18.1 %collective-permute-start.11 = (bf16[144,512]{1,0:T(8,128)(2,1)}, bf16[144,512]{1,0:T(8,128)(2,1)}, u32[]{:S(2)}, u32[]{:S(2)}) collective-permute-start(bf16[144,512]{1,0:T(8,128)(2,1)} %get-tuple-element.12), channel_id=1, source_target_pairs={{0,128},{32,160},{64,192},{96,224},{128,0},{160,32},{192,64},{224,... | collective-permute-start | bytes 442376 | tf_op jit(solution)/shard_map/ppermute | solution.py:169
  124.8 16.3 %collective-permute-start.12 = (bf16[144,512]{1,0:T(8,128)(2,1)}, bf16[144,512]{1,0:T(8,128)(2,1)}, u32[]{:S(2)}, u32[]{:S(2)}) collective-permute-start(bf16[144,512]{1,0:T(8,128)(2,1)} %get-tuple-element.11), channel_id=1, source_target_pairs={{0,160},{32,192},{64,224},{96,0},{128,32},{160,64},{192,96},{224,1... | collective-permute-start | bytes 442376 | tf_op jit(solution)/shard_map/ppermute | solution.py:169
  127.0 19.3 %copy-start.3 = (bf16[144,512]{1,0:T(8,128)(2,1)}, bf16[144,512]{1,0:T(8,128)(2,1)S(1)}, u32[]{:S(2)}) copy-start(bf16[144,512]{1,0:T(8,128)(2,1)S(1)} %collective-permute-done.8.refs_1_) | copy-start | bytes 442372
  127.0 17.6 %collective-permute-start.13 = (bf16[144,512]{1,0:T(8,128)(2,1)S(1)}, bf16[144,512]{1,0:T(8,128)(2,1)}, u32[]{:S(2)}, u32[]{:S(2)}) collective-permute-start(bf16[144,512]{1,0:T(8,128)(2,1)S(1)} %get-tuple-element.10), channel_id=1, source_target_pairs={{0,192},{32,224},{64,0},{96,32},{128,64},{160,96},{192,128},{224,1... | collective-permute-start | bytes 442376 | tf_op jit(solution)/shard_map/ppermute | solution.py:169
  136.1 10.2 %copy-start.4 = (bf16[144,512]{1,0:T(8,128)(2,1)}, bf16[144,512]{1,0:T(8,128)(2,1)S(1)}, u32[]{:S(2)}) copy-start(bf16[144,512]{1,0:T(8,128)(2,1)S(1)} %collective-permute-done.9.refs_2_) | copy-start | bytes 442372
  136.1 10.2 %collective-permute-start.14 = (bf16[144,512]{1,0:T(8,128)(2,1)S(1)}, bf16[144,512]{1,0:T(8,128)(2,1)}, u32[]{:S(2)}, u32[]{:S(2)}) collective-permute-start(bf16[144,512]{1,0:T(8,128)(2,1)S(1)} %get-tuple-element.9), channel_id=1, source_target_pairs={{0,224},{32,0},{64,32},{96,64},{128,96},{160,128},{192,160},{224,1... | collective-permute-start | bytes 442376 | tf_op jit(solution)/shard_map/ppermute | solution.py:169
  136.2 17.9 %copy-start = (bf16[2,4,128,512]{3,2,1,0:T(8,128)(2,1)S(1)}, bf16[2,4,128,512]{3,2,1,0:T(8,128)(2,1)}, u32[]{:S(2)}) copy-start(bf16[2,4,128,512]{3,2,1,0:T(8,128)(2,1)} %keys_ref.1) | copy-start | bytes 3145732
  136.2 17.9 %copy-start.1 = (bf16[2,4,128,512]{3,2,1,0:T(8,128)(2,1)S(1)}, bf16[2,4,128,512]{3,2,1,0:T(8,128)(2,1)}, u32[]{:S(2)}) copy-start(bf16[2,4,128,512]{3,2,1,0:T(8,128)(2,1)} %values_ref.1) | copy-start | bytes 3145732
  148.7 12.1 %all-to-all-start.2 = ((bf16[8,64,128]{2,1,0:T(8,128)(2,1)}), bf16[8,64,128]{2,1,0:T(8,128)(2,1)S(1)}, u32[]{:S(2)}, u32[]{:S(2)}) async-start(bf16[8,64,128]{2,1,0:T(8,128)(2,1)} %bitcast.142), calls=%async_computation.2 | async-start | bytes 262144 | tf_op jit(solution)/shard_map/all_to_all | solution.py:253

commit v2 on v0

v2 whole, which is shorter than its diff:
```python
import functools
import math

import jax
import jax.numpy as jnp
from jax import lax
from jax.experimental import pallas as pl
from jax.experimental.pallas import tpu as pltpu
from jax.sharding import Mesh, PartitionSpec as P

HEAD = 128
LOWEST = -1e30
SCALE = math.log2(math.e) / math.sqrt(HEAD)
F32, BF16, I32 = jnp.float32, jnp.bfloat16, jnp.int32
MIB = 2**20
EXTRA = 16
TILE = 512
COLUMNS = 8
SMEM = pl.BlockSpec(memory_space=pltpu.SMEM)
VMEM = pl.BlockSpec(memory_space=pltpu.VMEM)
ANY = pl.BlockSpec(memory_space=pl.ANY)

def dot(a, b):
    return jnp.dot(a, b, preferred_element_type=F32)


def shift(a, by, size=8):
    return lax.ppermute(a, "z", [(i, (i + by) % size) for i in range(size)])


def pack_turn_kernel(q_ref, k_ref, v_ref, out_ref):
    convs, tokens, width = q_ref.shape
    heads = k_ref.shape[2] // HEAD
    group = width // (heads * HEAD)
    for c in range(convs):
        for h in range(heads):
            pieces = []
            for g in range(group):
                at = (h * group + g) * HEAD
                pieces.append(q_ref[c, :, at : at + HEAD])
            pieces.append(k_ref[c, :, h * HEAD : (h + 1) * HEAD])
            pieces.append(v_ref[c, :, h * HEAD : (h + 1) * HEAD])
            out_ref[c * heads + h] = jnp.concatenate(pieces, axis=0)


def pack_turn(queries, new_keys, new_values):
    convs, tokens, width = queries.shape
    heads = new_keys.shape[2] // HEAD
    rows = tokens * (width // (heads * HEAD) + 2)
    return pl.pallas_call(
        pack_turn_kernel,
        in_specs=[VMEM] * 3,
        out_specs=VMEM,
        out_shape=jax.ShapeDtypeStruct((convs * heads, rows, HEAD), BF16),
        compiler_params=pltpu.CompilerParams(vmem_limit_bytes=6 * MIB),
        name="pack_turn",
    )(queries, new_keys, new_values)


def ring_message_kernel(rows_ref, out_ref, new_ref):
    columns, count, _ = rows_ref.shape
    tokens = 8
    q_rows = count - 2 * tokens
    q = jnp.concatenate([rows_ref[s, 0:q_rows] for s in range(columns)], axis=0)
    keys = [rows_ref[s, q_rows : q_rows + tokens] for s in range(columns)]
    values = [rows_ref[s, q_rows + tokens :] for s in range(columns)]
    new = jnp.concatenate(keys + values, axis=0)
    out_ref[:, 0 : columns * q_rows] = q.T
    out_ref[:, columns * q_rows :] = new
    new_ref[...] = new


def ring_message(rows):
    columns, count, _ = rows.shape
    width = columns * (count - 16)
    return pl.pallas_call(
        ring_message_kernel,
        in_specs=[VMEM],
        out_specs=[VMEM, VMEM],
        out_shape=[
            jax.ShapeDtypeStruct((HEAD, width + HEAD), BF16),
            jax.ShapeDtypeStruct((HEAD, HEAD), BF16),
        ],
        compiler_params=pltpu.CompilerParams(vmem_limit_bytes=6 * MIB),
        name="ring_message",
    )(rows)


def pack_cache_kernel(keys_ref, values_ref, *rest):
    outs, sems = rest[:-1], rest[-1]
    convs, slots, _, width = keys_ref.shape
    heads = width // HEAD
    per_out = slots // len(outs)
    copies = []
    for c in range(convs):
        for h in range(heads):
            for i, ref in enumerate((keys_ref, values_ref)):
                for n, out in enumerate(outs):
                    held = pl.ds(n * per_out, per_out)
                    copy = pltpu.make_async_copy(
                        ref.at[c, held, :, pl.ds(h * HEAD, HEAD)],
                        out.at[c * heads + h, i],
                        sems.at[len(copies)],
                    )
                    copy.start()
                    copies.append(copy)
    for copy in copies:
        copy.wait()


def pack_cache(cache_keys, cache_values, count):
    convs, slots, span, width = cache_keys.shape
    pairs = convs * width // HEAD
    return pl.pallas_call(
        pack_cache_kernel,
        in_specs=[ANY, ANY],
        out_specs=[VMEM] * count,
        out_shape=[jax.ShapeDtypeStruct((pairs, 2, slots // count, span, HEAD), BF16)] * count,
        scratch_shapes=[pltpu.SemaphoreType.DMA((2 * pairs * count,))],
        compiler_params=pltpu.CompilerParams(vmem_limit_bytes=8 * MIB),
        name="pack_cache",
    )(cache_keys, cache_values)


def prepare_kernel(first_slot, cycle, place, lengths, slots_ref, kv, *refs):
    rest, keys, sums = refs[:-2], refs[-2], refs[-1]
    sources, _, slots, span, _ = kv.shape
    all_slots = slots_ref.shape[1] // cycle
    z, b = place[0], place[1]
    conv = b // (COLUMNS // 2)
    length = lengths[conv]
    rotation = slots_ref[conv, 0] // all_slots
    cached = sources * slots * span

    def base(source, slot):
        member = z * COLUMNS + source
        return (slot * cycle + lax.rem(member - rotation + cycle, cycle)) * span

    if rest:
        new_ref, known = rest
        filler = known[0:16, :].astype(F32)[0:1]
    else:
        first = kv[0, 0, 0, 0:16, :].astype(F32)[0:1]
        second = kv[1, 0, 0, 0:16, :].astype(F32)[0:1]
        filler = jnp.where(base(0, 0) < length, first, second)
    for source in range(sources):
        for slot in range(slots):
            left = length - base(source, first_slot + slot)
            start = (source * slots + slot) * span
            at = slice(start, start + span)
            rows = lax.broadcasted_iota(I32, (span, HEAD), 0) < left
            cols = lax.broadcasted_iota(I32, (HEAD, span), 1) < left
            keys[at, :] = jnp.where(rows, kv[source, 0, slot].astype(F32), filler).astype(BF16)
            turned = kv[source, 1, slot].T.astype(F32)
            sums[0:HEAD, at] = jnp.where(cols, turned, 0.0).astype(BF16)
            sums[HEAD:, at] = jnp.where(cols[:EXTRA], 1.0, 0.0).astype(BF16)
    if rest:
        turn_part = new_ref.shape[0] // 2
        keys[cached:, :] = new_ref[0:turn_part, :]
        sums[0:HEAD, cached:] = new_ref[turn_part:, :].T
        sums[HEAD:, cached:] = jnp.ones((EXTRA, turn_part), BF16)


def prepare(place, lengths, span_slots, first_slot, kv, cycle, new=None, known=None):
    positions = kv.shape[0] * kv.shape[2] * kv.shape[3]
    rest = []
    if new is not None:
        positions += new.shape[0] // 2
        rest = [new, known]
    return pl.pallas_call(
        functools.partial(prepare_kernel, first_slot, cycle),
        in_specs=[SMEM] * 3 + [VMEM] * (1 + len(rest)),
        out_specs=[VMEM] * 2,
        out_shape=[
            jax.ShapeDtypeStruct((positions, HEAD), BF16),
            jax.ShapeDtypeStruct((HEAD + EXTRA, positions), BF16),
        ],
        compiler_params=pltpu.CompilerParams(vmem_limit_bytes=12 * MIB),
        name="prepare",
    )(place, lengths, span_slots, kv, *rest)


def level_of(part):
    coded = part[HEAD:].astype(F32)
    return coded[0:1] + coded[1:2] + coded[2:3]


def combine(parts):
    levels = [level_of(part) for part in parts]
    top = functools.reduce(jnp.maximum, levels)
    shares = [jnp.exp2(level - top) for level in levels]
    total = functools.reduce(jnp.add, shares)
    sums = functools.reduce(
        jnp.add, [part[:HEAD].astype(F32) * share for part, share in zip(parts, shares)]
    )
    return sums, total, top


def attend_kernel(parts, distances, inits, with_new, *refs):
    count = len(distances)
    place, refs = refs[0], refs[1:]
    q_refs, refs = refs[:count], refs[count:]
    init_refs, refs = refs[: sum(inits)], refs[sum(inits) :]
    keys, sums, outs = refs[0], refs[1], refs[2:]
    width = outs[0].shape[1]
    columns = count * width
    turn_part = width // 8
    cached = keys.shape[0] - with_new * turn_part
    z = place[0]

    q = jnp.concatenate([ref[:, 0:width] for ref in q_refs], axis=1).astype(F32) * SCALE
    high = q.astype(BF16)
    low = (q - high.astype(F32)).astype(BF16)
    q = jnp.concatenate([high, low], axis=0)
    tops, totals, at_init = [], [], 0
    for given in inits:
        if given:
            held, weight, level = combine(init_refs[at_init : at_init + given])
            at_init += given
            tops.append(level)
            totals.append(
                jnp.concatenate([held, jnp.broadcast_to(weight, (EXTRA, width))], axis=0)
            )
        else:
            tops.append(jnp.full((1, width), LOWEST, F32))
            totals.append(jnp.zeros((HEAD + EXTRA, width), F32))
    top = jnp.concatenate(tops, axis=1)
    total = jnp.concatenate(totals, axis=1)
    tiles = [slice(j, j + TILE) for j in range(0, cached, TILE)]
    if with_new:
        tiles.append(slice(cached, cached + turn_part))

    def scores_of(at):
        twice = jnp.concatenate([keys[at, :]] * 2, axis=1)
        scores = dot(twice, q)
        if at.start < cached:
            return scores
        row = lax.broadcasted_iota(I32, (turn_part, width), 0)
        lane = lax.broadcasted_iota(I32, (turn_part, width), 1)
        token = (lane // 64) * 8 + lax.rem(lane, 8)
        ahead = jnp.concatenate(
            [row - token + (z - lax.rem(z + d, parts)) * turn_part for d in distances], axis=1
        )
        return jnp.where(ahead <= 0, scores, LOWEST)

    scores = scores_of(tiles[0])
    for n, at in enumerate(tiles):
        following = scores_of(tiles[n + 1]) if n + 1 < len(tiles) else None
        higher = jnp.maximum(top, jnp.max(scores, axis=0, keepdims=True))
        weights = jnp.exp2(scores - higher).astype(BF16)
        total = total * jnp.exp2(top - higher) + dot(sums[:, at], weights)
        top, scores = higher, following
    denominator = total[HEAD : HEAD + 1]
    out = (total[:HEAD] * (1.0 / denominator)).astype(BF16)
    level = top + jnp.log2(denominator)
    first = level.astype(BF16).astype(F32)
    second = (level - first).astype(BF16).astype(F32)
    third = level - first - second
    row = lax.broadcasted_iota(I32, (EXTRA, columns), 0)
    coded = jnp.where(row == 0, first, jnp.where(row == 1, second, third)).astype(BF16)
    for c in range(count):
        at = slice(c * width, (c + 1) * width)
        outs[c][0:HEAD] = out[:, at]
        outs[c][HEAD:] = coded[:, at]


def attend(place, kv, chunks, distances, inits, parts, with_new):
    keys, sums = kv
    count = len(distances)
    width = chunks[0].shape[1] - HEAD
    given = [part for init in inits for part in init]
    return pl.pallas_call(
        functools.partial(attend_kernel, parts, distances, [len(i) for i in inits], with_new),
        in_specs=[SMEM] + [VMEM] * (count + len(given) + 2),
        out_specs=[VMEM] * count,
        out_shape=[jax.ShapeDtypeStruct((HEAD + EXTRA, width), BF16)] * count,
        compiler_params=pltpu.CompilerParams(vmem_limit_bytes=16 * MIB),
        cost_estimate=pl.CostEstimate(
            flops=8 * HEAD * count * width * keys.shape[0],
            bytes_accessed=3 * MIB,
            transcendentals=count * width * keys.shape[0],
        ),
        name="attend",
    )(place, *chunks, *given, keys, sums)


def merge_kernel(*refs):
    parts, out_ref = refs[:-1], refs[-1]
    sums, total, _ = combine(parts)
    turned = (sums * (1.0 / total)).astype(BF16).T
    columns, rows, _ = out_ref.shape
    for s in range(columns):
        out_ref[s] = turned[s * rows : (s + 1) * rows]


def merge(parts):
    width = parts[0].shape[1]
    return pl.pallas_call(
        merge_kernel,
        in_specs=[VMEM] * len(parts),
        out_specs=VMEM,
        out_shape=jax.ShapeDtypeStruct((COLUMNS, width // COLUMNS, HEAD), BF16),
        compiler_params=pltpu.CompilerParams(vmem_limit_bytes=8 * MIB),
        name="merge",
    )(*parts)


def unpack_kernel(rows_ref, out_ref):
    convs, tokens, width = out_ref.shape
    pairs, rows, _ = rows_ref.shape
    heads, group = pairs // convs, rows // tokens
    for c in range(convs):
        for h in range(heads):
            for g in range(group):
                at = (h * group + g) * HEAD
                piece = rows_ref[c * heads + h, g * tokens : (g + 1) * tokens]
                out_ref[c, :, at : at + HEAD] = piece


def unpack(rows, shape):
    return pl.pallas_call(
        unpack_kernel,
        out_shape=jax.ShapeDtypeStruct(shape, BF16),
        compiler_params=pltpu.CompilerParams(vmem_limit_bytes=6 * MIB),
        name="unpack",
    )(rows)


def turn_slot(length, rotation, member, slots, cycle, span):
    j = lax.rem(member - rotation + cycle, cycle)
    slot = jnp.clip((length // span - j + cycle - 1) // cycle, 0, slots - 1)
    return slot, (j + slot * cycle) * span - length


def windows_kernel(slots, span, cycle, place, lengths, slots_ref, *refs):
    chunks, out_ref, rows = refs[:-2], refs[-2], refs[-1]
    parts = len(chunks)
    width = chunks[0].shape[1] - HEAD
    turn_part = HEAD // 2
    turn = parts * turn_part
    z, b = place[0], place[1]
    conv = b // (COLUMNS // 2)
    rotation = slots_ref[conv, 0] // slots
    edge = jnp.zeros((span, 2 * HEAD), F32)
    rows[0:span] = edge
    rows[span + turn : turn + 2 * span] = edge
    rows[turn + 2 * span :] = edge[0:8]
    for d, chunk in enumerate(chunks):
        start = pl.multiple_of(span + lax.rem(z + d, parts) * turn_part, turn_part)
        rows[pl.ds(start, turn_part), 0:HEAD] = chunk[0:turn_part, width:].astype(F32)
        rows[pl.ds(start, turn_part), HEAD:] = chunk[turn_part:, width:].astype(F32)
    for to in range(COLUMNS):
        _, token = turn_slot(lengths[conv], rotation, z * COLUMNS + to, slots, cycle, span)
        start = jnp.clip(token + span, 0, turn + span)
        whole = pl.multiple_of(start // 8 * 8, 8)
        window = rows[pl.ds(whole, span + 8), :]
        window = pltpu.roll(window, lax.rem(span + 8 + whole - start, span + 8), 0)
        window = window[0:span].astype(BF16)
        out_ref[to, 0:span] = window[:, 0:HEAD]
        out_ref[to, span:] = window[:, HEAD:]


def windows(place, lengths, span_slots, chunks, slots, span, cycle):
    turn = len(chunks) * HEAD // 2
    return pl.pallas_call(
        functools.partial(windows_kernel, slots, span, cycle),
        in_specs=[SMEM] * 3 + [VMEM] * len(chunks),
        out_specs=VMEM,
        out_shape=jax.ShapeDtypeStruct((COLUMNS, 2 * span, HEAD), BF16),
        scratch_shapes=[pltpu.VMEM((turn + 2 * span + 8, 2 * HEAD), F32)],
        compiler_params=pltpu.CompilerParams(vmem_limit_bytes=8 * MIB),
        name="windows",
    )(place, lengths, span_slots, *chunks)


def write_kernel(turn, cycle, place, lengths, slots_ref, new_ref, k_ref, v_ref, ko_ref, vo_ref):
    conv = pl.program_id(0)
    _, slots, span, width = k_ref.shape
    heads = width // HEAD
    member = place[0] * COLUMNS + place[1]
    rotation = slots_ref[conv, 0] // slots
    slot, token = turn_slot(lengths[conv], rotation, member, slots, cycle, span)
    ko_ref[...] = k_ref[...]
    vo_ref[...] = v_ref[...]

    @pl.when((token > -span) & (token < turn))
    def _():
        row = lax.broadcasted_iota(I32, (span, HEAD), 0) + token
        inside = (row >= 0) & (row < turn)
        for h in range(heads):
            lanes = slice(h * HEAD, (h + 1) * HEAD)
            for i, (old, out) in enumerate(((k_ref, ko_ref), (v_ref, vo_ref))):
                new = new_ref[h, i * span : (i + 1) * span].astype(F32)
                kept = old[0, slot, :, lanes].astype(F32)
                out[0, slot, :, lanes] = jnp.where(inside, new, kept).astype(BF16)


def write(place, lengths, span_slots, new, cache_keys, cache_values, turn, cycle):
    convs, slots, span, width = cache_keys.shape
    spec = pl.BlockSpec((1, slots, span, width), lambda c: (c, 0, 0, 0))
    new_block = (new.shape[0] // convs,) + new.shape[1:]
    shape = jax.ShapeDtypeStruct(cache_keys.shape, BF16)
    return pl.pallas_call(
        functools.partial(write_kernel, turn, cycle),
        grid=(convs,),
        in_specs=[SMEM] * 3 + [pl.BlockSpec(new_block, lambda c: (c, 0, 0)), spec, spec],
        out_specs=[spec, spec],
        out_shape=[shape, shape],
        compiler_params=pltpu.CompilerParams(vmem_limit_bytes=12 * MIB),
        cost_estimate=pl.CostEstimate(flops=0, bytes_accessed=5 * MIB, transcendentals=0),
        name="write",
    )(place, lengths, span_slots, new, cache_keys, cache_values)


def on_device(parts, queries, new_keys, new_values, cache_keys, cache_values, lengths, span_slots):
    _, slots, span, _ = cache_keys.shape
    cycle = parts * COLUMNS
    place = jnp.stack([lax.axis_index("z"), lax.axis_index("b")]).astype(I32)
    tie = lax.optimization_barrier

    turn_rows = pack_turn(queries, new_keys, new_values)
    turn_rows, cache_k, cache_v = tie((turn_rows, cache_keys, cache_values))
    turn_rows = lax.all_to_all(turn_rows, "b", 0, 0, tiled=True)
    first, second = pack_cache(cache_k, cache_v, 2)
    turn_rows, first, second = tie((turn_rows, first, second))
    first = lax.all_to_all(first, "b", 0, 0, tiled=True)

    message, new = ring_message(turn_rows)
    chunks = [None] * parts
    chunks[0] = message
    half = message.shape[0] // 2

    def run(kv, distances, inits=None, after=()):
        held = [chunks[d] for d in distances]
        if after:
            held, _ = tie((held, after))
        inits = inits or [()] * len(distances)
        return attend(place, kv, held, distances, inits, parts, kv is far)

    far = None
    chunks[7], chunks[1] = shift(message, 1), shift(message, -1)
    second, first, chunks[7], chunks[1] = tie((second, first, chunks[7], chunks[1]))
    second = lax.all_to_all(second, "b", 0, 0, tiled=True)
    chunks[6], chunks[2] = shift(chunks[7], 1), shift(chunks[1], -1)
    near = prepare(place, lengths, span_slots, 0, first, cycle)
    own, a1, a7 = run(near, (0, 1, 7))
    chunks[6], chunks[2], own = tie((chunks[6], chunks[2], own))
    chunks[5], chunks[3] = shift(chunks[6], 1), shift(chunks[2], -1)
    a2, a6 = run(near, (2, 6))
    chunks[5], chunks[3], a2 = tie((chunks[5], chunks[3], a2))
    below, above = shift(chunks[5][:half], 1), shift(chunks[3][half:], -1)
    a3, a5 = run(near, (3, 5))
    below, above, a3, second = tie((below, above, a3, second))
    far = prepare(place, lengths, span_slots, slots // 2, second, cycle, new, near[0])
    chunks[4] = jnp.concatenate([below, above], axis=0)
    (a4,) = run(near, (4,))
    rows = windows(place, lengths, span_slots, chunks, slots, span, cycle)
    a4, rows = tie((a4, rows))

    up4, up3 = run(far, (4, 3), ((a4,), (a3,)))
    down3, own = run(far, (5, 0), ((a5,), (own,)), after=(up4,))
    up4, up3 = shift(up4, 2), shift(up3, 2)
    up2, down2 = run(far, (2, 6), ((a2, up4), (a6,)), after=(down3,))
    rows, _ = tie((rows, up2))
    rows = lax.all_to_all(rows, "b", 0, 0, tiled=True)
    down3 = shift(down3, -2)
    up1, down1 = run(far, (1, 7), ((a1, up3), (a7, down3)), after=(up2,))
    up2, down2 = shift(up2, 2), shift(down2, -2)
    up1, down1 = shift(up1, 1), shift(down1, -1)
    own, rows = tie((own, rows))
    done = merge([own, up2, down2, up1, down1])
    done = lax.all_to_all(done, "b", 0, 0, tiled=True)
    attended = unpack(done, queries.shape)
    keys_out, values_out = write(
        place, lengths, span_slots, rows, cache_keys, cache_values, parts * HEAD // 2, cycle
    )
    return attended, keys_out, values_out


def solution(mesh):
    members, heads, convs = mesh.devices.shape
    parts = members // COLUMNS
    grid = Mesh(mesh.devices.reshape(parts, COLUMNS, heads, convs), ("z", "b", "head", "conv"))
    ctx = ("z", "b")
    turn = P("conv", ctx, "head")
    cache = P("conv", ctx, None, "head")
    return jax.shard_map(
        functools.partial(on_device, parts),
        mesh=grid,
        in_specs=(turn, turn, turn, cache, cache, P("conv"), P("conv", None)),
        out_specs=(turn, cache, cache),
        check_vma=False,
    )
```

time: 1450 us -> 130 us (0.09)
  waiting for transfers between devices: 1150 us -> 24.3 us
  local copies, waits for them, and re-layouts: 168 us -> 11.8 us
  matrix products: 48.7 us -> 0 us
  Pallas kernels: 0 us -> 38 us
  other arithmetic: 36.8 us -> 0.08 us
  starting transfers between devices: 23.1 us -> 53.5 us
    all_gather x3 -> x0, waiting for transfers between devices: 818 us -> none  [the longest x1 295 us: on_device(): lax.all_gather(new_keys, 'ctx', axis=1, tiled=True)]
    all_to_all x3 -> x5, waiting for transfers between devices: 328 us -> 9.44 us  [the longest x1 4.69 us: on_device(): done = lax.all_to_all(done, 'b', 0, 0, tiled=True)]
    gather x2 -> x0, local copies, waits for them, and re-layouts: 82.1 us -> none  [the longest x1 41.1 us: on_device(): jnp.take_along_axis(turn_keys, source_rows, axis=1)]
    dot_general x16 -> x0, matrix products: 48.7 us -> none  [the longest x8 28.3 us: local_softmax(): jnp.dot(weights.astype(jnp.bfloat16), values_head, preferred_element_type...]
    pallas_call x0 -> x17, Pallas kernels: none -> 38 us  [the longest x8 28.1 us: attend(): pl.pallas_call(functools.partial(attend_kernel, parts, distances, [len(i)...]
    ppermute x0 -> x15, starting transfers between devices: none -> 29.9 us  [shift(): return lax.ppermute(a, 'z', [(i, (i + by) % size) for i in range(size)])]
    reduce_sum x11 -> x0, other arithmetic: 28.9 us -> none  [the longest x8 17.3 us: local_softmax(): totals = jnp.sum(weights, axis=1)]
    another operation x4 -> x0, local copies, waits for them, and re-layouts: 26.2 us -> none  [the longest x1 25.4 us: on_device(): numer_all[None]]
  transfers between devices with their start and end apart: 6 -> 20, of which waited for: 5 -> 10; matrix products, arithmetic and copies ran while one was open for 10% -> 0% of each run, Pallas kernels for 0% -> 21%
where the time goes in v2:
time: 130 us; the launch traced here: 129 us
  starting transfers between devices  53.5 us (41%)
  Pallas kernels  38 us (29%)
  waiting for transfers between devices  24.3 us (19%)
  local copies, waits for them, and re-layouts  11.8 us (9%)
    ppermute x15, starting transfers between devices, shift(): return lax.ppermute(a, 'z', [(i, (i + by) % size) for i in range(size)])  29.9 us
    pallas_call x8, Pallas kernels, attend(): pl.pallas_call(functools.partial(attend_kernel, parts, distances, [len(i)...  28.1 us
    ppermute x15, waiting for transfers between devices, shift(): return lax.ppermute(a, 'z', [(i, (i + by) % size) for i in range(size)])  14.8 us
    unnamed x67, local copies, waits for them, and re-layouts  11.8 us
    all_to_all x1, starting transfers between devices, on_device(): rows = lax.all_to_all(rows, 'b', 0, 0, tiled=True)  5.73 us
    all_to_all x1, starting transfers between devices, on_device(): done = lax.all_to_all(done, 'b', 0, 0, tiled=True)  5.7 us
    all_to_all x1, starting transfers between devices, on_device(): turn_rows = lax.all_to_all(turn_rows, 'b', 0, 0, tiled=True)  5.1 us
    all_to_all x1, waiting for transfers between devices, on_device(): done = lax.all_to_all(done, 'b', 0, 0, tiled=True)  4.69 us
  transfers between devices with their start and end apart: 20, of which 10 were waited for; matrix products, arithmetic and copies ran while one was open for 0% of the time, Pallas kernels for 21%

profile of v2, /device:TPU:4, one launch (start us, length us, event | category | flops | bytes accessed | tf_op | source)
XLA Modules:
  0.0 128.7 jit_solution(11399078001450206961)
XLA Ops:
  0.6 0.9 copy-done.6
  1.5 0.7 copy-done.8
  2.3 0.7 copy-done.9
  3.0 0.7 pack_turn.1
  3.7 5.1 %all-to-all-start = ((bf16[8,80,128]{2,1,0:T(8,128)(2,1)}), bf16[8,80,128]{2,1,0:T(8,128)(2,1)S(1)}, u32[]{:S(2)}, u32[]{:S(2)}) async-start(bf16[8,80,128]{2,1,0:T(8,128)(2,1)} %pack_turn.1), calls=%async_computation | async-start | bytes 327680 | tf_op jit(solution)/shard_map/all_to_all | solution.py:423
  8.8 1.2 copy-done
  10.0 1.2 copy-done.2
  11.2 2.0 %pack_cache.1 = (bf16[8,2,2,128,128]{4,3,2,1,0:T(8,128)(2,1)}, bf16[8,2,2,128,128]{4,3,2,1,0:T(8,128)(2,1)}) custom-call(bf16[2,4,128,512]{3,2,1,0:T(8,128)(2,1)S(1)} %copy-done, bf16[2,4,128,512]{3,2,1,0:T(8,128)(2,1)S(1)} %copy-done.2), custom_call_target="tpu_custom_call" | custom-call | tf_op jit(solution)/shard_map/pack_cache/pallas_call | solution.py:114
  13.2 2.3 %all-to-all-done.rows_ref = bf16[8,80,128]{2,1,0:T(8,128)(2,1)S(1)} async-done(((bf16[8,80,128]{2,1,0:T(8,128)(2,1)}), bf16[8,80,128]{2,1,0:T(8,128)(2,1)S(1)}, u32[]{:S(2)}, u32[]{:S(2)}) %all-to-all-start) | async-done | bytes 163872 | tf_op jit(solution)/shard_map/all_to_all | solution.py:423
  15.6 3.6 %all-to-all-start.1 = ((bf16[8,2,2,128,128]{4,3,2,1,0:T(8,128)(2,1)}), bf16[8,2,2,128,128]{4,3,2,1,0:T(8,128)(2,1)S(1)}, u32[]{:S(2)}, u32[]{:S(2)}) async-start(bf16[8,2,2,128,128]{4,3,2,1,0:T(8,128)(2,1)} %get-tuple-element.65), calls=%async_computation.1 | async-start | bytes 2097152 | tf_op jit(solution)/shard_map/all_to_all | solution.py:426
  19.2 0.1 ring_message.1
  19.3 5.9 %collective-permute-start.1 = (bf16[128,640]{1,0:T(8,128)(2,1)S(1)}, bf16[128,640]{1,0:T(8,128)(2,1)S(1)}, u32[]{:S(2)}, u32[]{:S(2)}) collective-permute-start(bf16[128,640]{1,0:T(8,128)(2,1)S(1)} %get-tuple-element.91.refs_1_.refs_0_.refs_2_), channel_id=1, source_target_pairs={{0,224},{32,0},{64,32},{96,64},{128,96},{160,128},{192,160},{224,1... | collective-permute-start | bytes 491528 | tf_op jit(solution)/shard_map/ppermute | solution.py:28
  25.2 2.8 %collective-permute-done.1.refs_2_.refs_1_ = bf16[128,640]{1,0:T(8,128)(2,1)S(1)} collective-permute-done((bf16[128,640]{1,0:T(8,128)(2,1)S(1)}, bf16[128,640]{1,0:T(8,128)(2,1)S(1)}, u32[]{:S(2)}, u32[]{:S(2)}) %collective-permute-start.1) | collective-permute-done | bytes 163872 | tf_op jit(solution)/shard_map/ppermute | solution.py:28
  28.0 3.7 %collective-permute-done.refs_3_.refs_7_.refs_2_ = bf16[128,640]{1,0:T(8,128)(2,1)S(1)} collective-permute-done((bf16[128,640]{1,0:T(8,128)(2,1)S(1)}, bf16[128,640]{1,0:T(8,128)(2,1)S(1)}, u32[]{:S(2)}, u32[]{:S(2)}) %collective-permute-start) | collective-permute-done | bytes 163872 | tf_op jit(solution)/shard_map/ppermute | solution.py:28
  31.7 2.4 %all-to-all-done.1.kv = bf16[8,2,2,128,128]{4,3,2,1,0:T(8,128)(2,1)S(1)} async-done(((bf16[8,2,2,128,128]{4,3,2,1,0:T(8,128)(2,1)}), bf16[8,2,2,128,128]{4,3,2,1,0:T(8,128)(2,1)S(1)}, u32[]{:S(2)}, u32[]{:S(2)}) %all-to-all-start.1) | async-done | bytes 1048608 | tf_op jit(solution)/shard_map/all_to_all | solution.py:426
  34.1 3.6 %all-to-all-start.2 = ((bf16[8,2,2,128,128]{4,3,2,1,0:T(8,128)(2,1)}), bf16[8,2,2,128,128]{4,3,2,1,0:T(8,128)(2,1)S(1)}, u32[]{:S(2)}, u32[]{:S(2)}) async-start(bf16[8,2,2,128,128]{4,3,2,1,0:T(8,128)(2,1)} %get-tuple-element.80), calls=%async_computation.2 | async-start | bytes 2097152 | tf_op jit(solution)/shard_map/all_to_all | solution.py:443
  37.7 0.0 copy-start.7
  37.7 0.0 copy-start.10
  37.7 0.1 pad_add_fusion.place.refs_0_
  37.8 1.9 %collective-permute-start.2 = (bf16[128,640]{1,0:T(8,128)(2,1)S(1)}, bf16[128,640]{1,0:T(8,128)(2,1)S(1)}, u32[]{:S(2)}, u32[]{:S(2)}) collective-permute-start(bf16[128,640]{1,0:T(8,128)(2,1)S(1)} %collective-permute-done.refs_3_.refs_7_.refs_2_), channel_id=1, source_target_pairs={{0,32},{32,64},{64,96},{96,128},{128,160},{160,192},{192,224},{224... | collective-permute-start | bytes 491528 | tf_op jit(solution)/shard_map/ppermute | solution.py:28
  39.7 4.0 %collective-permute-start.3 = (bf16[128,640]{1,0:T(8,128)(2,1)S(1)}, bf16[128,640]{1,0:T(8,128)(2,1)S(1)}, u32[]{:S(2)}, u32[]{:S(2)}) collective-permute-start(bf16[128,640]{1,0:T(8,128)(2,1)S(1)} %collective-permute-done.1.refs_2_.refs_1_), channel_id=1, source_target_pairs={{0,224},{32,0},{64,32},{96,64},{128,96},{160,128},{192,160},{224,1... | collective-permute-start | bytes 491528 | tf_op jit(solution)/shard_map/ppermute | solution.py:28
  43.8 0.9 prepare.2
  44.7 4.4 %attend.8 = (bf16[144,512]{1,0:T(8,128)(2,1)S(1)}, bf16[144,512]{1,0:T(8,128)(2,1)S(1)}, bf16[144,512]{1,0:T(8,128)(2,1)S(1)}) custom-call(s32[2]{0:T(128)S(1)} %pad_add_fusion.place.refs_0_, bf16[128,640]{1,0:T(8,128)(2,1)S(1)} %get-tuple-element.91.refs_1_.refs_0_.refs_2_, bf16[128,640]{1,0:T(8,128)(2,1)S(1)} %collective-permute-done.1.refs_2_.refs_1_, ...), custom_call_target="tpu_custom_call" | custom-call | flops 3221225472 | bytes 3145728 | tf_op jit(solution)/shard_map/attend/pallas_call | solution.py:272
  49.1 0.6 copy-done.27
  49.8 0.1 collective-permute-start.4
  49.9 3.2 %collective-permute-start.5 = (bf16[128,640]{1,0:T(8,128)(2,1)S(1)}, bf16[128,640]{1,0:T(8,128)(2,1)S(1)}, u32[]{:S(2)}, u32[]{:S(2)}) collective-permute-start(bf16[128,640]{1,0:T(8,128)(2,1)S(1)} %collective-permute-done.3.refs_1_.refs_2_), channel_id=1, source_target_pairs={{0,224},{32,0},{64,32},{96,64},{128,96},{160,128},{192,160},{224,1... | collective-permute-start | bytes 491528 | tf_op jit(solution)/shard_map/ppermute | solution.py:28
  53.1 3.2 %attend.9 = (bf16[144,512]{1,0:T(8,128)(2,1)S(1)}, bf16[144,512]{1,0:T(8,128)(2,1)S(1)}) custom-call(s32[2]{0:T(128)S(1)} %pad_add_fusion.place.refs_0_, bf16[128,640]{1,0:T(8,128)(2,1)S(1)} %collective-permute-done.3.refs_1_.refs_2_, bf16[128,640]{1,0:T(8,128)(2,1)S(1)} %collective-permute-done.2.refs_2_.refs_6_, ...), custom_call_target="tpu_custom_call" | custom-call | flops 2147483648 | bytes 3145728 | tf_op jit(solution)/shard_map/attend/pallas_call | solution.py:272
  56.4 0.0 collective-permute-done.4.refs_2_.refs_5_.refs_1_
  56.4 0.6 copy-done.23
  57.0 0.1 copy-done.25
  57.1 2.7 %collective-permute-start.7 = (bf16[64,640]{1,0:T(8,128)(2,1)S(1)}, bf16[64,640]{1,0:T(8,128)(2,1)S(1)}, u32[]{:S(2)}, u32[]{:S(2)}) collective-permute-start(bf16[64,640]{1,0:T(8,128)(2,1)S(1)} %slice.7), channel_id=1, source_target_pairs={{0,224},{32,0},{64,32},{96,64},{128,96},{160,128},{192,160},{224,1... | collective-permute-start | bytes 245768 | tf_op jit(solution)/shard_map/ppermute | solution.py:28
  59.8 3.2 %attend.10 = (bf16[144,512]{1,0:T(8,128)(2,1)S(1)}, bf16[144,512]{1,0:T(8,128)(2,1)S(1)}) custom-call(s32[2]{0:T(128)S(1)} %pad_add_fusion.place.refs_0_, bf16[128,640]{1,0:T(8,128)(2,1)S(1)} %collective-permute-done.5.refs_1_.refs_3_.refs_2_, bf16[128,640]{1,0:T(8,128)(2,1)S(1)} %collective-permute-done.4.refs_2_.refs_5_.refs_1_, ...), custom_call_target="tpu_custom_call" | custom-call | flops 2147483648 | bytes 3145728 | tf_op jit(solution)/shard_map/attend/pallas_call | solution.py:272
  63.0 0.6 copy-done.29
  63.7 0.6 copy-done.31
  64.3 1.1 collective-permute-done.6
  65.5 1.1 copy-done.14
  66.5 2.2 %attend.11.refs_3_ = bf16[144,512]{1,0:T(8,128)(2,1)S(1)} custom-call(s32[2]{0:T(128)S(1)} %pad_add_fusion.place.refs_0_, bf16[128,640]{1,0:T(8,128)(2,1)S(1)} %constant_dynamic-update-slice_fusion.refs_1_.refs_4_, bf16[2048,128]{1,0:T(8,128)(2,1)S(1)} %get-tuple-element.71.refs_4_.refs_3_.refs_2_.refs_1_, bf16[144,2048]{1,0:T(8,128)(2,1)S(1)} %copy-done.14), custom_call_target="tpu_custom_call" | custom-call | flops 1073741824 | bytes 3145728 | tf_op jit(solution)/shard_map/attend/pallas_call | solution.py:272
  68.7 1.8 %windows.1 = bf16[8,256,128]{2,1,0:T(8,128)(2,1)} custom-call(s32[2]{0:T(128)S(1)} %pad_add_fusion.place.refs_0_, s32[2]{0:T(128)S(1)} %copy-done.10, s32[2,256]{1,0:T(2,128)S(1)} %copy-done.7, bf16[128,640]{1,0:T(8,128)(2,1)S(1)} %get-tuple-element.91.refs_1_.refs_0_.refs_2_, bf16[128,640]{1,0:T(8,128)(2,1)S(1)} %collective-permute-done.1.refs_2_.refs_1_, ...), custom_call_target="tpu_custom_call" | custom-call | tf_op jit(solution)/shard_map/windows/pallas_call | solution.py:365
  70.5 0.9 prepare.3
  71.5 3.4 %attend.12 = (bf16[144,512]{1,0:T(8,128)(2,1)S(1)}, bf16[144,512]{1,0:T(8,128)(2,1)S(1)}) custom-call(s32[2]{0:T(128)S(1)} %pad_add_fusion.place.refs_0_, bf16[128,640]{1,0:T(8,128)(2,1)S(1)} %constant_dynamic-update-slice_fusion.refs_1_.refs_4_, bf16[128,640]{1,0:T(8,128)(2,1)S(1)} %collective-permute-done.5.refs_1_.refs_3_.refs_2_, ...), custom_call_target="tpu_custom_call" | custom-call | flops 2214592512 | bytes 3145728 | tf_op jit(solution)/shard_map/attend/pallas_call | solution.py:272
  74.9 1.7 %collective-permute-start.8 = (bf16[144,512]{1,0:T(8,128)(2,1)S(1)}, bf16[144,512]{1,0:T(8,128)(2,1)S(1)}, u32[]{:S(2)}, u32[]{:S(2)}) collective-permute-start(bf16[144,512]{1,0:T(8,128)(2,1)S(1)} %get-tuple-element.89), channel_id=1, source_target_pairs={{0,64},{32,96},{64,128},{96,160},{128,192},{160,224},{192,0},{224,... | collective-permute-start | bytes 442376 | tf_op jit(solution)/shard_map/ppermute | solution.py:28
  76.6 3.4 %attend.13 = (bf16[144,512]{1,0:T(8,128)(2,1)S(1)}, bf16[144,512]{1,0:T(8,128)(2,1)S(1)}) custom-call(s32[2]{0:T(128)S(1)} %pad_add_fusion.place.refs_0_, bf16[128,640]{1,0:T(8,128)(2,1)S(1)} %collective-permute-done.4.refs_2_.refs_5_.refs_1_, bf16[128,640]{1,0:T(8,128)(2,1)S(1)} %get-tuple-element.91.refs_1_.refs_0_.refs_2_, ...), custom_call_target="tpu_custom_call" | custom-call | flops 2214592512 | bytes 3145728 | tf_op jit(solution)/shard_map/attend/pallas_call | solution.py:272
  80.0 0.6 copy-done.4
  80.6 2.7 %collective-permute-start.12 = (bf16[144,512]{1,0:T(8,128)(2,1)S(1)}, bf16[144,512]{1,0:T(8,128)(2,1)S(1)}, u32[]{:S(2)}, u32[]{:S(2)}) collective-permute-start(bf16[144,512]{1,0:T(8,128)(2,1)S(1)} %get-tuple-element.96), channel_id=1, source_target_pairs={{0,192},{32,224},{64,0},{96,32},{128,64},{160,96},{192,128},{224,1... | collective-permute-start | bytes 442376 | tf_op jit(solution)/shard_map/ppermute | solution.py:28
  83.3 0.9 collective-permute-start.11
  84.3 4.1 %attend.14 = (bf16[144,512]{1,0:T(8,128)(2,1)}, bf16[144,512]{1,0:T(8,128)(2,1)}) custom-call(s32[2]{0:T(128)S(1)} %pad_add_fusion.place.refs_0_, bf16[128,640]{1,0:T(8,128)(2,1)S(1)} %collective-permute-done.3.refs_1_.refs_2_, bf16[128,640]{1,0:T(8,128)(2,1)S(1)} %collective-permute-done.2.refs_2_.refs_6_, bf16[144,512]{1,0:T(8,128)(2,1)S(1)} %copy-done.24, ...), custom_call_target="tpu_custom_call" | custom-call | flops 2214592512 | bytes 3145728 | tf_op jit(solution)/shard_map/attend/pallas_call | solution.py:272
  88.4 5.7 %all-to-all-start.3 = ((bf16[8,256,128]{2,1,0:T(8,128)(2,1)}), bf16[8,256,128]{2,1,0:T(8,128)(2,1)S(1)}, u32[]{:S(2)}, u32[]{:S(2)}) async-start(bf16[8,256,128]{2,1,0:T(8,128)(2,1)} %windows.1), calls=%async_computation.3 | async-start | bytes 1048576 | tf_op jit(solution)/shard_map/all_to_all | solution.py:465
  94.2 0.6 copy-done.17
  94.9 1.0 copy-done.16
  95.9 0.9 copy-done.18
  96.8 4.1 %attend.15 = (bf16[144,512]{1,0:T(8,128)(2,1)}, bf16[144,512]{1,0:T(8,128)(2,1)}) custom-call(s32[2]{0:T(128)S(1)} %pad_add_fusion.place.refs_0_, bf16[128,640]{1,0:T(8,128)(2,1)S(1)} %collective-permute-done.1.refs_2_.refs_1_, bf16[128,640]{1,0:T(8,128)(2,1)S(1)} %collective-permute-done.refs_3_.refs_7_.refs_2_, bf16[144,512]{1,0:T(8,128)(2,1)S(1)} %copy-done.20, ...), custom_call_target="tpu_custom_call" | custom-call | flops 2214592512 | bytes 3145728 | tf_op jit(solution)/shard_map/attend/pallas_call | solution.py:272
  100.9 2.4 %collective-permute-start.13 = (bf16[144,512]{1,0:T(8,128)(2,1)}, bf16[144,512]{1,0:T(8,128)(2,1)S(1)}, u32[]{:S(2)}, u32[]{:S(2)}) collective-permute-start(bf16[144,512]{1,0:T(8,128)(2,1)} %get-tuple-element.110), channel_id=1, source_target_pairs={{0,32},{32,64},{64,96},{96,128},{128,160},{160,192},{192,224},{224... | collective-permute-start | bytes 442376 | tf_op jit(solution)/shard_map/ppermute | solution.py:28
  103.3 1.3 %collective-permute-start.14 = (bf16[144,512]{1,0:T(8,128)(2,1)}, bf16[144,512]{1,0:T(8,128)(2,1)S(1)}, u32[]{:S(2)}, u32[]{:S(2)}) collective-permute-start(bf16[144,512]{1,0:T(8,128)(2,1)} %get-tuple-element.111), channel_id=1, source_target_pairs={{0,224},{32,0},{64,32},{96,64},{128,96},{160,128},{192,160},{224,1... | collective-permute-start | bytes 442376 | tf_op jit(solution)/shard_map/ppermute | solution.py:28
  104.6 1.5 %collective-permute-start.10 = (bf16[144,512]{1,0:T(8,128)(2,1)}, bf16[144,512]{1,0:T(8,128)(2,1)S(1)}, u32[]{:S(2)}, u32[]{:S(2)}) collective-permute-start(bf16[144,512]{1,0:T(8,128)(2,1)} %get-tuple-element.104), channel_id=1, source_target_pairs={{0,192},{32,224},{64,0},{96,32},{128,64},{160,96},{192,128},{224,1... | collective-permute-start | bytes 442376 | tf_op jit(solution)/shard_map/ppermute | solution.py:28
  106.1 1.4 %collective-permute-start.9 = (bf16[144,512]{1,0:T(8,128)(2,1)}, bf16[144,512]{1,0:T(8,128)(2,1)S(1)}, u32[]{:S(2)}, u32[]{:S(2)}) collective-permute-start(bf16[144,512]{1,0:T(8,128)(2,1)} %get-tuple-element.101), channel_id=1, source_target_pairs={{0,64},{32,96},{64,128},{96,160},{128,192},{160,224},{192,0},{224,... | collective-permute-start | bytes 442376 | tf_op jit(solution)/shard_map/ppermute | solution.py:28
  107.5 1.0 collective-permute-done.13.refs_3_
  108.6 0.4 collective-permute-done.14.refs_4_
  108.9 4.2 %collective-permute-done.10.refs_2_ = bf16[144,512]{1,0:T(8,128)(2,1)S(1)} collective-permute-done((bf16[144,512]{1,0:T(8,128)(2,1)}, bf16[144,512]{1,0:T(8,128)(2,1)S(1)}, u32[]{:S(2)}, u32[]{:S(2)}) %collective-permute-start.10) | collective-permute-done | bytes 147488 | tf_op jit(solution)/shard_map/ppermute | solution.py:28
  113.2 1.6 %collective-permute-done.9.refs_1_ = bf16[144,512]{1,0:T(8,128)(2,1)S(1)} collective-permute-done((bf16[144,512]{1,0:T(8,128)(2,1)}, bf16[144,512]{1,0:T(8,128)(2,1)S(1)}, u32[]{:S(2)}, u32[]{:S(2)}) %collective-permute-start.9) | collective-permute-done | bytes 147488 | tf_op jit(solution)/shard_map/ppermute | solution.py:28
  114.7 0.9 merge.1
  115.6 5.7 %all-to-all-start.4 = ((bf16[8,64,128]{2,1,0:T(8,128)(2,1)}), bf16[8,64,128]{2,1,0:T(8,128)(2,1)S(1)}, u32[]{:S(2)}, u32[]{:S(2)}) async-start(bf16[8,64,128]{2,1,0:T(8,128)(2,1)} %merge.1), calls=%async_computation.4 | async-start | bytes 262144 | tf_op jit(solution)/shard_map/all_to_all | solution.py:472
  121.3 2.0 %write.1 = (bf16[2,4,128,512]{3,2,1,0:T(8,128)(2,1)}, bf16[2,4,128,512]{3,2,1,0:T(8,128)(2,1)}) custom-call(s32[2]{0:T(128)S(1)} %pad_add_fusion.place.refs_0_, s32[2]{0:T(128)S(1)} %copy-done.10, s32[2,256]{1,0:T(2,128)S(1)} %copy-done.7, bf16[8,256,128]{2,1,0:T(8,128)(2,1)S(1)} %all-to-all-done.3.new_ref, bf16[2,4,128,512]{3,2,1,0:T(8,128)(2,1)S(1)} %copy-done.1, ...), custom_call_target="tpu_custom_call" | custom-call | bytes 5242880 | tf_op jit(solution)/shard_map/write/pallas_call | solution.py:403
  123.3 4.7 %all-to-all-done.4.rows_ref = bf16[8,64,128]{2,1,0:T(8,128)(2,1)S(1)} async-done(((bf16[8,64,128]{2,1,0:T(8,128)(2,1)}), bf16[8,64,128]{2,1,0:T(8,128)(2,1)S(1)}, u32[]{:S(2)}, u32[]{:S(2)}) %all-to-all-start.4) | async-done | bytes 131104 | tf_op jit(solution)/shard_map/all_to_all | solution.py:472
  128.0 0.7 unpack.1
  (64 shorter events, 0.2 us)
Async XLA Ops:
  0.6 0.9 copy-start.6
  1.5 0.7 copy-start.8
  2.3 0.7 copy-start.9
  3.7 11.9 %all-to-all-start = ((bf16[8,80,128]{2,1,0:T(8,128)(2,1)}), bf16[8,80,128]{2,1,0:T(8,128)(2,1)S(1)}, u32[]{:S(2)}, u32[]{:S(2)}) async-start(bf16[8,80,128]{2,1,0:T(8,128)(2,1)} %pack_turn.1), calls=%async_computation | async-start | bytes 327680 | tf_op jit(solution)/shard_map/all_to_all | solution.py:423
  8.8 1.2 copy-start
  10.0 1.2 copy-start.2
  15.6 18.5 %all-to-all-start.1 = ((bf16[8,2,2,128,128]{4,3,2,1,0:T(8,128)(2,1)}), bf16[8,2,2,128,128]{4,3,2,1,0:T(8,128)(2,1)S(1)}, u32[]{:S(2)}, u32[]{:S(2)}) async-start(bf16[8,2,2,128,128]{4,3,2,1,0:T(8,128)(2,1)} %get-tuple-element.65), calls=%async_computation.1 | async-start | bytes 2097152 | tf_op jit(solution)/shard_map/all_to_all | solution.py:426
  19.3 8.8 %collective-permute-start.1 = (bf16[128,640]{1,0:T(8,128)(2,1)S(1)}, bf16[128,640]{1,0:T(8,128)(2,1)S(1)}, u32[]{:S(2)}, u32[]{:S(2)}) collective-permute-start(bf16[128,640]{1,0:T(8,128)(2,1)S(1)} %get-tuple-element.91.refs_1_.refs_0_.refs_2_), channel_id=1, source_target_pairs={{0,224},{32,0},{64,32},{96,64},{128,96},{160,128},{192,160},{224,1... | collective-permute-start | bytes 491528 | tf_op jit(solution)/shard_map/ppermute | solution.py:28
  25.2 6.5 %collective-permute-start = (bf16[128,640]{1,0:T(8,128)(2,1)S(1)}, bf16[128,640]{1,0:T(8,128)(2,1)S(1)}, u32[]{:S(2)}, u32[]{:S(2)}) collective-permute-start(bf16[128,640]{1,0:T(8,128)(2,1)S(1)} %get-tuple-element.91.refs_1_.refs_0_.refs_2_), channel_id=1, source_target_pairs={{0,32},{32,64},{64,96},{96,128},{128,160},{160,192},{192,224},{224... | collective-permute-start | bytes 491528 | tf_op jit(solution)/shard_map/ppermute | solution.py:28
  34.1 31.3 %all-to-all-start.2 = ((bf16[8,2,2,128,128]{4,3,2,1,0:T(8,128)(2,1)}), bf16[8,2,2,128,128]{4,3,2,1,0:T(8,128)(2,1)S(1)}, u32[]{:S(2)}, u32[]{:S(2)}) async-start(bf16[8,2,2,128,128]{4,3,2,1,0:T(8,128)(2,1)} %get-tuple-element.80), calls=%async_computation.2 | async-start | bytes 2097152 | tf_op jit(solution)/shard_map/all_to_all | solution.py:443
  37.7 6.1 %copy-start.7 = (s32[2,256]{1,0:T(2,128)S(1)}, s32[2,256]{1,0:T(2,128)}, u32[]{:S(2)}) copy-start(s32[2,256]{1,0:T(2,128)} %slots_ref.7) | copy-start | bytes 6148
  37.7 6.1 %copy-start.10 = (s32[2]{0:T(128)S(1)}, s32[2]{0:T(128)}, u32[]{:S(2)}) copy-start(s32[2]{0:T(128)} %lengths.7) | copy-start | bytes 28
  37.8 12.0 %collective-permute-start.2 = (bf16[128,640]{1,0:T(8,128)(2,1)S(1)}, bf16[128,640]{1,0:T(8,128)(2,1)S(1)}, u32[]{:S(2)}, u32[]{:S(2)}) collective-permute-start(bf16[128,640]{1,0:T(8,128)(2,1)S(1)} %collective-permute-done.refs_3_.refs_7_.refs_2_), channel_id=1, source_target_pairs={{0,32},{32,64},{64,96},{96,128},{128,160},{160,192},{192,224},{224... | collective-permute-start | bytes 491528 | tf_op jit(solution)/shard_map/ppermute | solution.py:28
  39.7 10.1 %collective-permute-start.3 = (bf16[128,640]{1,0:T(8,128)(2,1)S(1)}, bf16[128,640]{1,0:T(8,128)(2,1)S(1)}, u32[]{:S(2)}, u32[]{:S(2)}) collective-permute-start(bf16[128,640]{1,0:T(8,128)(2,1)S(1)} %collective-permute-done.1.refs_2_.refs_1_), channel_id=1, source_target_pairs={{0,224},{32,0},{64,32},{96,64},{128,96},{160,128},{192,160},{224,1... | collective-permute-start | bytes 491528 | tf_op jit(solution)/shard_map/ppermute | solution.py:28
  44.7 15.1 %copy-start.13 = (bf16[144,2048]{1,0:T(8,128)(2,1)}, bf16[144,2048]{1,0:T(8,128)(2,1)S(1)}, u32[]{:S(2)}) copy-start(bf16[144,2048]{1,0:T(8,128)(2,1)S(1)} %get-tuple-element.72.refs_5_.refs_4_.refs_3_) | copy-start | bytes 1769476
  49.1 0.7 copy-start.27
  49.8 6.6 %copy-start.19 = (bf16[144,512]{1,0:T(8,128)(2,1)}, bf16[144,512]{1,0:T(8,128)(2,1)S(1)}, u32[]{:S(2)}) copy-start(bf16[144,512]{1,0:T(8,128)(2,1)S(1)} %get-tuple-element.107.refs_3_) | copy-start | bytes 442372
  49.8 6.6 %copy-start.21 = (bf16[144,512]{1,0:T(8,128)(2,1)}, bf16[144,512]{1,0:T(8,128)(2,1)S(1)}, u32[]{:S(2)}) copy-start(bf16[144,512]{1,0:T(8,128)(2,1)S(1)} %get-tuple-element.109.refs_5_) | copy-start | bytes 442372
  49.8 6.6 %collective-permute-start.4 = (bf16[128,640]{1,0:T(8,128)(2,1)S(1)}, bf16[128,640]{1,0:T(8,128)(2,1)S(1)}, u32[]{:S(2)}, u32[]{:S(2)}) collective-permute-start(bf16[128,640]{1,0:T(8,128)(2,1)S(1)} %collective-permute-done.2.refs_2_.refs_6_), channel_id=1, source_target_pairs={{0,32},{32,64},{64,96},{96,128},{128,160},{160,192},{192,224},{224... | collective-permute-start | bytes 491528 | tf_op jit(solution)/shard_map/ppermute | solution.py:28
  49.9 6.5 %collective-permute-start.5 = (bf16[128,640]{1,0:T(8,128)(2,1)S(1)}, bf16[128,640]{1,0:T(8,128)(2,1)S(1)}, u32[]{:S(2)}, u32[]{:S(2)}) collective-permute-start(bf16[128,640]{1,0:T(8,128)(2,1)S(1)} %collective-permute-done.3.refs_1_.refs_2_), channel_id=1, source_target_pairs={{0,224},{32,0},{64,32},{96,64},{128,96},{160,128},{192,160},{224,1... | collective-permute-start | bytes 491528 | tf_op jit(solution)/shard_map/ppermute | solution.py:28
  56.4 0.7 copy-start.23
  56.4 0.7 copy-start.25
  57.1 7.2 %collective-permute-start.7 = (bf16[64,640]{1,0:T(8,128)(2,1)S(1)}, bf16[64,640]{1,0:T(8,128)(2,1)S(1)}, u32[]{:S(2)}, u32[]{:S(2)}) collective-permute-start(bf16[64,640]{1,0:T(8,128)(2,1)S(1)} %slice.7), channel_id=1, source_target_pairs={{0,224},{32,0},{64,32},{96,64},{128,96},{160,128},{192,160},{224,1... | collective-permute-start | bytes 245768 | tf_op jit(solution)/shard_map/ppermute | solution.py:28
  59.8 5.7 %collective-permute-start.6 = (bf16[64,640]{1,0:T(8,128)(2,1)S(1)}, bf16[64,640]{1,0:T(8,128)(2,1)S(1)}, u32[]{:S(2)}, u32[]{:S(2)}) collective-permute-start(bf16[64,640]{1,0:T(8,128)(2,1)S(1)} %slice.6), channel_id=1, source_target_pairs={{0,32},{32,64},{64,96},{96,128},{128,160},{160,192},{192,224},{224... | collective-permute-start | bytes 245768 | tf_op jit(solution)/shard_map/ppermute | solution.py:28
  63.0 0.7 copy-start.29
  63.7 0.6 copy-start.31
  65.5 1.1 copy-start.14
  70.5 1.0 copy-start.32
  71.4 12.9 %copy-start.11 = (bf16[144,2112]{1,0:T(8,128)(2,1)}, bf16[144,2112]{1,0:T(8,128)(2,1)S(1)}, u32[]{:S(2)}) copy-start(bf16[144,2112]{1,0:T(8,128)(2,1)S(1)} %get-tuple-element.88.refs_6_.refs_7_.refs_8_) | copy-start | bytes 1824772
  71.4 12.8 %copy-start.15 = (bf16[2112,128]{1,0:T(8,128)(2,1)}, bf16[2112,128]{1,0:T(8,128)(2,1)S(1)}, u32[]{:S(2)}) copy-start(bf16[2112,128]{1,0:T(8,128)(2,1)S(1)} %get-tuple-element.87.refs_5_.refs_6_.refs_7_) | copy-start | bytes 1622020
  71.5 5.1 %copy-start.28 = (bf16[144,512]{1,0:T(8,128)(2,1)S(1)}, bf16[144,512]{1,0:T(8,128)(2,1)}, u32[]{:S(2)}) copy-start(bf16[144,512]{1,0:T(8,128)(2,1)} %copy-done.27) | copy-start | bytes 442372
  71.5 5.1 %copy-start.30 = (bf16[144,512]{1,0:T(8,128)(2,1)S(1)}, bf16[144,512]{1,0:T(8,128)(2,1)}, u32[]{:S(2)}) copy-start(bf16[144,512]{1,0:T(8,128)(2,1)} %copy-done.29) | copy-start | bytes 442372
  74.9 9.4 %collective-permute-start.8 = (bf16[144,512]{1,0:T(8,128)(2,1)S(1)}, bf16[144,512]{1,0:T(8,128)(2,1)S(1)}, u32[]{:S(2)}, u32[]{:S(2)}) collective-permute-start(bf16[144,512]{1,0:T(8,128)(2,1)S(1)} %get-tuple-element.89), channel_id=1, source_target_pairs={{0,64},{32,96},{64,128},{96,160},{128,192},{160,224},{192,0},{224,... | collective-permute-start | bytes 442376 | tf_op jit(solution)/shard_map/ppermute | solution.py:28
  76.6 7.7 %copy-start.24 = (bf16[144,512]{1,0:T(8,128)(2,1)S(1)}, bf16[144,512]{1,0:T(8,128)(2,1)}, u32[]{:S(2)}) copy-start(bf16[144,512]{1,0:T(8,128)(2,1)} %copy-done.23) | copy-start | bytes 442372
  76.6 7.7 %copy-start.26 = (bf16[144,512]{1,0:T(8,128)(2,1)S(1)}, bf16[144,512]{1,0:T(8,128)(2,1)}, u32[]{:S(2)}) copy-start(bf16[144,512]{1,0:T(8,128)(2,1)} %copy-done.25) | copy-start | bytes 442372
  79.9 0.7 copy-start.4
  80.6 13.6 %collective-permute-start.12 = (bf16[144,512]{1,0:T(8,128)(2,1)S(1)}, bf16[144,512]{1,0:T(8,128)(2,1)S(1)}, u32[]{:S(2)}, u32[]{:S(2)}) collective-permute-start(bf16[144,512]{1,0:T(8,128)(2,1)S(1)} %get-tuple-element.96), channel_id=1, source_target_pairs={{0,192},{32,224},{64,0},{96,32},{128,64},{160,96},{192,128},{224,1... | collective-permute-start | bytes 442376 | tf_op jit(solution)/shard_map/ppermute | solution.py:28
  83.3 10.8 %collective-permute-start.11 = (bf16[144,512]{1,0:T(8,128)(2,1)S(1)}, bf16[144,512]{1,0:T(8,128)(2,1)S(1)}, u32[]{:S(2)}, u32[]{:S(2)}) collective-permute-start(bf16[144,512]{1,0:T(8,128)(2,1)S(1)} %get-tuple-element.108), channel_id=1, source_target_pairs={{0,64},{32,96},{64,128},{96,160},{128,192},{160,224},{192,0},{224,... | collective-permute-start | bytes 442376 | tf_op jit(solution)/shard_map/ppermute | solution.py:28
  88.4 6.4 %copy-start.12 = (bf16[144,2112]{1,0:T(8,128)(2,1)S(1)}, bf16[144,2112]{1,0:T(8,128)(2,1)}, u32[]{:S(2)}) copy-start(bf16[144,2112]{1,0:T(8,128)(2,1)} %copy-done.11) | copy-start | bytes 1824772
  88.4 6.4 %copy-start.20 = (bf16[144,512]{1,0:T(8,128)(2,1)S(1)}, bf16[144,512]{1,0:T(8,128)(2,1)}, u32[]{:S(2)}) copy-start(bf16[144,512]{1,0:T(8,128)(2,1)} %copy-done.19) | copy-start | bytes 442372
  88.4 6.4 %copy-start.22 = (bf16[144,512]{1,0:T(8,128)(2,1)S(1)}, bf16[144,512]{1,0:T(8,128)(2,1)}, u32[]{:S(2)}) copy-start(bf16[144,512]{1,0:T(8,128)(2,1)} %copy-done.21) | copy-start | bytes 442372
  88.4 19.1 %all-to-all-start.3 = ((bf16[8,256,128]{2,1,0:T(8,128)(2,1)}), bf16[8,256,128]{2,1,0:T(8,128)(2,1)S(1)}, u32[]{:S(2)}, u32[]{:S(2)}) async-start(bf16[8,256,128]{2,1,0:T(8,128)(2,1)} %windows.1), calls=%async_computation.3 | async-start | bytes 1048576 | tf_op jit(solution)/shard_map/all_to_all | solution.py:465
  94.2 0.7 copy-start.17
  94.9 1.0 copy-start.16
  95.9 0.9 copy-start.18
  96.8 17.9 %copy-start.5 = (bf16[144,512]{1,0:T(8,128)(2,1)S(1)}, bf16[144,512]{1,0:T(8,128)(2,1)}, u32[]{:S(2)}) copy-start(bf16[144,512]{1,0:T(8,128)(2,1)} %copy-done.4) | copy-start | bytes 442372
  96.8 24.5 %copy-start.3 = (bf16[2,4,128,512]{3,2,1,0:T(8,128)(2,1)S(1)}, bf16[2,4,128,512]{3,2,1,0:T(8,128)(2,1)}, u32[]{:S(2)}) copy-start(bf16[2,4,128,512]{3,2,1,0:T(8,128)(2,1)} %v_ref.3) | copy-start | bytes 3145732
  100.9 20.4 %copy-start.1 = (bf16[2,4,128,512]{3,2,1,0:T(8,128)(2,1)S(1)}, bf16[2,4,128,512]{3,2,1,0:T(8,128)(2,1)}, u32[]{:S(2)}) copy-start(bf16[2,4,128,512]{3,2,1,0:T(8,128)(2,1)} %k_ref.3) | copy-start | bytes 3145732
  100.9 7.7 %collective-permute-start.13 = (bf16[144,512]{1,0:T(8,128)(2,1)}, bf16[144,512]{1,0:T(8,128)(2,1)S(1)}, u32[]{:S(2)}, u32[]{:S(2)}) collective-permute-start(bf16[144,512]{1,0:T(8,128)(2,1)} %get-tuple-element.110), channel_id=1, source_target_pairs={{0,32},{32,64},{64,96},{96,128},{128,160},{160,192},{192,224},{224... | collective-permute-start | bytes 442376 | tf_op jit(solution)/shard_map/ppermute | solution.py:28
  103.3 5.6 %collective-permute-start.14 = (bf16[144,512]{1,0:T(8,128)(2,1)}, bf16[144,512]{1,0:T(8,128)(2,1)S(1)}, u32[]{:S(2)}, u32[]{:S(2)}) collective-permute-start(bf16[144,512]{1,0:T(8,128)(2,1)} %get-tuple-element.111), channel_id=1, source_target_pairs={{0,224},{32,0},{64,32},{96,64},{128,96},{160,128},{192,160},{224,1... | collective-permute-start | bytes 442376 | tf_op jit(solution)/shard_map/ppermute | solution.py:28
  104.6 8.5 %collective-permute-start.10 = (bf16[144,512]{1,0:T(8,128)(2,1)}, bf16[144,512]{1,0:T(8,128)(2,1)S(1)}, u32[]{:S(2)}, u32[]{:S(2)}) collective-permute-start(bf16[144,512]{1,0:T(8,128)(2,1)} %get-tuple-element.104), channel_id=1, source_target_pairs={{0,192},{32,224},{64,0},{96,32},{128,64},{160,96},{192,128},{224,1... | collective-permute-start | bytes 442376 | tf_op jit(solution)/shard_map/ppermute | solution.py:28
  106.1 8.6 %collective-permute-start.9 = (bf16[144,512]{1,0:T(8,128)(2,1)}, bf16[144,512]{1,0:T(8,128)(2,1)S(1)}, u32[]{:S(2)}, u32[]{:S(2)}) collective-permute-start(bf16[144,512]{1,0:T(8,128)(2,1)} %get-tuple-element.101), channel_id=1, source_target_pairs={{0,64},{32,96},{64,128},{96,160},{128,192},{160,224},{192,0},{224,... | collective-permute-start | bytes 442376 | tf_op jit(solution)/shard_map/ppermute | solution.py:28
  115.6 12.4 %all-to-all-start.4 = ((bf16[8,64,128]{2,1,0:T(8,128)(2,1)}), bf16[8,64,128]{2,1,0:T(8,128)(2,1)S(1)}, u32[]{:S(2)}, u32[]{:S(2)}) async-start(bf16[8,64,128]{2,1,0:T(8,128)(2,1)} %merge.1), calls=%async_computation.4 | async-start | bytes 262144 | tf_op jit(solution)/shard_map/all_to_all | solution.py:472

commit v3 on v2

--- a/solution.py
+++ b/solution.py
@@ -19,6 +19,7 @@
 SMEM = pl.BlockSpec(memory_space=pltpu.SMEM)
 VMEM = pl.BlockSpec(memory_space=pltpu.VMEM)
 ANY = pl.BlockSpec(memory_space=pl.ANY)
+HBM = pl.BlockSpec(memory_space=pltpu.HBM)
 
 def dot(a, b):
     return jnp.dot(a, b, preferred_element_type=F32)
@@ -28,7 +29,17 @@
     return lax.ppermute(a, "z", [(i, (i + by) % size) for i in range(size)])
 
 
-def pack_turn_kernel(q_ref, k_ref, v_ref, out_ref):
+def pack_turn_kernel(*refs):
+    sources, out_ref, held, sems = refs[:3], refs[3], refs[4:7], refs[7]
+    copies = [
+        pltpu.make_async_copy(source, target, sems.at[i])
+        for i, (source, target) in enumerate(zip(sources, held))
+    ]
+    for copy in copies:
+        copy.start()
+    for copy in copies:
+        copy.wait()
+    q_ref, k_ref, v_ref = held
     convs, tokens, width = q_ref.shape
     heads = k_ref.shape[2] // HEAD
     group = width // (heads * HEAD)
@@ -49,10 +60,12 @@
     rows = tokens * (width // (heads * HEAD) + 2)
     return pl.pallas_call(
         pack_turn_kernel,
-        in_specs=[VMEM] * 3,
+        in_specs=[HBM] * 3,
         out_specs=VMEM,
         out_shape=jax.ShapeDtypeStruct((convs * heads, rows, HEAD), BF16),
-        compiler_params=pltpu.CompilerParams(vmem_limit_bytes=6 * MIB),
+        scratch_shapes=[pltpu.VMEM(x.shape, BF16) for x in (queries, new_keys, new_values)]
+        + [pltpu.SemaphoreType.DMA((3,))],
+        compiler_params=pltpu.CompilerParams(vmem_limit_bytes=60 * MIB),
         name="pack_turn",
     )(queries, new_keys, new_values)
 
@@ -113,11 +126,11 @@
     pairs = convs * width // HEAD
     return pl.pallas_call(
         pack_cache_kernel,
-        in_specs=[ANY, ANY],
+        in_specs=[HBM, HBM],
         out_specs=[VMEM] * count,
         out_shape=[jax.ShapeDtypeStruct((pairs, 2, slots // count, span, HEAD), BF16)] * count,
         scratch_shapes=[pltpu.SemaphoreType.DMA((2 * pairs * count,))],
-        compiler_params=pltpu.CompilerParams(vmem_limit_bytes=8 * MIB),
+        compiler_params=pltpu.CompilerParams(vmem_limit_bytes=60 * MIB),
         name="pack_cache",
     )(cache_keys, cache_values)
 
@@ -196,27 +209,35 @@
     return sums, total, top
 
 
-def attend_kernel(parts, distances, inits, with_new, *refs):
+def attend_kernel(parts, distances, cuts, inits, with_new, *refs):
     count = len(distances)
     place, refs = refs[0], refs[1:]
-    q_refs, refs = refs[:count], refs[count:]
-    init_refs, refs = refs[: sum(inits)], refs[sum(inits) :]
+    q_refs = []
+    for pieces in cuts:
+        q_refs.append(refs[:pieces])
+        refs = refs[pieces:]
+    picks = [pick for init in inits for pick in init]
+    init_refs, refs = refs[: len(picks)], refs[len(picks) :]
+    init_refs = [ref if pick is None else ref.at[pick] for ref, pick in zip(init_refs, picks)]
     keys, sums, outs = refs[0], refs[1], refs[2:]
+    if len(outs[0].shape) == 3:
+        outs = [outs[0].at[c] for c in range(count)]
     width = outs[0].shape[1]
     columns = count * width
     turn_part = width // 8
     cached = keys.shape[0] - with_new * turn_part
     z = place[0]
 
-    q = jnp.concatenate([ref[:, 0:width] for ref in q_refs], axis=1).astype(F32) * SCALE
+    q = [jnp.concatenate([ref[:, 0:width] for ref in held], axis=0) for held in q_refs]
+    q = jnp.concatenate(q, axis=1).astype(F32) * SCALE
     high = q.astype(BF16)
     low = (q - high.astype(F32)).astype(BF16)
     q = jnp.concatenate([high, low], axis=0)
     tops, totals, at_init = [], [], 0
     for given in inits:
         if given:
-            held, weight, level = combine(init_refs[at_init : at_init + given])
-            at_init += given
+            held, weight, level = combine(init_refs[at_init : at_init + len(given)])
+            at_init += len(given)
             tops.append(level)
             totals.append(
                 jnp.concatenate([held, jnp.broadcast_to(weight, (EXTRA, width))], axis=0)
@@ -264,16 +285,20 @@
         outs[c][HEAD:] = coded[:, at]
 
 
-def attend(place, kv, chunks, distances, inits, parts, with_new):
+def attend(place, kv, chunks, distances, inits, parts, with_new, joined):
     keys, sums = kv
     count = len(distances)
-    width = chunks[0].shape[1] - HEAD
-    given = [part for init in inits for part in init]
-    return pl.pallas_call(
-        functools.partial(attend_kernel, parts, distances, [len(i) for i in inits], with_new),
-        in_specs=[SMEM] + [VMEM] * (count + len(given) + 2),
-        out_specs=[VMEM] * count,
-        out_shape=[jax.ShapeDtypeStruct((HEAD + EXTRA, width), BF16)] * count,
+    width = chunks[0][0].shape[1] - HEAD
+    pieces = [piece for chunk in chunks for piece in chunk]
+    cuts = [len(chunk) for chunk in chunks]
+    given = [part[0] for init in inits for part in init]
+    shape = jax.ShapeDtypeStruct((count,) * joined + (HEAD + EXTRA, width), BF16)
+    picks = [[part[1] if len(part) > 1 else None for part in init] for init in inits]
+    return pl.pallas_call(
+        functools.partial(attend_kernel, parts, distances, cuts, picks, with_new),
+        in_specs=[SMEM] + [VMEM] * (len(pieces) + len(given) + 2),
+        out_specs=VMEM if joined else [VMEM] * count,
+        out_shape=shape if joined else [shape] * count,
         compiler_params=pltpu.CompilerParams(vmem_limit_bytes=16 * MIB),
         cost_estimate=pl.CostEstimate(
             flops=8 * HEAD * count * width * keys.shape[0],
@@ -281,49 +306,31 @@
             transcendentals=count * width * keys.shape[0],
         ),
         name="attend",
-    )(place, *chunks, *given, keys, sums)
+    )(place, *pieces, *given, keys, sums)
 
 
 def merge_kernel(*refs):
-    parts, out_ref = refs[:-1], refs[-1]
+    parts, window_ref, out_ref = refs[:-2], refs[-2], refs[-1]
     sums, total, _ = combine(parts)
     turned = (sums * (1.0 / total)).astype(BF16).T
     columns, rows, _ = out_ref.shape
+    rows -= window_ref.shape[1]
     for s in range(columns):
-        out_ref[s] = turned[s * rows : (s + 1) * rows]
-
-
-def merge(parts):
+        out_ref[s, 0:rows] = turned[s * rows : (s + 1) * rows]
+        out_ref[s, rows:] = window_ref[s]
+
+
+def merge(parts, windows):
     width = parts[0].shape[1]
+    rows = width // COLUMNS + windows.shape[1]
     return pl.pallas_call(
         merge_kernel,
-        in_specs=[VMEM] * len(parts),
+        in_specs=[VMEM] * (len(parts) + 1),
         out_specs=VMEM,
-        out_shape=jax.ShapeDtypeStruct((COLUMNS, width // COLUMNS, HEAD), BF16),
+        out_shape=jax.ShapeDtypeStruct((COLUMNS, rows, HEAD), BF16),
         compiler_params=pltpu.CompilerParams(vmem_limit_bytes=8 * MIB),
         name="merge",
-    )(*parts)
-
-
-def unpack_kernel(rows_ref, out_ref):
-    convs, tokens, width = out_ref.shape
-    pairs, rows, _ = rows_ref.shape
-    heads, group = pairs // convs, rows // tokens
-    for c in range(convs):
-        for h in range(heads):
-            for g in range(group):
-                at = (h * group + g) * HEAD
-                piece = rows_ref[c * heads + h, g * tokens : (g + 1) * tokens]
-                out_ref[c, :, at : at + HEAD] = piece
-
-
-def unpack(rows, shape):
-    return pl.pallas_call(
-        unpack_kernel,
-        out_shape=jax.ShapeDtypeStruct(shape, BF16),
-        compiler_params=pltpu.CompilerParams(vmem_limit_bytes=6 * MIB),
-        name="unpack",
-    )(rows)
+    )(*parts, windows)
 
 
 def turn_slot(length, rotation, member, slots, cycle, span):
@@ -333,10 +340,18 @@
 
 
 def windows_kernel(slots, span, cycle, place, lengths, slots_ref, *refs):
-    chunks, out_ref, rows = refs[:-2], refs[-2], refs[-1]
+    news, out_ref, rows = refs[:-2], refs[-2], refs[-1]
+    turn_part = HEAD // 2
+    chunks, at = [], 0
+    while at < len(news):
+        if news[at].shape[0] > turn_part:
+            chunks.append((news[at].at[0:turn_part], news[at].at[turn_part:]))
+            at += 1
+        else:
+            chunks.append((news[at], news[at + 1]))
+            at += 2
     parts = len(chunks)
-    width = chunks[0].shape[1] - HEAD
-    turn_part = HEAD // 2
+    width = news[0].shape[1] - HEAD
     turn = parts * turn_part
     z, b = place[0], place[1]
     conv = b // (COLUMNS // 2)
@@ -347,8 +362,8 @@
     rows[turn + 2 * span :] = edge[0:8]
     for d, chunk in enumerate(chunks):
         start = pl.multiple_of(span + lax.rem(z + d, parts) * turn_part, turn_part)
-        rows[pl.ds(start, turn_part), 0:HEAD] = chunk[0:turn_part, width:].astype(F32)
-        rows[pl.ds(start, turn_part), HEAD:] = chunk[turn_part:, width:].astype(F32)
+        rows[pl.ds(start, turn_part), 0:HEAD] = chunk[0][:, width:].astype(F32)
+        rows[pl.ds(start, turn_part), HEAD:] = chunk[1][:, width:].astype(F32)
     for to in range(COLUMNS):
         _, token = turn_slot(lengths[conv], rotation, z * COLUMNS + to, slots, cycle, span)
         start = jnp.clip(token + span, 0, turn + span)
@@ -362,21 +377,31 @@
 
 def windows(place, lengths, span_slots, chunks, slots, span, cycle):
     turn = len(chunks) * HEAD // 2
+    pieces = [piece for chunk in chunks for piece in chunk]
     return pl.pallas_call(
         functools.partial(windows_kernel, slots, span, cycle),
-        in_specs=[SMEM] * 3 + [VMEM] * len(chunks),
+        in_specs=[SMEM] * 3 + [VMEM] * len(pieces),
         out_specs=VMEM,
         out_shape=jax.ShapeDtypeStruct((COLUMNS, 2 * span, HEAD), BF16),
         scratch_shapes=[pltpu.VMEM((turn + 2 * span + 8, 2 * HEAD), F32)],
         compiler_params=pltpu.CompilerParams(vmem_limit_bytes=8 * MIB),
         name="windows",
-    )(place, lengths, span_slots, *chunks)
-
-
-def write_kernel(turn, cycle, place, lengths, slots_ref, new_ref, k_ref, v_ref, ko_ref, vo_ref):
+    )(place, lengths, span_slots, *pieces)
+
+
+def finish_kernel(
+    turn, cycle, place, lengths, slots_ref, new_ref, k_ref, v_ref, out_ref, ko_ref, vo_ref
+):
     conv = pl.program_id(0)
     _, slots, span, width = k_ref.shape
     heads = width // HEAD
+    _, tokens, query_width = out_ref.shape
+    group = query_width // width
+    done = tokens * group
+    for h in range(heads):
+        for g in range(group):
+            at = (h * group + g) * HEAD
+            out_ref[0, :, at : at + HEAD] = new_ref[h, g * tokens : (g + 1) * tokens]
     member = place[0] * COLUMNS + place[1]
     rotation = slots_ref[conv, 0] // slots
     slot, token = turn_slot(lengths[conv], rotation, member, slots, cycle, span)
@@ -390,26 +415,28 @@
         for h in range(heads):
             lanes = slice(h * HEAD, (h + 1) * HEAD)
             for i, (old, out) in enumerate(((k_ref, ko_ref), (v_ref, vo_ref))):
-                new = new_ref[h, i * span : (i + 1) * span].astype(F32)
+                start = done + i * span
+                new = new_ref[h, start : start + span].astype(F32)
                 kept = old[0, slot, :, lanes].astype(F32)
                 out[0, slot, :, lanes] = jnp.where(inside, new, kept).astype(BF16)
 
 
-def write(place, lengths, span_slots, new, cache_keys, cache_values, turn, cycle):
+def finish(place, lengths, span_slots, rows, cache_keys, cache_values, queries, turn, cycle):
     convs, slots, span, width = cache_keys.shape
+    _, tokens, query_width = queries.shape
     spec = pl.BlockSpec((1, slots, span, width), lambda c: (c, 0, 0, 0))
-    new_block = (new.shape[0] // convs,) + new.shape[1:]
+    block = (rows.shape[0] // convs,) + rows.shape[1:]
     shape = jax.ShapeDtypeStruct(cache_keys.shape, BF16)
     return pl.pallas_call(
-        functools.partial(write_kernel, turn, cycle),
+        functools.partial(finish_kernel, turn, cycle),
         grid=(convs,),
-        in_specs=[SMEM] * 3 + [pl.BlockSpec(new_block, lambda c: (c, 0, 0)), spec, spec],
-        out_specs=[spec, spec],
-        out_shape=[shape, shape],
+        in_specs=[SMEM] * 3 + [pl.BlockSpec(block, lambda c: (c, 0, 0)), spec, spec],
+        out_specs=[pl.BlockSpec((1, tokens, query_width), lambda c: (c, 0, 0)), spec, spec],
+        out_shape=[jax.ShapeDtypeStruct(queries.shape, BF16), shape, shape],
         compiler_params=pltpu.CompilerParams(vmem_limit_bytes=12 * MIB),
         cost_estimate=pl.CostEstimate(flops=0, bytes_accessed=5 * MIB, transcendentals=0),
-        name="write",
-    )(place, lengths, span_slots, new, cache_keys, cache_values)
+        name="finish",
+    )(place, lengths, span_slots, rows, cache_keys, cache_values)
 
 
 def on_device(parts, queries, new_keys, new_values, cache_keys, cache_values, lengths, span_slots):
@@ -429,52 +456,56 @@
     chunks = [None] * parts
     chunks[0] = message
     half = message.shape[0] // 2
-
-    def run(kv, distances, inits=None, after=()):
-        held = [chunks[d] for d in distances]
+    far = None
+
+    def run(kv, distances, inits=None, after=(), joined=True):
+        held = [c if isinstance(c, tuple) else (c,) for c in (chunks[d] for d in distances)]
         if after:
             held, _ = tie((held, after))
         inits = inits or [()] * len(distances)
-        return attend(place, kv, held, distances, inits, parts, kv is far)
-
-    far = None
+        return attend(place, kv, held, distances, inits, parts, kv is far, joined)
+
     chunks[7], chunks[1] = shift(message, 1), shift(message, -1)
-    second, first, chunks[7], chunks[1] = tie((second, first, chunks[7], chunks[1]))
-    second = lax.all_to_all(second, "b", 0, 0, tiled=True)
     chunks[6], chunks[2] = shift(chunks[7], 1), shift(chunks[1], -1)
     near = prepare(place, lengths, span_slots, 0, first, cycle)
-    own, a1, a7 = run(near, (0, 1, 7))
-    chunks[6], chunks[2], own = tie((chunks[6], chunks[2], own))
+    n017 = run(near, (0, 1, 7))
+    second, chunks[6], chunks[2], n017 = tie((second, chunks[6], chunks[2], n017))
+    second = lax.all_to_all(second, "b", 0, 0, tiled=True)
     chunks[5], chunks[3] = shift(chunks[6], 1), shift(chunks[2], -1)
-    a2, a6 = run(near, (2, 6))
-    chunks[5], chunks[3], a2 = tie((chunks[5], chunks[3], a2))
     below, above = shift(chunks[5][:half], 1), shift(chunks[3][half:], -1)
-    a3, a5 = run(near, (3, 5))
-    below, above, a3, second = tie((below, above, a3, second))
+    n35 = run(near, (3, 5))
+    below, above, n35, second = tie((below, above, n35, second))
     far = prepare(place, lengths, span_slots, slots // 2, second, cycle, new, near[0])
-    chunks[4] = jnp.concatenate([below, above], axis=0)
-    (a4,) = run(near, (4,))
-    rows = windows(place, lengths, span_slots, chunks, slots, span, cycle)
-    a4, rows = tie((a4, rows))
-
-    up4, up3 = run(far, (4, 3), ((a4,), (a3,)))
-    down3, own = run(far, (5, 0), ((a5,), (own,)), after=(up4,))
-    up4, up3 = shift(up4, 2), shift(up3, 2)
-    up2, down2 = run(far, (2, 6), ((a2, up4), (a6,)), after=(down3,))
-    rows, _ = tie((rows, up2))
+    chunks[4] = (below, above)
+    n4 = run(near, (4,))
+
+    ups = run(far, (4, 3), (((n4, 0),), ((n35, 0),)))
+    down3, own = run(far, (5, 0), (((n35, 1),), ((n017, 0),)), (ups,), False)
+    ups = shift(ups, 2)
+    n26 = run(near, (2, 6), after=(down3,))
+    down3 = shift(down3, -2)
+    up2, down2 = run(far, (2, 6), (((n26, 0), (ups, 0)), ((n26, 1),)), joined=False)
+    up1, down1 = run(
+        far, (1, 7), (((n017, 1), (ups, 1)), ((n017, 2), (down3,))), (up2,), False
+    )
+    up2, down2 = shift(up2, 2), shift(down2, -2)
+    seen = [c if isinstance(c, tuple) else (c,) for c in chunks]
+    seen, _ = tie((seen, up1))
+    rows = windows(place, lengths, span_slots, seen, slots, span, cycle)
+    up1, down1 = shift(up1, 1), shift(down1, -1)
+    rows = merge([own, up2, down2, up1, down1], rows)
     rows = lax.all_to_all(rows, "b", 0, 0, tiled=True)
-    down3 = shift(down3, -2)
-    up1, down1 = run(far, (1, 7), ((a1, up3), (a7, down3)), after=(up2,))
-    up2, down2 = shift(up2, 2), shift(down2, -2)
-    up1, down1 = shift(up1, 1), shift(down1, -1)
-    own, rows = tie((own, rows))
-    done = merge([own, up2, down2, up1, down1])
-    done = lax.all_to_all(done, "b", 0, 0, tiled=True)
-    attended = unpack(done, queries.shape)
-    keys_out, values_out = write(
-        place, lengths, span_slots, rows, cache_keys, cache_values, parts * HEAD // 2, cycle
+    return finish(
+        place,
+        lengths,
+        span_slots,
+        rows,
+        cache_keys,
+        cache_values,
+        queries,
+        parts * HEAD // 2,
+        cycle,
     )
-    return attended, keys_out, values_out
 
 
 def solution(mesh):

time: 130 us -> 116 us (0.89)
  blocking collectives: 0 us -> 12.9 us
  starting transfers between devices: 53.5 us -> 43.1 us
  local copies, waits for them, and re-layouts: 11.8 us -> 1.5 us
  waiting for transfers between devices: 24.3 us -> 19.6 us
    all_to_all x0 -> x1, blocking collectives: none -> 12.9 us  [on_device(): rows = lax.all_to_all(rows, 'b', 0, 0, tiled=True)]
    all_to_all x2 -> x0, starting transfers between devices: 11.4 us -> none  [the longest x1 5.73 us: on_device(): rows = lax.all_to_all(rows, 'b', 0, 0, tiled=True)]
    unnamed x67 -> x16, local copies, waits for them, and re-layouts: 11.8 us -> 1.48 us
    all_to_all x2 -> x0, waiting for transfers between devices: 4.69 us -> none  [the longest x1 4.69 us: on_device(): done = lax.all_to_all(done, 'b', 0, 0, tiled=True)]
    ppermute x15 -> x14, waiting for transfers between devices: 14.8 us -> 14 us  [shift(): return lax.ppermute(a, 'z', [(i, (i + by) % size) for i in range(size)])]
    ppermute x15 -> x14, starting transfers between devices: 29.9 us -> 30.5 us  [shift(): return lax.ppermute(a, 'z', [(i, (i + by) % size) for i in range(size)])]
    pallas_call x13 -> x12, Pallas kernels: 34.3 us -> 34 us  [the longest x8 26.9 us: attend(): pl.pallas_call(functools.partial(attend_kernel, parts, distances, cuts, p...]
  transfers between devices with their start and end apart: 20 -> 17, of which waited for: 10 -> 9; matrix products, arithmetic and copies ran while one was open for 0% -> 0% of each run, Pallas kernels for 21% -> 20%
where the time goes in v3:
time: 116 us; the launch traced here: 115 us
  starting transfers between devices  43.1 us (37%)
  Pallas kernels  36.9 us (32%)
  waiting for transfers between devices  19.6 us (17%)
  blocking collectives  12.9 us (11%)
  local copies, waits for them, and re-layouts  1.5 us (1%)
    ppermute x14, starting transfers between devices, shift(): return lax.ppermute(a, 'z', [(i, (i + by) % size) for i in range(size)])  30.5 us
    pallas_call x8, Pallas kernels, attend(): pl.pallas_call(functools.partial(attend_kernel, parts, distances, cuts, p...  26.9 us
    ppermute x14, waiting for transfers between devices, shift(): return lax.ppermute(a, 'z', [(i, (i + by) % size) for i in range(size)])  14 us
    all_to_all x1, blocking collectives, on_device(): rows = lax.all_to_all(rows, 'b', 0, 0, tiled=True)  12.9 us
    all_to_all x1, starting transfers between devices, on_device(): turn_rows = lax.all_to_all(turn_rows, 'b', 0, 0, tiled=True)  5.12 us
    all_to_all x1, starting transfers between devices, on_device(): second = lax.all_to_all(second, 'b', 0, 0, tiled=True)  3.95 us
    all_to_all x1, waiting for transfers between devices, on_device(): turn_rows = lax.all_to_all(turn_rows, 'b', 0, 0, tiled=True)  3.61 us
    all_to_all x1, starting transfers between devices, on_device(): first = lax.all_to_all(first, 'b', 0, 0, tiled=True)  3.56 us
  transfers between devices with their start and end apart: 17, of which 9 were waited for; matrix products, arithmetic and copies ran while one was open for 0% of the time, Pallas kernels for 20%

profile of v3, /device:TPU:4, one launch (start us, length us, event | category | flops | bytes accessed | tf_op | source)
XLA Modules:
  0.0 114.9 jit_solution(5746799394351920416)
XLA Ops:
  0.6 1.6 %pack_turn.1 = bf16[8,80,128]{2,1,0:T(8,128)(2,1)} custom-call(bf16[2,8,4096]{2,1,0:T(8,128)(2,1)} %refs_0_.1, bf16[2,8,512]{2,1,0:T(8,128)(2,1)} %refs_1_.1, bf16[2,8,512]{2,1,0:T(8,128)(2,1)} %refs_2_.1), custom_call_target="tpu_custom_call" | custom-call | tf_op jit(solution)/shard_map/pack_turn/pallas_call | solution.py:61
  2.3 5.1 %all-to-all-start = ((bf16[8,80,128]{2,1,0:T(8,128)(2,1)}), bf16[8,80,128]{2,1,0:T(8,128)(2,1)S(1)}, u32[]{:S(2)}, u32[]{:S(2)}) async-start(bf16[8,80,128]{2,1,0:T(8,128)(2,1)} %pack_turn.1), calls=%async_computation | async-start | bytes 327680 | tf_op jit(solution)/shard_map/all_to_all | solution.py:450
  7.4 3.2 %pack_cache.1 = (bf16[8,2,2,128,128]{4,3,2,1,0:T(8,128)(2,1)}, bf16[8,2,2,128,128]{4,3,2,1,0:T(8,128)(2,1)}) custom-call(bf16[2,4,128,512]{3,2,1,0:T(8,128)(2,1)} %k_ref.1, bf16[2,4,128,512]{3,2,1,0:T(8,128)(2,1)} %v_ref.1), custom_call_target="tpu_custom_call" | custom-call | tf_op jit(solution)/shard_map/pack_cache/pallas_call | solution.py:127
  10.6 3.6 %all-to-all-done.rows_ref = bf16[8,80,128]{2,1,0:T(8,128)(2,1)S(1)} async-done(((bf16[8,80,128]{2,1,0:T(8,128)(2,1)}), bf16[8,80,128]{2,1,0:T(8,128)(2,1)S(1)}, u32[]{:S(2)}, u32[]{:S(2)}) %all-to-all-start) | async-done | bytes 163872 | tf_op jit(solution)/shard_map/all_to_all | solution.py:450
  14.2 3.6 %all-to-all-start.1 = ((bf16[8,2,2,128,128]{4,3,2,1,0:T(8,128)(2,1)}), bf16[8,2,2,128,128]{4,3,2,1,0:T(8,128)(2,1)S(1)}, u32[]{:S(2)}, u32[]{:S(2)}) async-start(bf16[8,2,2,128,128]{4,3,2,1,0:T(8,128)(2,1)} %get-tuple-element.54), calls=%async_computation.1 | async-start | bytes 2097152 | tf_op jit(solution)/shard_map/all_to_all | solution.py:453
  17.8 0.1 ring_message.1
  17.9 5.9 %collective-permute-start.2 = (bf16[128,640]{1,0:T(8,128)(2,1)S(1)}, bf16[128,640]{1,0:T(8,128)(2,1)S(1)}, u32[]{:S(2)}, u32[]{:S(2)}) collective-permute-start(bf16[128,640]{1,0:T(8,128)(2,1)S(1)} %get-tuple-element.80.refs_1_.refs_2_.refs_0_), channel_id=1, source_target_pairs={{0,224},{32,0},{64,32},{96,64},{128,96},{160,128},{192,160},{224,1... | collective-permute-start | bytes 491528 | tf_op jit(solution)/shard_map/ppermute | solution.py:29
  23.8 0.0 collective-permute-start
  23.8 0.1 pad_add_fusion.place.refs_0_
  23.9 2.8 %collective-permute-done.2.refs_2_.refs_1_ = bf16[128,640]{1,0:T(8,128)(2,1)S(1)} collective-permute-done((bf16[128,640]{1,0:T(8,128)(2,1)S(1)}, bf16[128,640]{1,0:T(8,128)(2,1)S(1)}, u32[]{:S(2)}, u32[]{:S(2)}) %collective-permute-start.2) | collective-permute-done | bytes 163872 | tf_op jit(solution)/shard_map/ppermute | solution.py:29
  26.6 3.7 %collective-permute-start.3 = (bf16[128,640]{1,0:T(8,128)(2,1)S(1)}, bf16[128,640]{1,0:T(8,128)(2,1)S(1)}, u32[]{:S(2)}, u32[]{:S(2)}) collective-permute-start(bf16[128,640]{1,0:T(8,128)(2,1)S(1)} %collective-permute-done.2.refs_2_.refs_1_), channel_id=1, source_target_pairs={{0,224},{32,0},{64,32},{96,64},{128,96},{160,128},{192,160},{224,1... | collective-permute-start | bytes 491528 | tf_op jit(solution)/shard_map/ppermute | solution.py:29
  30.3 0.0 collective-permute-done.refs_3_.refs_2_.refs_8_
  30.3 0.0 collective-permute-start.1
  30.3 2.0 %all-to-all-done.1.kv = bf16[8,2,2,128,128]{4,3,2,1,0:T(8,128)(2,1)S(1)} async-done(((bf16[8,2,2,128,128]{4,3,2,1,0:T(8,128)(2,1)}), bf16[8,2,2,128,128]{4,3,2,1,0:T(8,128)(2,1)S(1)}, u32[]{:S(2)}, u32[]{:S(2)}) %all-to-all-start.1) | async-done | bytes 1048608 | tf_op jit(solution)/shard_map/all_to_all | solution.py:453
  32.3 0.0 copy-done.2
  32.3 0.0 copy-done.3
  32.4 0.9 prepare.2
  33.3 4.5 %attend.8.refs_4_.refs_3_.refs_5_ = bf16[3,144,512]{2,1,0:T(8,128)(2,1)S(1)} custom-call(s32[2]{0:T(128)S(1)} %pad_add_fusion.place.refs_0_, bf16[128,640]{1,0:T(8,128)(2,1)S(1)} %get-tuple-element.80.refs_1_.refs_2_.refs_0_, bf16[128,640]{1,0:T(8,128)(2,1)S(1)} %collective-permute-done.2.refs_2_.refs_1_, ...), custom_call_target="tpu_custom_call" | custom-call | flops 3221225472 | bytes 3145728 | tf_op jit(solution)/shard_map/attend/pallas_call | solution.py:297
  37.8 0.0 copy-start.4
  37.8 0.8 copy-done.4
  38.5 0.0 collective-permute-done.3.refs_1_.refs_2_
  38.5 0.0 collective-permute-done.1.refs_2_.refs_7_
  38.5 4.0 %all-to-all-start.2 = ((bf16[8,2,2,128,128]{4,3,2,1,0:T(8,128)(2,1)}), bf16[8,2,2,128,128]{4,3,2,1,0:T(8,128)(2,1)S(1)}, u32[]{:S(2)}, u32[]{:S(2)}) async-start(bf16[8,2,2,128,128]{4,3,2,1,0:T(8,128)(2,1)} %get-tuple-element.59), calls=%async_computation.2 | async-start | bytes 2097152 | tf_op jit(solution)/shard_map/all_to_all | solution.py:473
  42.5 1.6 %collective-permute-start.4 = (bf16[128,640]{1,0:T(8,128)(2,1)S(1)}, bf16[128,640]{1,0:T(8,128)(2,1)S(1)}, u32[]{:S(2)}, u32[]{:S(2)}) collective-permute-start(bf16[128,640]{1,0:T(8,128)(2,1)S(1)} %collective-permute-done.1.refs_2_.refs_7_), channel_id=1, source_target_pairs={{0,32},{32,64},{64,96},{96,128},{128,160},{160,192},{192,224},{224... | collective-permute-start | bytes 491528 | tf_op jit(solution)/shard_map/ppermute | solution.py:29
  44.1 4.0 %collective-permute-start.6 = (bf16[128,640]{1,0:T(8,128)(2,1)S(1)}, bf16[128,640]{1,0:T(8,128)(2,1)S(1)}, u32[]{:S(2)}, u32[]{:S(2)}) collective-permute-start(bf16[128,640]{1,0:T(8,128)(2,1)S(1)} %collective-permute-done.3.refs_1_.refs_2_), channel_id=1, source_target_pairs={{0,224},{32,0},{64,32},{96,64},{128,96},{160,128},{192,160},{224,1... | collective-permute-start | bytes 491528 | tf_op jit(solution)/shard_map/ppermute | solution.py:29
  48.1 3.2 %collective-permute-done.4.refs_2_.refs_1_.refs_6_ = bf16[128,640]{1,0:T(8,128)(2,1)S(1)} collective-permute-done((bf16[128,640]{1,0:T(8,128)(2,1)S(1)}, bf16[128,640]{1,0:T(8,128)(2,1)S(1)}, u32[]{:S(2)}, u32[]{:S(2)}) %collective-permute-start.4) | collective-permute-done | bytes 163872 | tf_op jit(solution)/shard_map/ppermute | solution.py:29
  51.3 0.1 collective-permute-start.5
  51.4 0.0 collective-permute-done.6.refs_1_.refs_3_
  51.5 3.5 %collective-permute-start.7 = (bf16[64,640]{1,0:T(8,128)(2,1)S(1)}, bf16[64,640]{1,0:T(8,128)(2,1)S(1)}, u32[]{:S(2)}, u32[]{:S(2)}) collective-permute-start(bf16[64,640]{1,0:T(8,128)(2,1)S(1)} %slice.9), channel_id=1, source_target_pairs={{0,224},{32,0},{64,32},{96,64},{128,96},{160,128},{192,160},{224,1... | collective-permute-start | bytes 245768 | tf_op jit(solution)/shard_map/ppermute | solution.py:29
  54.9 3.3 %attend.9.refs_5_.refs_3_ = bf16[2,144,512]{2,1,0:T(8,128)(2,1)S(1)} custom-call(s32[2]{0:T(128)S(1)} %pad_add_fusion.place.refs_0_, bf16[128,640]{1,0:T(8,128)(2,1)S(1)} %collective-permute-done.6.refs_1_.refs_3_, bf16[128,640]{1,0:T(8,128)(2,1)S(1)} %collective-permute-done.4.refs_2_.refs_1_.refs_6_, ...), custom_call_target="tpu_custom_call" | custom-call | flops 2147483648 | bytes 3145728 | tf_op jit(solution)/shard_map/attend/pallas_call | solution.py:297
  58.2 0.0 copy-start.6
  58.2 0.7 copy-done.6
  58.9 0.0 collective-permute-done.5.refs_1_.refs_4_
  58.9 0.0 collective-permute-done.7.refs_2_.refs_5_
  58.9 0.0 all-to-all-done.2.kv
  59.0 0.9 prepare.3
  59.9 0.0 copy-start.7
  59.9 2.2 %attend.10.refs_4_ = bf16[1,144,512]{2,1,0:T(8,128)(2,1)S(1)} custom-call(s32[2]{0:T(128)S(1)} %pad_add_fusion.place.refs_0_, bf16[64,640]{1,0:T(8,128)(2,1)S(1)} %collective-permute-done.5.refs_1_.refs_4_, bf16[64,640]{1,0:T(8,128)(2,1)S(1)} %collective-permute-done.7.refs_2_.refs_5_, bf16[2048,128]{1,0:T(8,128)(2,1)S(1)} %get-tuple-element.55.refs_4_.refs_3_.refs_1_, ...), custom_call_target="tpu_custom_call" | custom-call | flops 1073741824 | bytes 3145728 | tf_op jit(solution)/shard_map/attend/pallas_call | solution.py:297
  62.1 0.0 copy-done.7
  62.1 0.0 copy-start.5
  62.1 3.4 %attend.11 = bf16[2,144,512]{2,1,0:T(8,128)(2,1)S(1)} custom-call(s32[2]{0:T(128)S(1)} %pad_add_fusion.place.refs_0_, bf16[64,640]{1,0:T(8,128)(2,1)S(1)} %collective-permute-done.5.refs_1_.refs_4_, bf16[64,640]{1,0:T(8,128)(2,1)S(1)} %collective-permute-done.7.refs_2_.refs_5_, bf16[128,640]{1,0:T(8,128)(2,1)S(1)} %collective-permute-done.6.refs_1_.refs_3_, ...), custom_call_target="tpu_custom_call" | custom-call | flops 2214592512 | bytes 3145728 | tf_op jit(solution)/shard_map/attend/pallas_call | solution.py:297
  65.6 0.9 collective-permute-start.8
  66.5 0.0 copy-done.5
  66.5 3.4 %attend.12 = (bf16[144,512]{1,0:T(8,128)(2,1)S(1)}, bf16[144,512]{1,0:T(8,128)(2,1)S(1)}) custom-call(s32[2]{0:T(128)S(1)} %pad_add_fusion.place.refs_0_, bf16[128,640]{1,0:T(8,128)(2,1)S(1)} %collective-permute-done.4.refs_2_.refs_1_.refs_6_, bf16[128,640]{1,0:T(8,128)(2,1)S(1)} %get-tuple-element.80.refs_1_.refs_2_.refs_0_, ...), custom_call_target="tpu_custom_call" | custom-call | flops 2214592512 | bytes 3145728 | tf_op jit(solution)/shard_map/attend/pallas_call | solution.py:297
  69.9 3.6 %collective-permute-start.11 = (bf16[144,512]{1,0:T(8,128)(2,1)S(1)}, bf16[144,512]{1,0:T(8,128)(2,1)S(1)}, u32[]{:S(2)}, u32[]{:S(2)}) collective-permute-start(bf16[144,512]{1,0:T(8,128)(2,1)S(1)} %get-tuple-element.71), channel_id=1, source_target_pairs={{0,192},{32,224},{64,0},{96,32},{128,64},{160,96},{192,128},{224,1... | collective-permute-start | bytes 442376 | tf_op jit(solution)/shard_map/ppermute | solution.py:29
  73.5 3.3 %attend.13.refs_3_.refs_5_ = bf16[2,144,512]{2,1,0:T(8,128)(2,1)S(1)} custom-call(s32[2]{0:T(128)S(1)} %pad_add_fusion.place.refs_0_, bf16[128,640]{1,0:T(8,128)(2,1)S(1)} %collective-permute-done.3.refs_1_.refs_2_, bf16[128,640]{1,0:T(8,128)(2,1)S(1)} %collective-permute-done.1.refs_2_.refs_7_, ...), custom_call_target="tpu_custom_call" | custom-call | flops 2147483648 | bytes 3145728 | tf_op jit(solution)/shard_map/attend/pallas_call | solution.py:297
  76.8 0.4 collective-permute-done.8.refs_4_
  77.2 3.4 %attend.14 = (bf16[144,512]{1,0:T(8,128)(2,1)S(1)}, bf16[144,512]{1,0:T(8,128)(2,1)S(1)}) custom-call(s32[2]{0:T(128)S(1)} %pad_add_fusion.place.refs_0_, bf16[128,640]{1,0:T(8,128)(2,1)S(1)} %collective-permute-done.3.refs_1_.refs_2_, bf16[128,640]{1,0:T(8,128)(2,1)S(1)} %collective-permute-done.1.refs_2_.refs_7_, ...), custom_call_target="tpu_custom_call" | custom-call | flops 2214592512 | bytes 3145728 | tf_op jit(solution)/shard_map/attend/pallas_call | solution.py:297
  80.6 0.0 collective-permute-done.11.refs_6_
  80.6 3.4 %attend.15 = (bf16[144,512]{1,0:T(8,128)(2,1)S(1)}, bf16[144,512]{1,0:T(8,128)(2,1)S(1)}) custom-call(s32[2]{0:T(128)S(1)} %pad_add_fusion.place.refs_0_, bf16[128,640]{1,0:T(8,128)(2,1)S(1)} %collective-permute-done.2.refs_2_.refs_1_, bf16[128,640]{1,0:T(8,128)(2,1)S(1)} %collective-permute-done.refs_3_.refs_2_.refs_8_, bf16[3,144,512]{2,1,0:T(8,128)(2,1)S(1)} %copy-done.5, ...), custom_call_target="tpu_custom_call" | custom-call | flops 2214592512 | bytes 3145728 | tf_op jit(solution)/shard_map/attend/pallas_call | solution.py:297
  84.1 4.2 %collective-permute-start.13 = (bf16[144,512]{1,0:T(8,128)(2,1)S(1)}, bf16[144,512]{1,0:T(8,128)(2,1)S(1)}, u32[]{:S(2)}, u32[]{:S(2)}) collective-permute-start(bf16[144,512]{1,0:T(8,128)(2,1)S(1)} %get-tuple-element.79), channel_id=1, source_target_pairs={{0,224},{32,0},{64,32},{96,64},{128,96},{160,128},{192,160},{224,1... | collective-permute-start | bytes 442376 | tf_op jit(solution)/shard_map/ppermute | solution.py:29
  88.3 0.0 collective-permute-start.12
  88.3 2.8 %collective-permute-start.10 = (bf16[144,512]{1,0:T(8,128)(2,1)S(1)}, bf16[144,512]{1,0:T(8,128)(2,1)S(1)}, u32[]{:S(2)}, u32[]{:S(2)}) collective-permute-start(bf16[144,512]{1,0:T(8,128)(2,1)S(1)} %get-tuple-element.75), channel_id=1, source_target_pairs={{0,192},{32,224},{64,0},{96,32},{128,64},{160,96},{192,128},{224,1... | collective-permute-start | bytes 442376 | tf_op jit(solution)/shard_map/ppermute | solution.py:29
  91.1 0.1 collective-permute-start.9
  91.2 0.9 windows.1.refs_5_
  92.2 0.1 collective-permute-done.13.refs_4_
  92.2 4.5 %collective-permute-done.12.refs_3_ = bf16[144,512]{1,0:T(8,128)(2,1)S(1)} collective-permute-done((bf16[144,512]{1,0:T(8,128)(2,1)S(1)}, bf16[144,512]{1,0:T(8,128)(2,1)S(1)}, u32[]{:S(2)}, u32[]{:S(2)}) %collective-permute-start.12) | collective-permute-done | bytes 147488 | tf_op jit(solution)/shard_map/ppermute | solution.py:29
  96.8 1.1 collective-permute-done.10.refs_2_
  97.9 1.9 %collective-permute-done.9.refs_1_ = bf16[144,512]{1,0:T(8,128)(2,1)S(1)} collective-permute-done((bf16[144,512]{1,0:T(8,128)(2,1)S(1)}, bf16[144,512]{1,0:T(8,128)(2,1)S(1)}, u32[]{:S(2)}, u32[]{:S(2)}) %collective-permute-start.9) | collective-permute-done | bytes 147488 | tf_op jit(solution)/shard_map/ppermute | solution.py:29
  99.8 0.2 merge.1
  100.0 0.0 copy-start
  100.0 12.9 %all_to_all.20.new_ref = bf16[8,320,128]{2,1,0:T(8,128)(2,1)S(1)} all-to-all(bf16[8,320,128]{2,1,0:T(8,128)(2,1)S(1)} %merge.1), channel_id=1, replica_groups=mesh['z'=8,'b'=8,'head'=2,'conv'=2] {'b'}, dimensions={0} | all-to-all | bytes 1310720 | tf_op jit(solution)/shard_map/all_to_all | solution.py:497
  112.9 0.0 copy-done.1
  112.9 2.0 %finish.1 = (bf16[2,8,4096]{2,1,0:T(8,128)(2,1)}, bf16[2,4,128,512]{3,2,1,0:T(8,128)(2,1)}, bf16[2,4,128,512]{3,2,1,0:T(8,128)(2,1)}) custom-call(s32[2]{0:T(128)S(1)} %pad_add_fusion.place.refs_0_, s32[2]{0:T(128)S(1)} %copy-done.3, s32[2,256]{1,0:T(2,128)S(1)} %copy-done.2, bf16[8,320,128]{2,1,0:T(8,128)(2,1)S(1)} %all_to_all.20.new_ref, ...), custom_call_target="tpu_custom_call" | custom-call | bytes 5242880 | tf_op jit(solution)/shard_map/finish/pallas_call | solution.py:430
  (6 shorter events, 0.0 us)
Async XLA Ops:
  2.3 11.9 %all-to-all-start = ((bf16[8,80,128]{2,1,0:T(8,128)(2,1)}), bf16[8,80,128]{2,1,0:T(8,128)(2,1)S(1)}, u32[]{:S(2)}, u32[]{:S(2)}) async-start(bf16[8,80,128]{2,1,0:T(8,128)(2,1)} %pack_turn.1), calls=%async_computation | async-start | bytes 327680 | tf_op jit(solution)/shard_map/all_to_all | solution.py:450
  14.2 18.1 %all-to-all-start.1 = ((bf16[8,2,2,128,128]{4,3,2,1,0:T(8,128)(2,1)}), bf16[8,2,2,128,128]{4,3,2,1,0:T(8,128)(2,1)S(1)}, u32[]{:S(2)}, u32[]{:S(2)}) async-start(bf16[8,2,2,128,128]{4,3,2,1,0:T(8,128)(2,1)} %get-tuple-element.54), calls=%async_computation.1 | async-start | bytes 2097152 | tf_op jit(solution)/shard_map/all_to_all | solution.py:453
  17.9 8.8 %collective-permute-start.2 = (bf16[128,640]{1,0:T(8,128)(2,1)S(1)}, bf16[128,640]{1,0:T(8,128)(2,1)S(1)}, u32[]{:S(2)}, u32[]{:S(2)}) collective-permute-start(bf16[128,640]{1,0:T(8,128)(2,1)S(1)} %get-tuple-element.80.refs_1_.refs_2_.refs_0_), channel_id=1, source_target_pairs={{0,224},{32,0},{64,32},{96,64},{128,96},{160,128},{192,160},{224,1... | collective-permute-start | bytes 491528 | tf_op jit(solution)/shard_map/ppermute | solution.py:29
  23.8 6.5 %collective-permute-start = (bf16[128,640]{1,0:T(8,128)(2,1)S(1)}, bf16[128,640]{1,0:T(8,128)(2,1)S(1)}, u32[]{:S(2)}, u32[]{:S(2)}) collective-permute-start(bf16[128,640]{1,0:T(8,128)(2,1)S(1)} %get-tuple-element.80.refs_1_.refs_2_.refs_0_), channel_id=1, source_target_pairs={{0,32},{32,64},{64,96},{96,128},{128,160},{160,192},{192,224},{224... | collective-permute-start | bytes 491528 | tf_op jit(solution)/shard_map/ppermute | solution.py:29
  23.8 8.6 %copy-start.2 = (s32[2,256]{1,0:T(2,128)S(1)}, s32[2,256]{1,0:T(2,128)}, u32[]{:S(2)}) copy-start(s32[2,256]{1,0:T(2,128)} %slots_ref.7) | copy-start | bytes 6148
  23.8 8.6 %copy-start.3 = (s32[2]{0:T(128)S(1)}, s32[2]{0:T(128)}, u32[]{:S(2)}) copy-start(s32[2]{0:T(128)} %lengths.7) | copy-start | bytes 28
  26.6 11.9 %collective-permute-start.3 = (bf16[128,640]{1,0:T(8,128)(2,1)S(1)}, bf16[128,640]{1,0:T(8,128)(2,1)S(1)}, u32[]{:S(2)}, u32[]{:S(2)}) collective-permute-start(bf16[128,640]{1,0:T(8,128)(2,1)S(1)} %collective-permute-done.2.refs_2_.refs_1_), channel_id=1, source_target_pairs={{0,224},{32,0},{64,32},{96,64},{128,96},{160,128},{192,160},{224,1... | collective-permute-start | bytes 491528 | tf_op jit(solution)/shard_map/ppermute | solution.py:29
  30.3 8.2 %collective-permute-start.1 = (bf16[128,640]{1,0:T(8,128)(2,1)S(1)}, bf16[128,640]{1,0:T(8,128)(2,1)S(1)}, u32[]{:S(2)}, u32[]{:S(2)}) collective-permute-start(bf16[128,640]{1,0:T(8,128)(2,1)S(1)} %collective-permute-done.refs_3_.refs_2_.refs_8_), channel_id=1, source_target_pairs={{0,32},{32,64},{64,96},{96,128},{128,160},{160,192},{192,224},{224... | collective-permute-start | bytes 491528 | tf_op jit(solution)/shard_map/ppermute | solution.py:29
  37.8 0.8 copy-start.4
  38.5 20.4 %all-to-all-start.2 = ((bf16[8,2,2,128,128]{4,3,2,1,0:T(8,128)(2,1)}), bf16[8,2,2,128,128]{4,3,2,1,0:T(8,128)(2,1)S(1)}, u32[]{:S(2)}, u32[]{:S(2)}) async-start(bf16[8,2,2,128,128]{4,3,2,1,0:T(8,128)(2,1)} %get-tuple-element.59), calls=%async_computation.2 | async-start | bytes 2097152 | tf_op jit(solution)/shard_map/all_to_all | solution.py:473
  42.5 8.9 %collective-permute-start.4 = (bf16[128,640]{1,0:T(8,128)(2,1)S(1)}, bf16[128,640]{1,0:T(8,128)(2,1)S(1)}, u32[]{:S(2)}, u32[]{:S(2)}) collective-permute-start(bf16[128,640]{1,0:T(8,128)(2,1)S(1)} %collective-permute-done.1.refs_2_.refs_7_), channel_id=1, source_target_pairs={{0,32},{32,64},{64,96},{96,128},{128,160},{160,192},{192,224},{224... | collective-permute-start | bytes 491528 | tf_op jit(solution)/shard_map/ppermute | solution.py:29
  44.1 7.3 %collective-permute-start.6 = (bf16[128,640]{1,0:T(8,128)(2,1)S(1)}, bf16[128,640]{1,0:T(8,128)(2,1)S(1)}, u32[]{:S(2)}, u32[]{:S(2)}) collective-permute-start(bf16[128,640]{1,0:T(8,128)(2,1)S(1)} %collective-permute-done.3.refs_1_.refs_2_), channel_id=1, source_target_pairs={{0,224},{32,0},{64,32},{96,64},{128,96},{160,128},{192,160},{224,1... | collective-permute-start | bytes 491528 | tf_op jit(solution)/shard_map/ppermute | solution.py:29
  51.3 7.6 %collective-permute-start.5 = (bf16[64,640]{1,0:T(8,128)(2,1)S(1)}, bf16[64,640]{1,0:T(8,128)(2,1)S(1)}, u32[]{:S(2)}, u32[]{:S(2)}) collective-permute-start(bf16[64,640]{1,0:T(8,128)(2,1)S(1)} %slice.8), channel_id=1, source_target_pairs={{0,32},{32,64},{64,96},{96,128},{128,160},{160,192},{192,224},{224... | collective-permute-start | bytes 245768 | tf_op jit(solution)/shard_map/ppermute | solution.py:29
  51.5 7.5 %collective-permute-start.7 = (bf16[64,640]{1,0:T(8,128)(2,1)S(1)}, bf16[64,640]{1,0:T(8,128)(2,1)S(1)}, u32[]{:S(2)}, u32[]{:S(2)}) collective-permute-start(bf16[64,640]{1,0:T(8,128)(2,1)S(1)} %slice.9), channel_id=1, source_target_pairs={{0,224},{32,0},{64,32},{96,64},{128,96},{160,128},{192,160},{224,1... | collective-permute-start | bytes 245768 | tf_op jit(solution)/shard_map/ppermute | solution.py:29
  58.2 0.7 copy-start.6
  59.9 2.2 %copy-start.7 = (bf16[2,144,512]{2,1,0:T(8,128)(2,1)S(1)}, bf16[2,144,512]{2,1,0:T(8,128)(2,1)}, u32[]{:S(2)}) copy-start(bf16[2,144,512]{2,1,0:T(8,128)(2,1)} %copy-done.6) | copy-start | bytes 884740
  62.1 4.4 %copy-start.5 = (bf16[3,144,512]{2,1,0:T(8,128)(2,1)S(1)}, bf16[3,144,512]{2,1,0:T(8,128)(2,1)}, u32[]{:S(2)}) copy-start(bf16[3,144,512]{2,1,0:T(8,128)(2,1)} %copy-done.4) | copy-start | bytes 1327108
  65.6 11.6 %collective-permute-start.8 = (bf16[2,144,512]{2,1,0:T(8,128)(2,1)S(1)}, bf16[2,144,512]{2,1,0:T(8,128)(2,1)S(1)}, u32[]{:S(2)}, u32[]{:S(2)}) collective-permute-start(bf16[2,144,512]{2,1,0:T(8,128)(2,1)S(1)} %attend.11), channel_id=1, source_target_pairs={{0,64},{32,96},{64,128},{96,160},{128,192},{160,224},{192,0},{224,... | collective-permute-start | bytes 884744 | tf_op jit(solution)/shard_map/ppermute | solution.py:29
  69.9 10.7 %collective-permute-start.11 = (bf16[144,512]{1,0:T(8,128)(2,1)S(1)}, bf16[144,512]{1,0:T(8,128)(2,1)S(1)}, u32[]{:S(2)}, u32[]{:S(2)}) collective-permute-start(bf16[144,512]{1,0:T(8,128)(2,1)S(1)} %get-tuple-element.71), channel_id=1, source_target_pairs={{0,192},{32,224},{64,0},{96,32},{128,64},{160,96},{192,128},{224,1... | collective-permute-start | bytes 442376 | tf_op jit(solution)/shard_map/ppermute | solution.py:29
  84.1 8.2 %collective-permute-start.13 = (bf16[144,512]{1,0:T(8,128)(2,1)S(1)}, bf16[144,512]{1,0:T(8,128)(2,1)S(1)}, u32[]{:S(2)}, u32[]{:S(2)}) collective-permute-start(bf16[144,512]{1,0:T(8,128)(2,1)S(1)} %get-tuple-element.79), channel_id=1, source_target_pairs={{0,224},{32,0},{64,32},{96,64},{128,96},{160,128},{192,160},{224,1... | collective-permute-start | bytes 442376 | tf_op jit(solution)/shard_map/ppermute | solution.py:29
  88.3 8.5 %collective-permute-start.12 = (bf16[144,512]{1,0:T(8,128)(2,1)S(1)}, bf16[144,512]{1,0:T(8,128)(2,1)S(1)}, u32[]{:S(2)}, u32[]{:S(2)}) collective-permute-start(bf16[144,512]{1,0:T(8,128)(2,1)S(1)} %get-tuple-element.78), channel_id=1, source_target_pairs={{0,32},{32,64},{64,96},{96,128},{128,160},{160,192},{192,224},{224... | collective-permute-start | bytes 442376 | tf_op jit(solution)/shard_map/ppermute | solution.py:29
  88.3 9.6 %collective-permute-start.10 = (bf16[144,512]{1,0:T(8,128)(2,1)S(1)}, bf16[144,512]{1,0:T(8,128)(2,1)S(1)}, u32[]{:S(2)}, u32[]{:S(2)}) collective-permute-start(bf16[144,512]{1,0:T(8,128)(2,1)S(1)} %get-tuple-element.75), channel_id=1, source_target_pairs={{0,192},{32,224},{64,0},{96,32},{128,64},{160,96},{192,128},{224,1... | collective-permute-start | bytes 442376 | tf_op jit(solution)/shard_map/ppermute | solution.py:29
  91.1 8.7 %collective-permute-start.9 = (bf16[144,512]{1,0:T(8,128)(2,1)S(1)}, bf16[144,512]{1,0:T(8,128)(2,1)S(1)}, u32[]{:S(2)}, u32[]{:S(2)}) collective-permute-start(bf16[144,512]{1,0:T(8,128)(2,1)S(1)} %get-tuple-element.74), channel_id=1, source_target_pairs={{0,64},{32,96},{64,128},{96,160},{128,192},{160,224},{192,0},{224,... | collective-permute-start | bytes 442376 | tf_op jit(solution)/shard_map/ppermute | solution.py:29
  99.8 13.1 %copy-start.1 = (bf16[2,4,128,512]{3,2,1,0:T(8,128)(2,1)S(1)}, bf16[2,4,128,512]{3,2,1,0:T(8,128)(2,1)}, u32[]{:S(2)}) copy-start(bf16[2,4,128,512]{3,2,1,0:T(8,128)(2,1)} %v_ref.1) | copy-start | bytes 3145732
  100.0 12.9 %copy-start = (bf16[2,4,128,512]{3,2,1,0:T(8,128)(2,1)S(1)}, bf16[2,4,128,512]{3,2,1,0:T(8,128)(2,1)}, u32[]{:S(2)}) copy-start(bf16[2,4,128,512]{3,2,1,0:T(8,128)(2,1)} %k_ref.1) | copy-start | bytes 3145732

commit v4 on v3

--- a/solution.py
+++ b/solution.py
@@ -51,7 +51,8 @@
                 pieces.append(q_ref[c, :, at : at + HEAD])
             pieces.append(k_ref[c, :, h * HEAD : (h + 1) * HEAD])
             pieces.append(v_ref[c, :, h * HEAD : (h + 1) * HEAD])
-            out_ref[c * heads + h] = jnp.concatenate(pieces, axis=0)
+            pieces = [piece.astype(F32) for piece in pieces]
+            out_ref[c * heads + h] = jnp.concatenate(pieces, axis=0).astype(BF16)
 
 
 def pack_turn(queries, new_keys, new_values):
@@ -75,9 +76,9 @@
     tokens = 8
     q_rows = count - 2 * tokens
     q = jnp.concatenate([rows_ref[s, 0:q_rows] for s in range(columns)], axis=0)
-    keys = [rows_ref[s, q_rows : q_rows + tokens] for s in range(columns)]
-    values = [rows_ref[s, q_rows + tokens :] for s in range(columns)]
-    new = jnp.concatenate(keys + values, axis=0)
+    news = [rows_ref[s, q_rows:].astype(F32) for s in range(columns)]
+    new = [held[:tokens] for held in news] + [held[tokens:] for held in news]
+    new = jnp.concatenate(new, axis=0).astype(BF16)
     out_ref[:, 0 : columns * q_rows] = q.T
     out_ref[:, columns * q_rows :] = new
     new_ref[...] = new
@@ -101,35 +102,35 @@
 
 def pack_cache_kernel(keys_ref, values_ref, *rest):
     outs, sems = rest[:-1], rest[-1]
-    convs, slots, _, width = keys_ref.shape
+    convs, _, _, width = keys_ref.shape
     heads = width // HEAD
-    per_out = slots // len(outs)
     copies = []
     for c in range(convs):
         for h in range(heads):
             for i, ref in enumerate((keys_ref, values_ref)):
-                for n, out in enumerate(outs):
-                    held = pl.ds(n * per_out, per_out)
+                at = 0
+                for out in outs:
                     copy = pltpu.make_async_copy(
-                        ref.at[c, held, :, pl.ds(h * HEAD, HEAD)],
+                        ref.at[c, pl.ds(at, out.shape[2]), :, pl.ds(h * HEAD, HEAD)],
                         out.at[c * heads + h, i],
                         sems.at[len(copies)],
                     )
                     copy.start()
                     copies.append(copy)
+                    at += out.shape[2]
     for copy in copies:
         copy.wait()
 
 
-def pack_cache(cache_keys, cache_values, count):
-    convs, slots, span, width = cache_keys.shape
+def pack_cache(cache_keys, cache_values, counts):
+    convs, _, span, width = cache_keys.shape
     pairs = convs * width // HEAD
     return pl.pallas_call(
         pack_cache_kernel,
         in_specs=[HBM, HBM],
-        out_specs=[VMEM] * count,
-        out_shape=[jax.ShapeDtypeStruct((pairs, 2, slots // count, span, HEAD), BF16)] * count,
-        scratch_shapes=[pltpu.SemaphoreType.DMA((2 * pairs * count,))],
+        out_specs=[VMEM] * len(counts),
+        out_shape=[jax.ShapeDtypeStruct((pairs, 2, count, span, HEAD), BF16) for count in counts],
+        scratch_shapes=[pltpu.SemaphoreType.DMA((2 * pairs * len(counts),))],
         compiler_params=pltpu.CompilerParams(vmem_limit_bytes=60 * MIB),
         name="pack_cache",
     )(cache_keys, cache_values)
@@ -399,9 +400,10 @@
     group = query_width // width
     done = tokens * group
     for h in range(heads):
+        held = new_ref[h, 0:done].astype(F32)
         for g in range(group):
             at = (h * group + g) * HEAD
-            out_ref[0, :, at : at + HEAD] = new_ref[h, g * tokens : (g + 1) * tokens]
+            out_ref[0, :, at : at + HEAD] = held[g * tokens : (g + 1) * tokens].astype(BF16)
     member = place[0] * COLUMNS + place[1]
     rotation = slots_ref[conv, 0] // slots
     slot, token = turn_slot(lengths[conv], rotation, member, slots, cycle, span)
@@ -448,7 +450,7 @@
     turn_rows = pack_turn(queries, new_keys, new_values)
     turn_rows, cache_k, cache_v = tie((turn_rows, cache_keys, cache_values))
     turn_rows = lax.all_to_all(turn_rows, "b", 0, 0, tiled=True)
-    first, second = pack_cache(cache_k, cache_v, 2)
+    first, second = pack_cache(cache_k, cache_v, (1, slots - 1))
     turn_rows, first, second = tie((turn_rows, first, second))
     first = lax.all_to_all(first, "b", 0, 0, tiled=True)
 
@@ -466,31 +468,30 @@
         return attend(place, kv, held, distances, inits, parts, kv is far, joined)
 
     chunks[7], chunks[1] = shift(message, 1), shift(message, -1)
+    second, chunks[7], chunks[1] = tie((second, chunks[7], chunks[1]))
+    second = lax.all_to_all(second, "b", 0, 0, tiled=True)
     chunks[6], chunks[2] = shift(chunks[7], 1), shift(chunks[1], -1)
     near = prepare(place, lengths, span_slots, 0, first, cycle)
     n017 = run(near, (0, 1, 7))
-    second, chunks[6], chunks[2], n017 = tie((second, chunks[6], chunks[2], n017))
-    second = lax.all_to_all(second, "b", 0, 0, tiled=True)
+    chunks[6], chunks[2], n017 = tie((chunks[6], chunks[2], n017))
     chunks[5], chunks[3] = shift(chunks[6], 1), shift(chunks[2], -1)
-    below, above = shift(chunks[5][:half], 1), shift(chunks[3][half:], -1)
-    n35 = run(near, (3, 5))
-    below, above, n35, second = tie((below, above, n35, second))
-    far = prepare(place, lengths, span_slots, slots // 2, second, cycle, new, near[0])
-    chunks[4] = (below, above)
-    n4 = run(near, (4,))
-
-    ups = run(far, (4, 3), (((n4, 0),), ((n35, 0),)))
-    down3, own = run(far, (5, 0), (((n35, 1),), ((n017, 0),)), (ups,), False)
-    ups = shift(ups, 2)
-    n26 = run(near, (2, 6), after=(down3,))
+    chunks[4] = (shift(chunks[6][:half], 2), shift(chunks[2][half:], -2))
+    n26 = run(near, (2, 6), after=(n017,))
+    n435 = run(near, (4, 3, 5), after=(n26,))
+    n435, second = tie((n435, second))
+    far = prepare(place, lengths, span_slots, 1, second, cycle, new, near[0])
+
+    up4, up3 = run(far, (4, 3), (((n435, 0),), ((n435, 1),)), joined=False)
+    down3, own = run(far, (5, 0), (((n435, 2),), ((n017, 0),)), (up4,), False)
+    up4, up3 = shift(up4, 2), shift(up3, 2)
+    up2, down2 = run(far, (2, 6), (((n26, 0), (up4,)), ((n26, 1),)), (down3,), False)
     down3 = shift(down3, -2)
-    up2, down2 = run(far, (2, 6), (((n26, 0), (ups, 0)), ((n26, 1),)), joined=False)
     up1, down1 = run(
-        far, (1, 7), (((n017, 1), (ups, 1)), ((n017, 2), (down3,))), (up2,), False
+        far, (1, 7), (((n017, 1), (up3,)), ((n017, 2), (down3,))), (up2,), False
     )
     up2, down2 = shift(up2, 2), shift(down2, -2)
     seen = [c if isinstance(c, tuple) else (c,) for c in chunks]
-    seen, _ = tie((seen, up1))
+    seen, up2, down2 = tie((seen, up2, down2))
     rows = windows(place, lengths, span_slots, seen, slots, span, cycle)
     up1, down1 = shift(up1, 1), shift(down1, -1)
     rows = merge([own, up2, down2, up1, down1], rows)

time: 116 us -> 114 us (0.983)
  waiting for transfers between devices: 19.6 us -> 15.7 us
  blocking collectives: 12.9 us -> 15.5 us
    all_to_all x1, blocking collectives: 12.9 us -> 15.5 us  [on_device(): rows = lax.all_to_all(rows, 'b', 0, 0, tiled=True)]
    ppermute x14 -> x15, starting transfers between devices: 30.5 us -> 28.4 us  [shift(): return lax.ppermute(a, 'z', [(i, (i + by) % size) for i in range(size)])]
    all_to_all x1, waiting for transfers between devices: 2.01 us -> 0.01 us  [on_device(): first = lax.all_to_all(first, 'b', 0, 0, tiled=True)]
    ppermute x14 -> x15, waiting for transfers between devices: 14 us -> 12.2 us  [shift(): return lax.ppermute(a, 'z', [(i, (i + by) % size) for i in range(size)])]
    all_to_all x1, starting transfers between devices: 3.95 us -> 5.63 us  [on_device(): second = lax.all_to_all(second, 'b', 0, 0, tiled=True)]
    pallas_call x8 -> x7, Pallas kernels: 26.9 us -> 25.9 us  [attend(): pl.pallas_call(functools.partial(attend_kernel, parts, distances, cuts, p...]
  transfers between devices with their start and end apart: 17 -> 18, of which waited for: 9 -> 6; matrix products, arithmetic and copies ran while one was open for 0% -> 0% of each run, Pallas kernels for 20% -> 23%
where the time goes in v4:
time: 114 us; the launch traced here: 113 us
  starting transfers between devices  42.7 us (37%)
  Pallas kernels  36 us (32%)
  waiting for transfers between devices  15.7 us (14%)
  blocking collectives  15.5 us (14%)
  local copies, waits for them, and re-layouts  2.27 us (2%)
    ppermute x15, starting transfers between devices, shift(): return lax.ppermute(a, 'z', [(i, (i + by) % size) for i in range(size)])  28.4 us
    pallas_call x7, Pallas kernels, attend(): pl.pallas_call(functools.partial(attend_kernel, parts, distances, cuts, p...  25.9 us
    all_to_all x1, blocking collectives, on_device(): rows = lax.all_to_all(rows, 'b', 0, 0, tiled=True)  15.5 us
    ppermute x15, waiting for transfers between devices, shift(): return lax.ppermute(a, 'z', [(i, (i + by) % size) for i in range(size)])  12.2 us
    all_to_all x1, starting transfers between devices, on_device(): second = lax.all_to_all(second, 'b', 0, 0, tiled=True)  5.63 us
    all_to_all x1, starting transfers between devices, on_device(): turn_rows = lax.all_to_all(turn_rows, 'b', 0, 0, tiled=True)  5.12 us
    all_to_all x1, waiting for transfers between devices, on_device(): turn_rows = lax.all_to_all(turn_rows, 'b', 0, 0, tiled=True)  3.51 us
    all_to_all x1, starting transfers between devices, on_device(): first = lax.all_to_all(first, 'b', 0, 0, tiled=True)  3.49 us
  transfers between devices with their start and end apart: 18, of which 6 were waited for; matrix products, arithmetic and copies ran while one was open for 0% of the time, Pallas kernels for 23%

profile of v4, /device:TPU:4, one launch (start us, length us, event | category | flops | bytes accessed | tf_op | source)
XLA Modules:
  0.0 113.1 jit_solution(5959633216333662014)
XLA Ops:
  0.6 1.6 %pack_turn.1 = bf16[8,80,128]{2,1,0:T(8,128)(2,1)} custom-call(bf16[2,8,4096]{2,1,0:T(8,128)(2,1)} %refs_0_.1, bf16[2,8,512]{2,1,0:T(8,128)(2,1)} %refs_1_.1, bf16[2,8,512]{2,1,0:T(8,128)(2,1)} %refs_2_.1), custom_call_target="tpu_custom_call" | custom-call | tf_op jit(solution)/shard_map/pack_turn/pallas_call | solution.py:62
  2.3 5.1 %all-to-all-start = ((bf16[8,80,128]{2,1,0:T(8,128)(2,1)}), bf16[8,80,128]{2,1,0:T(8,128)(2,1)S(1)}, u32[]{:S(2)}, u32[]{:S(2)}) async-start(bf16[8,80,128]{2,1,0:T(8,128)(2,1)} %pack_turn.1), calls=%async_computation | async-start | bytes 327680 | tf_op jit(solution)/shard_map/all_to_all | solution.py:452
  7.4 3.3 %pack_cache.1 = (bf16[8,2,1,128,128]{4,3,2,1,0:T(8,128)(2,1)}, bf16[8,2,3,128,128]{4,3,2,1,0:T(8,128)(2,1)}) custom-call(bf16[2,4,128,512]{3,2,1,0:T(8,128)(2,1)} %k_ref.1, bf16[2,4,128,512]{3,2,1,0:T(8,128)(2,1)} %v_ref.1), custom_call_target="tpu_custom_call" | custom-call | tf_op jit(solution)/shard_map/pack_cache/pallas_call | solution.py:128
  10.7 3.5 %all-to-all-done.rows_ref = bf16[8,80,128]{2,1,0:T(8,128)(2,1)S(1)} async-done(((bf16[8,80,128]{2,1,0:T(8,128)(2,1)}), bf16[8,80,128]{2,1,0:T(8,128)(2,1)S(1)}, u32[]{:S(2)}, u32[]{:S(2)}) %all-to-all-start) | async-done | bytes 163872 | tf_op jit(solution)/shard_map/all_to_all | solution.py:452
  14.2 3.5 %all-to-all-start.1 = ((bf16[8,2,1,128,128]{4,3,2,1,0:T(8,128)(2,1)}), bf16[8,2,1,128,128]{4,3,2,1,0:T(8,128)(2,1)S(1)}, u32[]{:S(2)}, u32[]{:S(2)}) async-start(bf16[8,2,1,128,128]{4,3,2,1,0:T(8,128)(2,1)} %get-tuple-element.66), calls=%async_computation.1 | async-start | bytes 1048576 | tf_op jit(solution)/shard_map/all_to_all | solution.py:455
  17.7 0.1 ring_message.1
  17.8 0.0 copy-start.2
  17.8 0.0 copy-start.3
  17.8 5.9 %collective-permute-start.1 = (bf16[128,640]{1,0:T(8,128)(2,1)S(1)}, bf16[128,640]{1,0:T(8,128)(2,1)S(1)}, u32[]{:S(2)}, u32[]{:S(2)}) collective-permute-start(bf16[128,640]{1,0:T(8,128)(2,1)S(1)} %get-tuple-element.100.refs_1_.refs_2_.refs_0_), channel_id=1, source_target_pairs={{0,224},{32,0},{64,32},{96,64},{128,96},{160,128},{192,160},{224,1... | collective-permute-start | bytes 491528 | tf_op jit(solution)/shard_map/ppermute | solution.py:29
  23.8 0.0 collective-permute-start
  23.8 2.8 %collective-permute-done.1.refs_2_.refs_1_ = bf16[128,640]{1,0:T(8,128)(2,1)S(1)} collective-permute-done((bf16[128,640]{1,0:T(8,128)(2,1)S(1)}, bf16[128,640]{1,0:T(8,128)(2,1)S(1)}, u32[]{:S(2)}, u32[]{:S(2)}) %collective-permute-start.1) | collective-permute-done | bytes 163872 | tf_op jit(solution)/shard_map/ppermute | solution.py:29
  26.6 3.7 %collective-permute-done.refs_3_.refs_2_.refs_8_ = bf16[128,640]{1,0:T(8,128)(2,1)S(1)} collective-permute-done((bf16[128,640]{1,0:T(8,128)(2,1)S(1)}, bf16[128,640]{1,0:T(8,128)(2,1)S(1)}, u32[]{:S(2)}, u32[]{:S(2)}) %collective-permute-start) | collective-permute-done | bytes 163872 | tf_op jit(solution)/shard_map/ppermute | solution.py:29
  30.3 0.0 all-to-all-done.1.kv
  30.3 5.6 %all-to-all-start.2 = ((bf16[8,2,3,128,128]{4,3,2,1,0:T(8,128)(2,1)}), bf16[8,2,3,128,128]{4,3,2,1,0:T(8,128)(2,1)S(1)}, u32[]{:S(2)}, u32[]{:S(2)}) async-start(bf16[8,2,3,128,128]{4,3,2,1,0:T(8,128)(2,1)} %get-tuple-element.78), calls=%async_computation.2 | async-start | bytes 3145728 | tf_op jit(solution)/shard_map/all_to_all | solution.py:472
  35.9 0.0 collective-permute-start.2
  35.9 3.2 %collective-permute-start.3 = (bf16[128,640]{1,0:T(8,128)(2,1)S(1)}, bf16[128,640]{1,0:T(8,128)(2,1)S(1)}, u32[]{:S(2)}, u32[]{:S(2)}) collective-permute-start(bf16[128,640]{1,0:T(8,128)(2,1)S(1)} %collective-permute-done.1.refs_2_.refs_1_), channel_id=1, source_target_pairs={{0,224},{32,0},{64,32},{96,64},{128,96},{160,128},{192,160},{224,1... | collective-permute-start | bytes 491528 | tf_op jit(solution)/shard_map/ppermute | solution.py:29
  39.2 0.1 pad_add_fusion.place.refs_0_
  39.2 0.0 copy-done.3
  39.2 0.8 prepare.2
  40.0 2.6 %attend.7.refs_4_.refs_3_.refs_5_ = bf16[3,144,512]{2,1,0:T(8,128)(2,1)S(1)} custom-call(s32[2]{0:T(128)S(1)} %pad_add_fusion.place.refs_0_, bf16[128,640]{1,0:T(8,128)(2,1)S(1)} %get-tuple-element.100.refs_1_.refs_2_.refs_0_, bf16[128,640]{1,0:T(8,128)(2,1)S(1)} %collective-permute-done.1.refs_2_.refs_1_, ...), custom_call_target="tpu_custom_call" | custom-call | flops 1610612736 | bytes 3145728 | tf_op jit(solution)/shard_map/attend/pallas_call | solution.py:298
  42.6 0.0 copy-start.6
  42.7 0.8 copy-done.6
  43.4 0.0 collective-permute-done.2.refs_2_.refs_7_
  43.4 0.0 collective-permute-done.3.refs_1_.refs_2_
  43.4 0.0 collective-permute-start.4
  43.4 3.2 %collective-permute-start.7 = (bf16[128,640]{1,0:T(8,128)(2,1)S(1)}, bf16[128,640]{1,0:T(8,128)(2,1)S(1)}, u32[]{:S(2)}, u32[]{:S(2)}) collective-permute-start(bf16[128,640]{1,0:T(8,128)(2,1)S(1)} %collective-permute-done.3.refs_1_.refs_2_), channel_id=1, source_target_pairs={{0,224},{32,0},{64,32},{96,64},{128,96},{160,128},{192,160},{224,1... | collective-permute-start | bytes 491528 | tf_op jit(solution)/shard_map/ppermute | solution.py:29
  46.7 0.6 collective-permute-start.6
  47.3 2.4 %collective-permute-start.5 = (bf16[64,640]{1,0:T(8,128)(2,1)S(1)}, bf16[64,640]{1,0:T(8,128)(2,1)S(1)}, u32[]{:S(2)}, u32[]{:S(2)}) collective-permute-start(bf16[64,640]{1,0:T(8,128)(2,1)S(1)} %slice.6), channel_id=1, source_target_pairs={{0,64},{32,96},{64,128},{96,160},{128,192},{160,224},{192,0},{224,... | collective-permute-start | bytes 245768 | tf_op jit(solution)/shard_map/ppermute | solution.py:29
  49.7 2.0 %attend.8.refs_3_.refs_5_ = bf16[2,144,512]{2,1,0:T(8,128)(2,1)S(1)} custom-call(s32[2]{0:T(128)S(1)} %pad_add_fusion.place.refs_0_, bf16[128,640]{1,0:T(8,128)(2,1)S(1)} %collective-permute-done.3.refs_1_.refs_2_, bf16[128,640]{1,0:T(8,128)(2,1)S(1)} %collective-permute-done.2.refs_2_.refs_7_, ...), custom_call_target="tpu_custom_call" | custom-call | flops 1073741824 | bytes 3145728 | tf_op jit(solution)/shard_map/attend/pallas_call | solution.py:298
  51.7 0.7 copy-done.4
  52.4 0.0 collective-permute-done.6.refs_2_.refs_5_
  52.4 1.5 %collective-permute-done.5.refs_1_.refs_4_ = bf16[64,640]{1,0:T(8,128)(2,1)S(1)} collective-permute-done((bf16[64,640]{1,0:T(8,128)(2,1)S(1)}, bf16[64,640]{1,0:T(8,128)(2,1)S(1)}, u32[]{:S(2)}, u32[]{:S(2)}) %collective-permute-start.5) | collective-permute-done | bytes 81952 | tf_op jit(solution)/shard_map/ppermute | solution.py:29
  53.8 0.0 collective-permute-done.4.refs_4_.refs_1_.refs_6_
  53.8 0.0 collective-permute-done.7.refs_3_
  53.9 2.6 %attend.9.refs_4_.refs_5_.refs_3_ = bf16[3,144,512]{2,1,0:T(8,128)(2,1)S(1)} custom-call(s32[2]{0:T(128)S(1)} %pad_add_fusion.place.refs_0_, bf16[64,640]{1,0:T(8,128)(2,1)S(1)} %collective-permute-done.5.refs_1_.refs_4_, bf16[64,640]{1,0:T(8,128)(2,1)S(1)} %collective-permute-done.6.refs_2_.refs_5_, bf16[128,640]{1,0:T(8,128)(2,1)S(1)} %collective-permute-done.7.refs_3_, ...), custom_call_target="tpu_custom_call" | custom-call | flops 1610612736 | bytes 3145728 | tf_op jit(solution)/shard_map/attend/pallas_call | solution.py:298
  56.5 0.0 copy-start.8
  56.5 0.8 copy-done.8
  57.3 0.0 all-to-all-done.2.kv
  57.3 1.0 prepare.3
  58.3 0.0 copy-done.9
  58.3 0.0 copy-start.7
  58.3 4.7 %attend.10 = (bf16[144,512]{1,0:T(8,128)(2,1)S(1)}, bf16[144,512]{1,0:T(8,128)(2,1)S(1)}) custom-call(s32[2]{0:T(128)S(1)} %pad_add_fusion.place.refs_0_, bf16[64,640]{1,0:T(8,128)(2,1)S(1)} %collective-permute-done.5.refs_1_.refs_4_, bf16[64,640]{1,0:T(8,128)(2,1)S(1)} %collective-permute-done.6.refs_2_.refs_5_, ...), custom_call_target="tpu_custom_call" | custom-call | flops 3288334336 | bytes 3145728 | tf_op jit(solution)/shard_map/attend/pallas_call | solution.py:298
  63.0 0.0 copy-start.5
  63.0 1.5 %collective-permute-start.8 = (bf16[144,512]{1,0:T(8,128)(2,1)S(1)}, bf16[144,512]{1,0:T(8,128)(2,1)S(1)}, u32[]{:S(2)}, u32[]{:S(2)}) collective-permute-start(bf16[144,512]{1,0:T(8,128)(2,1)S(1)} %get-tuple-element.84), channel_id=1, source_target_pairs={{0,64},{32,96},{64,128},{96,160},{128,192},{160,224},{192,0},{224,... | collective-permute-start | bytes 442376 | tf_op jit(solution)/shard_map/ppermute | solution.py:29
  64.5 4.7 %attend.11 = (bf16[144,512]{1,0:T(8,128)(2,1)S(1)}, bf16[144,512]{1,0:T(8,128)(2,1)S(1)}) custom-call(s32[2]{0:T(128)S(1)} %pad_add_fusion.place.refs_0_, bf16[128,640]{1,0:T(8,128)(2,1)S(1)} %collective-permute-done.4.refs_4_.refs_1_.refs_6_, bf16[128,640]{1,0:T(8,128)(2,1)S(1)} %get-tuple-element.100.refs_1_.refs_2_.refs_0_, ...), custom_call_target="tpu_custom_call" | custom-call | flops 3288334336 | bytes 3145728 | tf_op jit(solution)/shard_map/attend/pallas_call | solution.py:298
  69.2 3.0 %collective-permute-start.12 = (bf16[144,512]{1,0:T(8,128)(2,1)S(1)}, bf16[144,512]{1,0:T(8,128)(2,1)S(1)}, u32[]{:S(2)}, u32[]{:S(2)}) collective-permute-start(bf16[144,512]{1,0:T(8,128)(2,1)S(1)} %get-tuple-element.88), channel_id=1, source_target_pairs={{0,192},{32,224},{64,0},{96,32},{128,64},{160,96},{192,128},{224,1... | collective-permute-start | bytes 442376 | tf_op jit(solution)/shard_map/ppermute | solution.py:29
  72.2 0.0 collective-permute-start.11
  72.2 0.0 collective-permute-done.8.refs_4_
  72.2 4.7 %attend.12 = (bf16[144,512]{1,0:T(8,128)(2,1)S(1)}, bf16[144,512]{1,0:T(8,128)(2,1)S(1)}) custom-call(s32[2]{0:T(128)S(1)} %pad_add_fusion.place.refs_0_, bf16[128,640]{1,0:T(8,128)(2,1)S(1)} %collective-permute-done.3.refs_1_.refs_2_, bf16[128,640]{1,0:T(8,128)(2,1)S(1)} %collective-permute-done.2.refs_2_.refs_7_, bf16[2,144,512]{2,1,0:T(8,128)(2,1)S(1)} %copy-done.5, ...), custom_call_target="tpu_custom_call" | custom-call | flops 3288334336 | bytes 3145728 | tf_op jit(solution)/shard_map/attend/pallas_call | solution.py:298
  76.9 3.3 %collective-permute-start.9 = (bf16[144,512]{1,0:T(8,128)(2,1)S(1)}, bf16[144,512]{1,0:T(8,128)(2,1)S(1)}, u32[]{:S(2)}, u32[]{:S(2)}) collective-permute-start(bf16[144,512]{1,0:T(8,128)(2,1)S(1)} %get-tuple-element.91), channel_id=1, source_target_pairs={{0,64},{32,96},{64,128},{96,160},{128,192},{160,224},{192,0},{224,... | collective-permute-start | bytes 442376 | tf_op jit(solution)/shard_map/ppermute | solution.py:29
  80.3 1.2 %collective-permute-start.10 = (bf16[144,512]{1,0:T(8,128)(2,1)S(1)}, bf16[144,512]{1,0:T(8,128)(2,1)S(1)}, u32[]{:S(2)}, u32[]{:S(2)}) collective-permute-start(bf16[144,512]{1,0:T(8,128)(2,1)S(1)} %get-tuple-element.92), channel_id=1, source_target_pairs={{0,192},{32,224},{64,0},{96,32},{128,64},{160,96},{192,128},{224,1... | collective-permute-start | bytes 442376 | tf_op jit(solution)/shard_map/ppermute | solution.py:29
  81.5 0.0 collective-permute-done.12.refs_6_
  81.5 0.0 collective-permute-done.11.refs_4_
  81.5 4.6 %attend.13 = (bf16[144,512]{1,0:T(8,128)(2,1)S(1)}, bf16[144,512]{1,0:T(8,128)(2,1)S(1)}) custom-call(s32[2]{0:T(128)S(1)} %pad_add_fusion.place.refs_0_, bf16[128,640]{1,0:T(8,128)(2,1)S(1)} %collective-permute-done.1.refs_2_.refs_1_, bf16[128,640]{1,0:T(8,128)(2,1)S(1)} %collective-permute-done.refs_3_.refs_2_.refs_8_, bf16[3,144,512]{2,1,0:T(8,128)(2,1)S(1)} %copy-done.7, ...), custom_call_target="tpu_custom_call" | custom-call | flops 3288334336 | bytes 3145728 | tf_op jit(solution)/shard_map/attend/pallas_call | solution.py:298
  86.1 3.9 %collective-permute-start.13 = (bf16[144,512]{1,0:T(8,128)(2,1)S(1)}, bf16[144,512]{1,0:T(8,128)(2,1)S(1)}, u32[]{:S(2)}, u32[]{:S(2)}) collective-permute-start(bf16[144,512]{1,0:T(8,128)(2,1)S(1)} %get-tuple-element.98), channel_id=1, source_target_pairs={{0,32},{32,64},{64,96},{96,128},{128,160},{160,192},{192,224},{224... | collective-permute-start | bytes 442376 | tf_op jit(solution)/shard_map/ppermute | solution.py:29
  90.1 0.0 collective-permute-start.14
  90.1 0.0 collective-permute-done.10.refs_2_
  90.1 0.0 collective-permute-done.9.refs_1_
  90.1 1.0 windows.1.refs_5_
  91.1 1.7 %collective-permute-done.13.refs_3_ = bf16[144,512]{1,0:T(8,128)(2,1)S(1)} collective-permute-done((bf16[144,512]{1,0:T(8,128)(2,1)S(1)}, bf16[144,512]{1,0:T(8,128)(2,1)S(1)}, u32[]{:S(2)}, u32[]{:S(2)}) %collective-permute-start.13) | collective-permute-done | bytes 147488 | tf_op jit(solution)/shard_map/ppermute | solution.py:29
  92.8 2.5 %collective-permute-done.14.refs_4_ = bf16[144,512]{1,0:T(8,128)(2,1)S(1)} collective-permute-done((bf16[144,512]{1,0:T(8,128)(2,1)S(1)}, bf16[144,512]{1,0:T(8,128)(2,1)S(1)}, u32[]{:S(2)}, u32[]{:S(2)}) %collective-permute-start.14) | collective-permute-done | bytes 147488 | tf_op jit(solution)/shard_map/ppermute | solution.py:29
  95.2 0.2 merge.1
  95.5 15.5 %all_to_all.20.new_ref = bf16[8,320,128]{2,1,0:T(8,128)(2,1)S(1)} all-to-all(bf16[8,320,128]{2,1,0:T(8,128)(2,1)S(1)} %merge.1), channel_id=1, replica_groups=mesh['z'=8,'b'=8,'head'=2,'conv'=2] {'b'}, dimensions={0} | all-to-all | bytes 1310720 | tf_op jit(solution)/shard_map/all_to_all | solution.py:498
  111.0 2.0 %finish.1 = (bf16[2,8,4096]{2,1,0:T(8,128)(2,1)}, bf16[2,4,128,512]{3,2,1,0:T(8,128)(2,1)}, bf16[2,4,128,512]{3,2,1,0:T(8,128)(2,1)}) custom-call(s32[2]{0:T(128)S(1)} %pad_add_fusion.place.refs_0_, s32[2]{0:T(128)S(1)} %copy-done.3, s32[2,256]{1,0:T(2,128)S(1)} %copy-done.2, bf16[8,320,128]{2,1,0:T(8,128)(2,1)S(1)} %all_to_all.20.new_ref, ...), custom_call_target="tpu_custom_call" | custom-call | bytes 5242880 | tf_op jit(solution)/shard_map/finish/pallas_call | solution.py:432
  (11 shorter events, 0.0 us)
Async XLA Ops:
  2.3 11.9 %all-to-all-start = ((bf16[8,80,128]{2,1,0:T(8,128)(2,1)}), bf16[8,80,128]{2,1,0:T(8,128)(2,1)S(1)}, u32[]{:S(2)}, u32[]{:S(2)}) async-start(bf16[8,80,128]{2,1,0:T(8,128)(2,1)} %pack_turn.1), calls=%async_computation | async-start | bytes 327680 | tf_op jit(solution)/shard_map/all_to_all | solution.py:452
  14.2 16.1 %all-to-all-start.1 = ((bf16[8,2,1,128,128]{4,3,2,1,0:T(8,128)(2,1)}), bf16[8,2,1,128,128]{4,3,2,1,0:T(8,128)(2,1)S(1)}, u32[]{:S(2)}, u32[]{:S(2)}) async-start(bf16[8,2,1,128,128]{4,3,2,1,0:T(8,128)(2,1)} %get-tuple-element.66), calls=%async_computation.1 | async-start | bytes 1048576 | tf_op jit(solution)/shard_map/all_to_all | solution.py:455
  17.8 21.4 %copy-start.2 = (s32[2,256]{1,0:T(2,128)S(1)}, s32[2,256]{1,0:T(2,128)}, u32[]{:S(2)}) copy-start(s32[2,256]{1,0:T(2,128)} %slots_ref.7) | copy-start | bytes 6148
  17.8 21.4 %copy-start.3 = (s32[2]{0:T(128)S(1)}, s32[2]{0:T(128)}, u32[]{:S(2)}) copy-start(s32[2]{0:T(128)} %lengths.7) | copy-start | bytes 28
  17.8 8.8 %collective-permute-start.1 = (bf16[128,640]{1,0:T(8,128)(2,1)S(1)}, bf16[128,640]{1,0:T(8,128)(2,1)S(1)}, u32[]{:S(2)}, u32[]{:S(2)}) collective-permute-start(bf16[128,640]{1,0:T(8,128)(2,1)S(1)} %get-tuple-element.100.refs_1_.refs_2_.refs_0_), channel_id=1, source_target_pairs={{0,224},{32,0},{64,32},{96,64},{128,96},{160,128},{192,160},{224,1... | collective-permute-start | bytes 491528 | tf_op jit(solution)/shard_map/ppermute | solution.py:29
  23.8 6.5 %collective-permute-start = (bf16[128,640]{1,0:T(8,128)(2,1)S(1)}, bf16[128,640]{1,0:T(8,128)(2,1)S(1)}, u32[]{:S(2)}, u32[]{:S(2)}) collective-permute-start(bf16[128,640]{1,0:T(8,128)(2,1)S(1)} %get-tuple-element.100.refs_1_.refs_2_.refs_0_), channel_id=1, source_target_pairs={{0,32},{32,64},{64,96},{96,128},{128,160},{160,192},{192,224},{224... | collective-permute-start | bytes 491528 | tf_op jit(solution)/shard_map/ppermute | solution.py:29
  30.3 27.0 %all-to-all-start.2 = ((bf16[8,2,3,128,128]{4,3,2,1,0:T(8,128)(2,1)}), bf16[8,2,3,128,128]{4,3,2,1,0:T(8,128)(2,1)S(1)}, u32[]{:S(2)}, u32[]{:S(2)}) async-start(bf16[8,2,3,128,128]{4,3,2,1,0:T(8,128)(2,1)} %get-tuple-element.78), calls=%async_computation.2 | async-start | bytes 3145728 | tf_op jit(solution)/shard_map/all_to_all | solution.py:472
  35.9 7.5 %collective-permute-start.2 = (bf16[128,640]{1,0:T(8,128)(2,1)S(1)}, bf16[128,640]{1,0:T(8,128)(2,1)S(1)}, u32[]{:S(2)}, u32[]{:S(2)}) collective-permute-start(bf16[128,640]{1,0:T(8,128)(2,1)S(1)} %collective-permute-done.refs_3_.refs_2_.refs_8_), channel_id=1, source_target_pairs={{0,32},{32,64},{64,96},{96,128},{128,160},{160,192},{192,224},{224... | collective-permute-start | bytes 491528 | tf_op jit(solution)/shard_map/ppermute | solution.py:29
  35.9 7.5 %collective-permute-start.3 = (bf16[128,640]{1,0:T(8,128)(2,1)S(1)}, bf16[128,640]{1,0:T(8,128)(2,1)S(1)}, u32[]{:S(2)}, u32[]{:S(2)}) collective-permute-start(bf16[128,640]{1,0:T(8,128)(2,1)S(1)} %collective-permute-done.1.refs_2_.refs_1_), channel_id=1, source_target_pairs={{0,224},{32,0},{64,32},{96,64},{128,96},{160,128},{192,160},{224,1... | collective-permute-start | bytes 491528 | tf_op jit(solution)/shard_map/ppermute | solution.py:29
  42.6 0.8 copy-start.6
  43.4 10.4 %collective-permute-start.4 = (bf16[128,640]{1,0:T(8,128)(2,1)S(1)}, bf16[128,640]{1,0:T(8,128)(2,1)S(1)}, u32[]{:S(2)}, u32[]{:S(2)}) collective-permute-start(bf16[128,640]{1,0:T(8,128)(2,1)S(1)} %collective-permute-done.2.refs_2_.refs_7_), channel_id=1, source_target_pairs={{0,32},{32,64},{64,96},{96,128},{128,160},{160,192},{192,224},{224... | collective-permute-start | bytes 491528 | tf_op jit(solution)/shard_map/ppermute | solution.py:29
  43.4 10.4 %collective-permute-start.7 = (bf16[128,640]{1,0:T(8,128)(2,1)S(1)}, bf16[128,640]{1,0:T(8,128)(2,1)S(1)}, u32[]{:S(2)}, u32[]{:S(2)}) collective-permute-start(bf16[128,640]{1,0:T(8,128)(2,1)S(1)} %collective-permute-done.3.refs_1_.refs_2_), channel_id=1, source_target_pairs={{0,224},{32,0},{64,32},{96,64},{128,96},{160,128},{192,160},{224,1... | collective-permute-start | bytes 491528 | tf_op jit(solution)/shard_map/ppermute | solution.py:29
  46.7 5.7 %collective-permute-start.6 = (bf16[64,640]{1,0:T(8,128)(2,1)S(1)}, bf16[64,640]{1,0:T(8,128)(2,1)S(1)}, u32[]{:S(2)}, u32[]{:S(2)}) collective-permute-start(bf16[64,640]{1,0:T(8,128)(2,1)S(1)} %slice.7), channel_id=1, source_target_pairs={{0,192},{32,224},{64,0},{96,32},{128,64},{160,96},{192,128},{224,1... | collective-permute-start | bytes 245768 | tf_op jit(solution)/shard_map/ppermute | solution.py:29
  47.3 6.6 %collective-permute-start.5 = (bf16[64,640]{1,0:T(8,128)(2,1)S(1)}, bf16[64,640]{1,0:T(8,128)(2,1)S(1)}, u32[]{:S(2)}, u32[]{:S(2)}) collective-permute-start(bf16[64,640]{1,0:T(8,128)(2,1)S(1)} %slice.6), channel_id=1, source_target_pairs={{0,64},{32,96},{64,128},{96,160},{128,192},{160,224},{192,0},{224,... | collective-permute-start | bytes 245768 | tf_op jit(solution)/shard_map/ppermute | solution.py:29
  51.7 0.7 copy-start.4
  56.5 0.8 copy-start.8
  57.3 1.0 copy-start.9
  58.3 6.2 %copy-start.7 = (bf16[3,144,512]{2,1,0:T(8,128)(2,1)S(1)}, bf16[3,144,512]{2,1,0:T(8,128)(2,1)}, u32[]{:S(2)}) copy-start(bf16[3,144,512]{2,1,0:T(8,128)(2,1)} %copy-done.6) | copy-start | bytes 1327108
  63.0 9.2 %copy-start.5 = (bf16[2,144,512]{2,1,0:T(8,128)(2,1)S(1)}, bf16[2,144,512]{2,1,0:T(8,128)(2,1)}, u32[]{:S(2)}) copy-start(bf16[2,144,512]{2,1,0:T(8,128)(2,1)} %copy-done.4) | copy-start | bytes 884740
  63.0 9.2 %collective-permute-start.8 = (bf16[144,512]{1,0:T(8,128)(2,1)S(1)}, bf16[144,512]{1,0:T(8,128)(2,1)S(1)}, u32[]{:S(2)}, u32[]{:S(2)}) collective-permute-start(bf16[144,512]{1,0:T(8,128)(2,1)S(1)} %get-tuple-element.84), channel_id=1, source_target_pairs={{0,64},{32,96},{64,128},{96,160},{128,192},{160,224},{192,0},{224,... | collective-permute-start | bytes 442376 | tf_op jit(solution)/shard_map/ppermute | solution.py:29
  69.2 12.3 %collective-permute-start.12 = (bf16[144,512]{1,0:T(8,128)(2,1)S(1)}, bf16[144,512]{1,0:T(8,128)(2,1)S(1)}, u32[]{:S(2)}, u32[]{:S(2)}) collective-permute-start(bf16[144,512]{1,0:T(8,128)(2,1)S(1)} %get-tuple-element.88), channel_id=1, source_target_pairs={{0,192},{32,224},{64,0},{96,32},{128,64},{160,96},{192,128},{224,1... | collective-permute-start | bytes 442376 | tf_op jit(solution)/shard_map/ppermute | solution.py:29
  72.2 9.3 %collective-permute-start.11 = (bf16[144,512]{1,0:T(8,128)(2,1)S(1)}, bf16[144,512]{1,0:T(8,128)(2,1)S(1)}, u32[]{:S(2)}, u32[]{:S(2)}) collective-permute-start(bf16[144,512]{1,0:T(8,128)(2,1)S(1)} %get-tuple-element.97), channel_id=1, source_target_pairs={{0,64},{32,96},{64,128},{96,160},{128,192},{160,224},{192,0},{224,... | collective-permute-start | bytes 442376 | tf_op jit(solution)/shard_map/ppermute | solution.py:29
  76.9 13.2 %collective-permute-start.9 = (bf16[144,512]{1,0:T(8,128)(2,1)S(1)}, bf16[144,512]{1,0:T(8,128)(2,1)S(1)}, u32[]{:S(2)}, u32[]{:S(2)}) collective-permute-start(bf16[144,512]{1,0:T(8,128)(2,1)S(1)} %get-tuple-element.91), channel_id=1, source_target_pairs={{0,64},{32,96},{64,128},{96,160},{128,192},{160,224},{192,0},{224,... | collective-permute-start | bytes 442376 | tf_op jit(solution)/shard_map/ppermute | solution.py:29
  80.3 9.8 %collective-permute-start.10 = (bf16[144,512]{1,0:T(8,128)(2,1)S(1)}, bf16[144,512]{1,0:T(8,128)(2,1)S(1)}, u32[]{:S(2)}, u32[]{:S(2)}) collective-permute-start(bf16[144,512]{1,0:T(8,128)(2,1)S(1)} %get-tuple-element.92), channel_id=1, source_target_pairs={{0,192},{32,224},{64,0},{96,32},{128,64},{160,96},{192,128},{224,1... | collective-permute-start | bytes 442376 | tf_op jit(solution)/shard_map/ppermute | solution.py:29
  86.1 6.6 %collective-permute-start.13 = (bf16[144,512]{1,0:T(8,128)(2,1)S(1)}, bf16[144,512]{1,0:T(8,128)(2,1)S(1)}, u32[]{:S(2)}, u32[]{:S(2)}) collective-permute-start(bf16[144,512]{1,0:T(8,128)(2,1)S(1)} %get-tuple-element.98), channel_id=1, source_target_pairs={{0,32},{32,64},{64,96},{96,128},{128,160},{160,192},{192,224},{224... | collective-permute-start | bytes 442376 | tf_op jit(solution)/shard_map/ppermute | solution.py:29
  90.1 5.1 %collective-permute-start.14 = (bf16[144,512]{1,0:T(8,128)(2,1)S(1)}, bf16[144,512]{1,0:T(8,128)(2,1)S(1)}, u32[]{:S(2)}, u32[]{:S(2)}) collective-permute-start(bf16[144,512]{1,0:T(8,128)(2,1)S(1)} %get-tuple-element.99), channel_id=1, source_target_pairs={{0,224},{32,0},{64,32},{96,64},{128,96},{160,128},{192,160},{224,1... | collective-permute-start | bytes 442376 | tf_op jit(solution)/shard_map/ppermute | solution.py:29
  95.2 15.8 %copy-start = (bf16[2,4,128,512]{3,2,1,0:T(8,128)(2,1)S(1)}, bf16[2,4,128,512]{3,2,1,0:T(8,128)(2,1)}, u32[]{:S(2)}) copy-start(bf16[2,4,128,512]{3,2,1,0:T(8,128)(2,1)} %k_ref.1) | copy-start | bytes 3145732
  95.2 15.8 %copy-start.1 = (bf16[2,4,128,512]{3,2,1,0:T(8,128)(2,1)S(1)}, bf16[2,4,128,512]{3,2,1,0:T(8,128)(2,1)}, u32[]{:S(2)}) copy-start(bf16[2,4,128,512]{3,2,1,0:T(8,128)(2,1)} %v_ref.1) | copy-start | bytes 3145732

commit v5 on v4

--- a/solution.py
+++ b/solution.py
@@ -481,8 +481,8 @@
     n435, second = tie((n435, second))
     far = prepare(place, lengths, span_slots, 1, second, cycle, new, near[0])
 
-    up4, up3 = run(far, (4, 3), (((n435, 0),), ((n435, 1),)), joined=False)
-    down3, own = run(far, (5, 0), (((n435, 2),), ((n017, 0),)), (up4,), False)
+    (up4,) = run(far, (4,), (((n435, 0),),), joined=False)
+    up3, down3 = run(far, (3, 5), (((n435, 1),), ((n435, 2),)), (up4,), False)
     up4, up3 = shift(up4, 2), shift(up3, 2)
     up2, down2 = run(far, (2, 6), (((n26, 0), (up4,)), ((n26, 1),)), (down3,), False)
     down3 = shift(down3, -2)
@@ -494,6 +494,7 @@
     seen, up2, down2 = tie((seen, up2, down2))
     rows = windows(place, lengths, span_slots, seen, slots, span, cycle)
     up1, down1 = shift(up1, 1), shift(down1, -1)
+    (own,) = run(far, (0,), (((n017, 0),),), (rows,), False)
     rows = merge([own, up2, down2, up1, down1], rows)
     rows = lax.all_to_all(rows, "b", 0, 0, tiled=True)
     return finish(

time: 114 us -> 109 us (0.956)
  waiting for transfers between devices: 15.7 us -> 12.7 us
  starting transfers between devices: 42.7 us -> 40.5 us
  Pallas kernels: 36 us -> 37.3 us
    ppermute x15, waiting for transfers between devices: 12.2 us -> 9.17 us  [shift(): return lax.ppermute(a, 'z', [(i, (i + by) % size) for i in range(size)])]
    ppermute x15, starting transfers between devices: 28.4 us -> 26.2 us  [shift(): return lax.ppermute(a, 'z', [(i, (i + by) % size) for i in range(size)])]
    pallas_call x7 -> x8, Pallas kernels: 25.9 us -> 27.2 us  [attend(): pl.pallas_call(functools.partial(attend_kernel, parts, distances, cuts, p...]
  transfers between devices with their start and end apart: 18 -> 18, of which waited for: 6 -> 6; matrix products, arithmetic and copies ran while one was open for 0% -> 0% of each run, Pallas kernels for 23% -> 27%
where the time goes in v5:
time: 109 us; the launch traced here: 108 us
  starting transfers between devices  40.5 us (37%)
  Pallas kernels  37.3 us (34%)
  blocking collectives  14.5 us (13%)
  waiting for transfers between devices  12.7 us (12%)
  local copies, waits for them, and re-layouts  2.27 us (2%)
    pallas_call x8, Pallas kernels, attend(): pl.pallas_call(functools.partial(attend_kernel, parts, distances, cuts, p...  27.2 us
    ppermute x15, starting transfers between devices, shift(): return lax.ppermute(a, 'z', [(i, (i + by) % size) for i in range(size)])  26.2 us
    all_to_all x1, blocking collectives, on_device(): rows = lax.all_to_all(rows, 'b', 0, 0, tiled=True)  14.5 us
    ppermute x15, waiting for transfers between devices, shift(): return lax.ppermute(a, 'z', [(i, (i + by) % size) for i in range(size)])  9.17 us
    all_to_all x1, starting transfers between devices, on_device(): second = lax.all_to_all(second, 'b', 0, 0, tiled=True)  5.63 us
    all_to_all x1, starting transfers between devices, on_device(): turn_rows = lax.all_to_all(turn_rows, 'b', 0, 0, tiled=True)  5.12 us
    all_to_all x1, waiting for transfers between devices, on_device(): turn_rows = lax.all_to_all(turn_rows, 'b', 0, 0, tiled=True)  3.52 us
    all_to_all x1, starting transfers between devices, on_device(): first = lax.all_to_all(first, 'b', 0, 0, tiled=True)  3.49 us
  transfers between devices with their start and end apart: 18, of which 6 were waited for; matrix products, arithmetic and copies ran while one was open for 0% of the time, Pallas kernels for 27%

profile of v5, /device:TPU:4, one launch (start us, length us, event | category | flops | bytes accessed | tf_op | source)
XLA Modules:
  0.0 108.1 jit_solution(7694498198229240941)
XLA Ops:
  0.6 1.6 %pack_turn.1 = bf16[8,80,128]{2,1,0:T(8,128)(2,1)} custom-call(bf16[2,8,4096]{2,1,0:T(8,128)(2,1)} %refs_0_.1, bf16[2,8,512]{2,1,0:T(8,128)(2,1)} %refs_1_.1, bf16[2,8,512]{2,1,0:T(8,128)(2,1)} %refs_2_.1), custom_call_target="tpu_custom_call" | custom-call | tf_op jit(solution)/shard_map/pack_turn/pallas_call | solution.py:62
  2.3 5.1 %all-to-all-start = ((bf16[8,80,128]{2,1,0:T(8,128)(2,1)}), bf16[8,80,128]{2,1,0:T(8,128)(2,1)S(1)}, u32[]{:S(2)}, u32[]{:S(2)}) async-start(bf16[8,80,128]{2,1,0:T(8,128)(2,1)} %pack_turn.1), calls=%async_computation | async-start | bytes 327680 | tf_op jit(solution)/shard_map/all_to_all | solution.py:452
  7.4 3.3 %pack_cache.1 = (bf16[8,2,1,128,128]{4,3,2,1,0:T(8,128)(2,1)}, bf16[8,2,3,128,128]{4,3,2,1,0:T(8,128)(2,1)}) custom-call(bf16[2,4,128,512]{3,2,1,0:T(8,128)(2,1)} %k_ref.1, bf16[2,4,128,512]{3,2,1,0:T(8,128)(2,1)} %v_ref.1), custom_call_target="tpu_custom_call" | custom-call | tf_op jit(solution)/shard_map/pack_cache/pallas_call | solution.py:128
  10.7 3.5 %all-to-all-done.rows_ref = bf16[8,80,128]{2,1,0:T(8,128)(2,1)S(1)} async-done(((bf16[8,80,128]{2,1,0:T(8,128)(2,1)}), bf16[8,80,128]{2,1,0:T(8,128)(2,1)S(1)}, u32[]{:S(2)}, u32[]{:S(2)}) %all-to-all-start) | async-done | bytes 163872 | tf_op jit(solution)/shard_map/all_to_all | solution.py:452
  14.2 3.5 %all-to-all-start.1 = ((bf16[8,2,1,128,128]{4,3,2,1,0:T(8,128)(2,1)}), bf16[8,2,1,128,128]{4,3,2,1,0:T(8,128)(2,1)S(1)}, u32[]{:S(2)}, u32[]{:S(2)}) async-start(bf16[8,2,1,128,128]{4,3,2,1,0:T(8,128)(2,1)} %get-tuple-element.65), calls=%async_computation.1 | async-start | bytes 1048576 | tf_op jit(solution)/shard_map/all_to_all | solution.py:455
  17.7 0.1 ring_message.1
  17.8 0.0 copy-start.2
  17.8 0.0 copy-start.3
  17.8 5.9 %collective-permute-start.1 = (bf16[128,640]{1,0:T(8,128)(2,1)S(1)}, bf16[128,640]{1,0:T(8,128)(2,1)S(1)}, u32[]{:S(2)}, u32[]{:S(2)}) collective-permute-start(bf16[128,640]{1,0:T(8,128)(2,1)S(1)} %get-tuple-element.99.refs_1_.refs_0_), channel_id=1, source_target_pairs={{0,224},{32,0},{64,32},{96,64},{128,96},{160,128},{192,160},{224,1... | collective-permute-start | bytes 491528 | tf_op jit(solution)/shard_map/ppermute | solution.py:29
  23.8 0.0 collective-permute-start
  23.8 2.8 %collective-permute-done.1.refs_2_.refs_1_ = bf16[128,640]{1,0:T(8,128)(2,1)S(1)} collective-permute-done((bf16[128,640]{1,0:T(8,128)(2,1)S(1)}, bf16[128,640]{1,0:T(8,128)(2,1)S(1)}, u32[]{:S(2)}, u32[]{:S(2)}) %collective-permute-start.1) | collective-permute-done | bytes 163872 | tf_op jit(solution)/shard_map/ppermute | solution.py:29
  26.6 3.7 %collective-permute-done.refs_3_.refs_8_.refs_2_ = bf16[128,640]{1,0:T(8,128)(2,1)S(1)} collective-permute-done((bf16[128,640]{1,0:T(8,128)(2,1)S(1)}, bf16[128,640]{1,0:T(8,128)(2,1)S(1)}, u32[]{:S(2)}, u32[]{:S(2)}) %collective-permute-start) | collective-permute-done | bytes 163872 | tf_op jit(solution)/shard_map/ppermute | solution.py:29
  30.3 0.0 all-to-all-done.1.kv
  30.3 5.6 %all-to-all-start.2 = ((bf16[8,2,3,128,128]{4,3,2,1,0:T(8,128)(2,1)}), bf16[8,2,3,128,128]{4,3,2,1,0:T(8,128)(2,1)S(1)}, u32[]{:S(2)}, u32[]{:S(2)}) async-start(bf16[8,2,3,128,128]{4,3,2,1,0:T(8,128)(2,1)} %get-tuple-element.77), calls=%async_computation.2 | async-start | bytes 3145728 | tf_op jit(solution)/shard_map/all_to_all | solution.py:472
  35.9 0.2 collective-permute-start.3
  36.2 1.8 %collective-permute-start.2 = (bf16[128,640]{1,0:T(8,128)(2,1)S(1)}, bf16[128,640]{1,0:T(8,128)(2,1)S(1)}, u32[]{:S(2)}, u32[]{:S(2)}) collective-permute-start(bf16[128,640]{1,0:T(8,128)(2,1)S(1)} %collective-permute-done.refs_3_.refs_8_.refs_2_), channel_id=1, source_target_pairs={{0,32},{32,64},{64,96},{96,128},{128,160},{160,192},{192,224},{224... | collective-permute-start | bytes 491528 | tf_op jit(solution)/shard_map/ppermute | solution.py:29
  37.9 0.1 pad_add_fusion.place.refs_0_
  38.0 0.8 prepare.2
  38.8 2.6 %attend.8.refs_2_.refs_3_.refs_5_ = bf16[3,144,512]{2,1,0:T(8,128)(2,1)S(1)} custom-call(s32[2]{0:T(128)S(1)} %pad_add_fusion.place.refs_0_, bf16[128,640]{1,0:T(8,128)(2,1)S(1)} %get-tuple-element.99.refs_1_.refs_0_, bf16[128,640]{1,0:T(8,128)(2,1)S(1)} %collective-permute-done.1.refs_2_.refs_1_, ...), custom_call_target="tpu_custom_call" | custom-call | flops 1610612736 | bytes 3145728 | tf_op jit(solution)/shard_map/attend/pallas_call | solution.py:298
  41.4 0.0 copy-start.6
  41.5 0.8 copy-done.6
  42.2 0.0 collective-permute-done.3.refs_1_.refs_2_
  42.2 0.5 collective-permute-done.2.refs_2_.refs_7_
  42.7 1.0 collective-permute-start.4
  43.7 1.1 collective-permute-start.7
  44.7 0.4 collective-permute-start.5
  45.1 3.8 %collective-permute-start.6 = (bf16[64,640]{1,0:T(8,128)(2,1)S(1)}, bf16[64,640]{1,0:T(8,128)(2,1)S(1)}, u32[]{:S(2)}, u32[]{:S(2)}) collective-permute-start(bf16[64,640]{1,0:T(8,128)(2,1)S(1)} %slice.7), channel_id=1, source_target_pairs={{0,192},{32,224},{64,0},{96,32},{128,64},{160,96},{192,128},{224,1... | collective-permute-start | bytes 245768 | tf_op jit(solution)/shard_map/ppermute | solution.py:29
  49.0 2.0 %attend.9.refs_3_.refs_5_ = bf16[2,144,512]{2,1,0:T(8,128)(2,1)S(1)} custom-call(s32[2]{0:T(128)S(1)} %pad_add_fusion.place.refs_0_, bf16[128,640]{1,0:T(8,128)(2,1)S(1)} %collective-permute-done.3.refs_1_.refs_2_, bf16[128,640]{1,0:T(8,128)(2,1)S(1)} %collective-permute-done.2.refs_2_.refs_7_, ...), custom_call_target="tpu_custom_call" | custom-call | flops 1073741824 | bytes 3145728 | tf_op jit(solution)/shard_map/attend/pallas_call | solution.py:298
  51.0 0.7 copy-done.4
  51.7 0.6 collective-permute-done.5.refs_1_.refs_4_
  52.2 0.0 collective-permute-done.6.refs_2_.refs_5_
  52.2 0.0 collective-permute-done.4.refs_3_.refs_1_
  52.3 0.0 collective-permute-done.7.refs_4_.refs_2_.refs_6_
  52.3 2.6 %attend.10.refs_3_.refs_4_ = bf16[3,144,512]{2,1,0:T(8,128)(2,1)S(1)} custom-call(s32[2]{0:T(128)S(1)} %pad_add_fusion.place.refs_0_, bf16[64,640]{1,0:T(8,128)(2,1)S(1)} %collective-permute-done.5.refs_1_.refs_4_, bf16[64,640]{1,0:T(8,128)(2,1)S(1)} %collective-permute-done.6.refs_2_.refs_5_, bf16[128,640]{1,0:T(8,128)(2,1)S(1)} %collective-permute-done.4.refs_3_.refs_1_, ...), custom_call_target="tpu_custom_call" | custom-call | flops 1610612736 | bytes 3145728 | tf_op jit(solution)/shard_map/attend/pallas_call | solution.py:298
  54.9 0.0 copy-start.8
  54.9 0.8 copy-done.8
  55.7 0.0 all-to-all-done.2.kv
  55.7 1.0 prepare.3
  56.7 3.0 %attend.11 = bf16[144,512]{1,0:T(8,128)(2,1)S(1)} custom-call(s32[2]{0:T(128)S(1)} %pad_add_fusion.place.refs_0_, bf16[64,640]{1,0:T(8,128)(2,1)S(1)} %collective-permute-done.5.refs_1_.refs_4_, bf16[64,640]{1,0:T(8,128)(2,1)S(1)} %collective-permute-done.6.refs_2_.refs_5_, bf16[3,144,512]{2,1,0:T(8,128)(2,1)S(1)} %copy-done.9, ...), custom_call_target="tpu_custom_call" | custom-call | flops 1644167168 | bytes 3145728 | tf_op jit(solution)/shard_map/attend/pallas_call | solution.py:298
  59.7 1.5 %collective-permute-start.8 = (bf16[144,512]{1,0:T(8,128)(2,1)S(1)}, bf16[144,512]{1,0:T(8,128)(2,1)S(1)}, u32[]{:S(2)}, u32[]{:S(2)}) collective-permute-start(bf16[144,512]{1,0:T(8,128)(2,1)S(1)} %attend.11), channel_id=1, source_target_pairs={{0,64},{32,96},{64,128},{96,160},{128,192},{160,224},{192,0},{224,... | collective-permute-start | bytes 442376 | tf_op jit(solution)/shard_map/ppermute | solution.py:29
  61.2 4.7 %attend.12 = (bf16[144,512]{1,0:T(8,128)(2,1)S(1)}, bf16[144,512]{1,0:T(8,128)(2,1)S(1)}) custom-call(s32[2]{0:T(128)S(1)} %pad_add_fusion.place.refs_0_, bf16[128,640]{1,0:T(8,128)(2,1)S(1)} %collective-permute-done.4.refs_3_.refs_1_, bf16[128,640]{1,0:T(8,128)(2,1)S(1)} %collective-permute-done.7.refs_4_.refs_2_.refs_6_, ...), custom_call_target="tpu_custom_call" | custom-call | flops 3288334336 | bytes 3145728 | tf_op jit(solution)/shard_map/attend/pallas_call | solution.py:298
  65.9 2.8 %collective-permute-start.12 = (bf16[144,512]{1,0:T(8,128)(2,1)S(1)}, bf16[144,512]{1,0:T(8,128)(2,1)S(1)}, u32[]{:S(2)}, u32[]{:S(2)}) collective-permute-start(bf16[144,512]{1,0:T(8,128)(2,1)S(1)} %get-tuple-element.85), channel_id=1, source_target_pairs={{0,192},{32,224},{64,0},{96,32},{128,64},{160,96},{192,128},{224,1... | collective-permute-start | bytes 442376 | tf_op jit(solution)/shard_map/ppermute | solution.py:29
  68.7 0.2 collective-permute-start.11
  68.9 1.6 %collective-permute-done.8.refs_4_ = bf16[144,512]{1,0:T(8,128)(2,1)S(1)} collective-permute-done((bf16[144,512]{1,0:T(8,128)(2,1)S(1)}, bf16[144,512]{1,0:T(8,128)(2,1)S(1)}, u32[]{:S(2)}, u32[]{:S(2)}) %collective-permute-start.8) | collective-permute-done | bytes 147488 | tf_op jit(solution)/shard_map/ppermute | solution.py:29
  70.5 0.0 copy-done.5
  70.5 4.7 %attend.13 = (bf16[144,512]{1,0:T(8,128)(2,1)S(1)}, bf16[144,512]{1,0:T(8,128)(2,1)S(1)}) custom-call(s32[2]{0:T(128)S(1)} %pad_add_fusion.place.refs_0_, bf16[128,640]{1,0:T(8,128)(2,1)S(1)} %collective-permute-done.3.refs_1_.refs_2_, bf16[128,640]{1,0:T(8,128)(2,1)S(1)} %collective-permute-done.2.refs_2_.refs_7_, bf16[2,144,512]{2,1,0:T(8,128)(2,1)S(1)} %copy-done.5, ...), custom_call_target="tpu_custom_call" | custom-call | flops 3288334336 | bytes 3145728 | tf_op jit(solution)/shard_map/attend/pallas_call | solution.py:298
  75.2 1.5 %collective-permute-start.9 = (bf16[144,512]{1,0:T(8,128)(2,1)S(1)}, bf16[144,512]{1,0:T(8,128)(2,1)S(1)}, u32[]{:S(2)}, u32[]{:S(2)}) collective-permute-start(bf16[144,512]{1,0:T(8,128)(2,1)S(1)} %get-tuple-element.88), channel_id=1, source_target_pairs={{0,64},{32,96},{64,128},{96,160},{128,192},{160,224},{192,0},{224,... | collective-permute-start | bytes 442376 | tf_op jit(solution)/shard_map/ppermute | solution.py:29
  76.7 2.7 %collective-permute-start.10 = (bf16[144,512]{1,0:T(8,128)(2,1)S(1)}, bf16[144,512]{1,0:T(8,128)(2,1)S(1)}, u32[]{:S(2)}, u32[]{:S(2)}) collective-permute-start(bf16[144,512]{1,0:T(8,128)(2,1)S(1)} %get-tuple-element.89), channel_id=1, source_target_pairs={{0,192},{32,224},{64,0},{96,32},{128,64},{160,96},{192,128},{224,1... | collective-permute-start | bytes 442376 | tf_op jit(solution)/shard_map/ppermute | solution.py:29
  79.4 0.0 collective-permute-done.11.refs_4_
  79.4 0.0 collective-permute-done.12.refs_6_
  79.4 4.6 %attend.15 = (bf16[144,512]{1,0:T(8,128)(2,1)S(1)}, bf16[144,512]{1,0:T(8,128)(2,1)S(1)}) custom-call(s32[2]{0:T(128)S(1)} %pad_add_fusion.place.refs_0_, bf16[128,640]{1,0:T(8,128)(2,1)S(1)} %collective-permute-done.1.refs_2_.refs_1_, bf16[128,640]{1,0:T(8,128)(2,1)S(1)} %collective-permute-done.refs_3_.refs_8_.refs_2_, bf16[3,144,512]{2,1,0:T(8,128)(2,1)S(1)} %copy-done.7, ...), custom_call_target="tpu_custom_call" | custom-call | flops 3288334336 | bytes 3145728 | tf_op jit(solution)/shard_map/attend/pallas_call | solution.py:298
  84.0 1.5 %collective-permute-start.13 = (bf16[144,512]{1,0:T(8,128)(2,1)S(1)}, bf16[144,512]{1,0:T(8,128)(2,1)S(1)}, u32[]{:S(2)}, u32[]{:S(2)}) collective-permute-start(bf16[144,512]{1,0:T(8,128)(2,1)S(1)} %get-tuple-element.105), channel_id=1, source_target_pairs={{0,32},{32,64},{64,96},{96,128},{128,160},{160,192},{192,224},{224... | collective-permute-start | bytes 442376 | tf_op jit(solution)/shard_map/ppermute | solution.py:29
  85.5 1.8 %collective-permute-start.14 = (bf16[144,512]{1,0:T(8,128)(2,1)S(1)}, bf16[144,512]{1,0:T(8,128)(2,1)S(1)}, u32[]{:S(2)}, u32[]{:S(2)}) collective-permute-start(bf16[144,512]{1,0:T(8,128)(2,1)S(1)} %get-tuple-element.106), channel_id=1, source_target_pairs={{0,224},{32,0},{64,32},{96,64},{128,96},{160,128},{192,160},{224,1... | collective-permute-start | bytes 442376 | tf_op jit(solution)/shard_map/ppermute | solution.py:29
  87.3 0.0 collective-permute-done.10.refs_2_
  87.3 0.0 collective-permute-done.9.refs_1_
  87.4 0.9 windows.1.refs_5_
  88.3 3.0 %attend.14.refs_0_ = bf16[144,512]{1,0:T(8,128)(2,1)S(1)} custom-call(s32[2]{0:T(128)S(1)} %pad_add_fusion.place.refs_0_, bf16[128,640]{1,0:T(8,128)(2,1)S(1)} %get-tuple-element.99.refs_1_.refs_0_, bf16[3,144,512]{2,1,0:T(8,128)(2,1)S(1)} %copy-done.7, bf16[3136,128]{1,0:T(8,128)(2,1)S(1)} %get-tuple-element.81.refs_4_.refs_5_.refs_6_.refs_3_.refs_7_, ...), custom_call_target="tpu_custom_call" | custom-call | flops 1644167168 | bytes 3145728 | tf_op jit(solution)/shard_map/attend/pallas_call | solution.py:298
  91.3 0.0 copy-start
  91.3 0.0 copy-start.1
  91.3 0.0 collective-permute-done.13.refs_3_
  91.3 0.0 collective-permute-done.14.refs_4_
  91.4 0.2 merge.1
  91.6 14.5 %all_to_all.20.new_ref = bf16[8,320,128]{2,1,0:T(8,128)(2,1)S(1)} all-to-all(bf16[8,320,128]{2,1,0:T(8,128)(2,1)S(1)} %merge.1), channel_id=1, replica_groups=mesh['z'=8,'b'=8,'head'=2,'conv'=2] {'b'}, dimensions={0} | all-to-all | bytes 1310720 | tf_op jit(solution)/shard_map/all_to_all | solution.py:499
  106.1 2.0 %finish.1 = (bf16[2,8,4096]{2,1,0:T(8,128)(2,1)}, bf16[2,4,128,512]{3,2,1,0:T(8,128)(2,1)}, bf16[2,4,128,512]{3,2,1,0:T(8,128)(2,1)}) custom-call(s32[2]{0:T(128)S(1)} %pad_add_fusion.place.refs_0_, s32[2]{0:T(128)S(1)} %copy-done.3, s32[2,256]{1,0:T(2,128)S(1)} %copy-done.2, bf16[8,320,128]{2,1,0:T(8,128)(2,1)S(1)} %all_to_all.20.new_ref, ...), custom_call_target="tpu_custom_call" | custom-call | bytes 5242880 | tf_op jit(solution)/shard_map/finish/pallas_call | solution.py:432
  (12 shorter events, 0.0 us)
Async XLA Ops:
  2.3 11.9 %all-to-all-start = ((bf16[8,80,128]{2,1,0:T(8,128)(2,1)}), bf16[8,80,128]{2,1,0:T(8,128)(2,1)S(1)}, u32[]{:S(2)}, u32[]{:S(2)}) async-start(bf16[8,80,128]{2,1,0:T(8,128)(2,1)} %pack_turn.1), calls=%async_computation | async-start | bytes 327680 | tf_op jit(solution)/shard_map/all_to_all | solution.py:452
  14.2 16.1 %all-to-all-start.1 = ((bf16[8,2,1,128,128]{4,3,2,1,0:T(8,128)(2,1)}), bf16[8,2,1,128,128]{4,3,2,1,0:T(8,128)(2,1)S(1)}, u32[]{:S(2)}, u32[]{:S(2)}) async-start(bf16[8,2,1,128,128]{4,3,2,1,0:T(8,128)(2,1)} %get-tuple-element.65), calls=%async_computation.1 | async-start | bytes 1048576 | tf_op jit(solution)/shard_map/all_to_all | solution.py:455
  17.8 20.2 %copy-start.2 = (s32[2,256]{1,0:T(2,128)S(1)}, s32[2,256]{1,0:T(2,128)}, u32[]{:S(2)}) copy-start(s32[2,256]{1,0:T(2,128)} %slots_ref.7) | copy-start | bytes 6148
  17.8 20.2 %copy-start.3 = (s32[2]{0:T(128)S(1)}, s32[2]{0:T(128)}, u32[]{:S(2)}) copy-start(s32[2]{0:T(128)} %lengths.7) | copy-start | bytes 28
  17.8 8.8 %collective-permute-start.1 = (bf16[128,640]{1,0:T(8,128)(2,1)S(1)}, bf16[128,640]{1,0:T(8,128)(2,1)S(1)}, u32[]{:S(2)}, u32[]{:S(2)}) collective-permute-start(bf16[128,640]{1,0:T(8,128)(2,1)S(1)} %get-tuple-element.99.refs_1_.refs_0_), channel_id=1, source_target_pairs={{0,224},{32,0},{64,32},{96,64},{128,96},{160,128},{192,160},{224,1... | collective-permute-start | bytes 491528 | tf_op jit(solution)/shard_map/ppermute | solution.py:29
  23.8 6.5 %collective-permute-start = (bf16[128,640]{1,0:T(8,128)(2,1)S(1)}, bf16[128,640]{1,0:T(8,128)(2,1)S(1)}, u32[]{:S(2)}, u32[]{:S(2)}) collective-permute-start(bf16[128,640]{1,0:T(8,128)(2,1)S(1)} %get-tuple-element.99.refs_1_.refs_0_), channel_id=1, source_target_pairs={{0,32},{32,64},{64,96},{96,128},{128,160},{160,192},{192,224},{224... | collective-permute-start | bytes 491528 | tf_op jit(solution)/shard_map/ppermute | solution.py:29
  30.3 25.4 %all-to-all-start.2 = ((bf16[8,2,3,128,128]{4,3,2,1,0:T(8,128)(2,1)}), bf16[8,2,3,128,128]{4,3,2,1,0:T(8,128)(2,1)S(1)}, u32[]{:S(2)}, u32[]{:S(2)}) async-start(bf16[8,2,3,128,128]{4,3,2,1,0:T(8,128)(2,1)} %get-tuple-element.77), calls=%async_computation.2 | async-start | bytes 3145728 | tf_op jit(solution)/shard_map/all_to_all | solution.py:472
  35.9 6.3 %collective-permute-start.3 = (bf16[128,640]{1,0:T(8,128)(2,1)S(1)}, bf16[128,640]{1,0:T(8,128)(2,1)S(1)}, u32[]{:S(2)}, u32[]{:S(2)}) collective-permute-start(bf16[128,640]{1,0:T(8,128)(2,1)S(1)} %collective-permute-done.1.refs_2_.refs_1_), channel_id=1, source_target_pairs={{0,224},{32,0},{64,32},{96,64},{128,96},{160,128},{192,160},{224,1... | collective-permute-start | bytes 491528 | tf_op jit(solution)/shard_map/ppermute | solution.py:29
  36.2 6.5 %collective-permute-start.2 = (bf16[128,640]{1,0:T(8,128)(2,1)S(1)}, bf16[128,640]{1,0:T(8,128)(2,1)S(1)}, u32[]{:S(2)}, u32[]{:S(2)}) collective-permute-start(bf16[128,640]{1,0:T(8,128)(2,1)S(1)} %collective-permute-done.refs_3_.refs_8_.refs_2_), channel_id=1, source_target_pairs={{0,32},{32,64},{64,96},{96,128},{128,160},{160,192},{192,224},{224... | collective-permute-start | bytes 491528 | tf_op jit(solution)/shard_map/ppermute | solution.py:29
  41.4 0.8 copy-start.6
  42.7 9.6 %collective-permute-start.4 = (bf16[128,640]{1,0:T(8,128)(2,1)S(1)}, bf16[128,640]{1,0:T(8,128)(2,1)S(1)}, u32[]{:S(2)}, u32[]{:S(2)}) collective-permute-start(bf16[128,640]{1,0:T(8,128)(2,1)S(1)} %collective-permute-done.3.refs_1_.refs_2_), channel_id=1, source_target_pairs={{0,224},{32,0},{64,32},{96,64},{128,96},{160,128},{192,160},{224,1... | collective-permute-start | bytes 491528 | tf_op jit(solution)/shard_map/ppermute | solution.py:29
  43.7 8.6 %collective-permute-start.7 = (bf16[128,640]{1,0:T(8,128)(2,1)S(1)}, bf16[128,640]{1,0:T(8,128)(2,1)S(1)}, u32[]{:S(2)}, u32[]{:S(2)}) collective-permute-start(bf16[128,640]{1,0:T(8,128)(2,1)S(1)} %collective-permute-done.2.refs_2_.refs_7_), channel_id=1, source_target_pairs={{0,32},{32,64},{64,96},{96,128},{128,160},{160,192},{192,224},{224... | collective-permute-start | bytes 491528 | tf_op jit(solution)/shard_map/ppermute | solution.py:29
  44.7 7.5 %collective-permute-start.5 = (bf16[64,640]{1,0:T(8,128)(2,1)S(1)}, bf16[64,640]{1,0:T(8,128)(2,1)S(1)}, u32[]{:S(2)}, u32[]{:S(2)}) collective-permute-start(bf16[64,640]{1,0:T(8,128)(2,1)S(1)} %slice.6), channel_id=1, source_target_pairs={{0,64},{32,96},{64,128},{96,160},{128,192},{160,224},{192,0},{224,... | collective-permute-start | bytes 245768 | tf_op jit(solution)/shard_map/ppermute | solution.py:29
  45.1 7.1 %collective-permute-start.6 = (bf16[64,640]{1,0:T(8,128)(2,1)S(1)}, bf16[64,640]{1,0:T(8,128)(2,1)S(1)}, u32[]{:S(2)}, u32[]{:S(2)}) collective-permute-start(bf16[64,640]{1,0:T(8,128)(2,1)S(1)} %slice.7), channel_id=1, source_target_pairs={{0,192},{32,224},{64,0},{96,32},{128,64},{160,96},{192,128},{224,1... | collective-permute-start | bytes 245768 | tf_op jit(solution)/shard_map/ppermute | solution.py:29
  50.9 0.7 copy-start.4
  54.9 0.8 copy-start.8
  55.7 1.0 copy-start.9
  59.7 10.8 %copy-start.5 = (bf16[2,144,512]{2,1,0:T(8,128)(2,1)S(1)}, bf16[2,144,512]{2,1,0:T(8,128)(2,1)}, u32[]{:S(2)}) copy-start(bf16[2,144,512]{2,1,0:T(8,128)(2,1)} %copy-done.4) | copy-start | bytes 884740
  59.7 10.7 %collective-permute-start.8 = (bf16[144,512]{1,0:T(8,128)(2,1)S(1)}, bf16[144,512]{1,0:T(8,128)(2,1)S(1)}, u32[]{:S(2)}, u32[]{:S(2)}) collective-permute-start(bf16[144,512]{1,0:T(8,128)(2,1)S(1)} %attend.11), channel_id=1, source_target_pairs={{0,64},{32,96},{64,128},{96,160},{128,192},{160,224},{192,0},{224,... | collective-permute-start | bytes 442376 | tf_op jit(solution)/shard_map/ppermute | solution.py:29
  65.9 13.5 %collective-permute-start.12 = (bf16[144,512]{1,0:T(8,128)(2,1)S(1)}, bf16[144,512]{1,0:T(8,128)(2,1)S(1)}, u32[]{:S(2)}, u32[]{:S(2)}) collective-permute-start(bf16[144,512]{1,0:T(8,128)(2,1)S(1)} %get-tuple-element.85), channel_id=1, source_target_pairs={{0,192},{32,224},{64,0},{96,32},{128,64},{160,96},{192,128},{224,1... | collective-permute-start | bytes 442376 | tf_op jit(solution)/shard_map/ppermute | solution.py:29
  68.7 10.7 %copy-start.7 = (bf16[3,144,512]{2,1,0:T(8,128)(2,1)S(1)}, bf16[3,144,512]{2,1,0:T(8,128)(2,1)}, u32[]{:S(2)}) copy-start(bf16[3,144,512]{2,1,0:T(8,128)(2,1)} %copy-done.6) | copy-start | bytes 1327108
  68.7 10.7 %collective-permute-start.11 = (bf16[144,512]{1,0:T(8,128)(2,1)S(1)}, bf16[144,512]{1,0:T(8,128)(2,1)S(1)}, u32[]{:S(2)}, u32[]{:S(2)}) collective-permute-start(bf16[144,512]{1,0:T(8,128)(2,1)S(1)} %get-tuple-element.104), channel_id=1, source_target_pairs={{0,64},{32,96},{64,128},{96,160},{128,192},{160,224},{192,0},{224,... | collective-permute-start | bytes 442376 | tf_op jit(solution)/shard_map/ppermute | solution.py:29
  75.2 12.2 %collective-permute-start.9 = (bf16[144,512]{1,0:T(8,128)(2,1)S(1)}, bf16[144,512]{1,0:T(8,128)(2,1)S(1)}, u32[]{:S(2)}, u32[]{:S(2)}) collective-permute-start(bf16[144,512]{1,0:T(8,128)(2,1)S(1)} %get-tuple-element.88), channel_id=1, source_target_pairs={{0,64},{32,96},{64,128},{96,160},{128,192},{160,224},{192,0},{224,... | collective-permute-start | bytes 442376 | tf_op jit(solution)/shard_map/ppermute | solution.py:29
  76.7 10.7 %collective-permute-start.10 = (bf16[144,512]{1,0:T(8,128)(2,1)S(1)}, bf16[144,512]{1,0:T(8,128)(2,1)S(1)}, u32[]{:S(2)}, u32[]{:S(2)}) collective-permute-start(bf16[144,512]{1,0:T(8,128)(2,1)S(1)} %get-tuple-element.89), channel_id=1, source_target_pairs={{0,192},{32,224},{64,0},{96,32},{128,64},{160,96},{192,128},{224,1... | collective-permute-start | bytes 442376 | tf_op jit(solution)/shard_map/ppermute | solution.py:29
  84.0 7.3 %collective-permute-start.13 = (bf16[144,512]{1,0:T(8,128)(2,1)S(1)}, bf16[144,512]{1,0:T(8,128)(2,1)S(1)}, u32[]{:S(2)}, u32[]{:S(2)}) collective-permute-start(bf16[144,512]{1,0:T(8,128)(2,1)S(1)} %get-tuple-element.105), channel_id=1, source_target_pairs={{0,32},{32,64},{64,96},{96,128},{128,160},{160,192},{192,224},{224... | collective-permute-start | bytes 442376 | tf_op jit(solution)/shard_map/ppermute | solution.py:29
  85.5 5.8 %collective-permute-start.14 = (bf16[144,512]{1,0:T(8,128)(2,1)S(1)}, bf16[144,512]{1,0:T(8,128)(2,1)S(1)}, u32[]{:S(2)}, u32[]{:S(2)}) collective-permute-start(bf16[144,512]{1,0:T(8,128)(2,1)S(1)} %get-tuple-element.106), channel_id=1, source_target_pairs={{0,224},{32,0},{64,32},{96,64},{128,96},{160,128},{192,160},{224,1... | collective-permute-start | bytes 442376 | tf_op jit(solution)/shard_map/ppermute | solution.py:29
  91.3 14.8 %copy-start = (bf16[2,4,128,512]{3,2,1,0:T(8,128)(2,1)S(1)}, bf16[2,4,128,512]{3,2,1,0:T(8,128)(2,1)}, u32[]{:S(2)}) copy-start(bf16[2,4,128,512]{3,2,1,0:T(8,128)(2,1)} %k_ref.1) | copy-start | bytes 3145732
  91.3 14.8 %copy-start.1 = (bf16[2,4,128,512]{3,2,1,0:T(8,128)(2,1)S(1)}, bf16[2,4,128,512]{3,2,1,0:T(8,128)(2,1)}, u32[]{:S(2)}) copy-start(bf16[2,4,128,512]{3,2,1,0:T(8,128)(2,1)} %v_ref.1) | copy-start | bytes 3145732

commit v6 on v5

--- a/solution.py
+++ b/solution.py
@@ -248,7 +248,8 @@
             totals.append(jnp.zeros((HEAD + EXTRA, width), F32))
     top = jnp.concatenate(tops, axis=1)
     total = jnp.concatenate(totals, axis=1)
-    tiles = [slice(j, j + TILE) for j in range(0, cached, TILE)]
+    tile = TILE * 2 if count == 1 else TILE
+    tiles = [slice(j, j + tile) for j in range(0, cached, tile)]
     if with_new:
         tiles.append(slice(cached, cached + turn_part))
 
@@ -268,9 +269,12 @@
     scores = scores_of(tiles[0])
     for n, at in enumerate(tiles):
         following = scores_of(tiles[n + 1]) if n + 1 < len(tiles) else None
-        higher = jnp.maximum(top, jnp.max(scores, axis=0, keepdims=True))
+        higher = jnp.max(scores, axis=0, keepdims=True)
+        if n > 0 or init_refs:
+            higher = jnp.maximum(top, higher)
         weights = jnp.exp2(scores - higher).astype(BF16)
-        total = total * jnp.exp2(top - higher) + dot(sums[:, at], weights)
+        share = dot(sums[:, at], weights)
+        total = total * jnp.exp2(top - higher) + share if n > 0 or init_refs else share
         top, scores = higher, following
     denominator = total[HEAD : HEAD + 1]
     out = (total[:HEAD] * (1.0 / denominator)).astype(BF16)

time: 109 us -> 109 us (level)
  no operation moved by 1% of the time
where the time goes in v6:
time: 109 us; the launch traced here: 108 us
  starting transfers between devices  40.5 us (37%)
  Pallas kernels  37.2 us (34%)
  blocking collectives  14.5 us (13%)
  waiting for transfers between devices  12.7 us (12%)
  local copies, waits for them, and re-layouts  2.27 us (2%)
    pallas_call x8, Pallas kernels, attend(): pl.pallas_call(functools.partial(attend_kernel, parts, distances, cuts, p...  27.1 us
    ppermute x15, starting transfers between devices, shift(): return lax.ppermute(a, 'z', [(i, (i + by) % size) for i in range(size)])  26.2 us
    all_to_all x1, blocking collectives, on_device(): rows = lax.all_to_all(rows, 'b', 0, 0, tiled=True)  14.5 us
    ppermute x15, waiting for transfers between devices, shift(): return lax.ppermute(a, 'z', [(i, (i + by) % size) for i in range(size)])  9.22 us
    all_to_all x1, starting transfers between devices, on_device(): second = lax.all_to_all(second, 'b', 0, 0, tiled=True)  5.63 us
    all_to_all x1, starting transfers between devices, on_device(): turn_rows = lax.all_to_all(turn_rows, 'b', 0, 0, tiled=True)  5.12 us
    all_to_all x1, waiting for transfers between devices, on_device(): turn_rows = lax.all_to_all(turn_rows, 'b', 0, 0, tiled=True)  3.52 us
    all_to_all x1, starting transfers between devices, on_device(): first = lax.all_to_all(first, 'b', 0, 0, tiled=True)  3.49 us
  transfers between devices with their start and end apart: 18, of which 6 were waited for; matrix products, arithmetic and copies ran while one was open for 0% of the time, Pallas kernels for 27%

profile of v6, /device:TPU:4, one launch (start us, length us, event | category | flops | bytes accessed | tf_op | source)
XLA Modules:
  0.0 108.1 jit_solution(9755734832348416125)
XLA Ops:
  0.6 1.6 %pack_turn.1 = bf16[8,80,128]{2,1,0:T(8,128)(2,1)} custom-call(bf16[2,8,4096]{2,1,0:T(8,128)(2,1)} %refs_0_.1, bf16[2,8,512]{2,1,0:T(8,128)(2,1)} %refs_1_.1, bf16[2,8,512]{2,1,0:T(8,128)(2,1)} %refs_2_.1), custom_call_target="tpu_custom_call" | custom-call | tf_op jit(solution)/shard_map/pack_turn/pallas_call | solution.py:62
  2.3 5.1 %all-to-all-start = ((bf16[8,80,128]{2,1,0:T(8,128)(2,1)}), bf16[8,80,128]{2,1,0:T(8,128)(2,1)S(1)}, u32[]{:S(2)}, u32[]{:S(2)}) async-start(bf16[8,80,128]{2,1,0:T(8,128)(2,1)} %pack_turn.1), calls=%async_computation | async-start | bytes 327680 | tf_op jit(solution)/shard_map/all_to_all | solution.py:456
  7.4 3.3 %pack_cache.1 = (bf16[8,2,1,128,128]{4,3,2,1,0:T(8,128)(2,1)}, bf16[8,2,3,128,128]{4,3,2,1,0:T(8,128)(2,1)}) custom-call(bf16[2,4,128,512]{3,2,1,0:T(8,128)(2,1)} %k_ref.1, bf16[2,4,128,512]{3,2,1,0:T(8,128)(2,1)} %v_ref.1), custom_call_target="tpu_custom_call" | custom-call | tf_op jit(solution)/shard_map/pack_cache/pallas_call | solution.py:128
  10.7 3.5 %all-to-all-done.rows_ref = bf16[8,80,128]{2,1,0:T(8,128)(2,1)S(1)} async-done(((bf16[8,80,128]{2,1,0:T(8,128)(2,1)}), bf16[8,80,128]{2,1,0:T(8,128)(2,1)S(1)}, u32[]{:S(2)}, u32[]{:S(2)}) %all-to-all-start) | async-done | bytes 163872 | tf_op jit(solution)/shard_map/all_to_all | solution.py:456
  14.2 3.5 %all-to-all-start.1 = ((bf16[8,2,1,128,128]{4,3,2,1,0:T(8,128)(2,1)}), bf16[8,2,1,128,128]{4,3,2,1,0:T(8,128)(2,1)S(1)}, u32[]{:S(2)}, u32[]{:S(2)}) async-start(bf16[8,2,1,128,128]{4,3,2,1,0:T(8,128)(2,1)} %get-tuple-element.65), calls=%async_computation.1 | async-start | bytes 1048576 | tf_op jit(solution)/shard_map/all_to_all | solution.py:459
  17.7 0.1 ring_message.1
  17.8 0.0 copy-start.2
  17.8 0.0 copy-start.3
  17.8 5.9 %collective-permute-start.1 = (bf16[128,640]{1,0:T(8,128)(2,1)S(1)}, bf16[128,640]{1,0:T(8,128)(2,1)S(1)}, u32[]{:S(2)}, u32[]{:S(2)}) collective-permute-start(bf16[128,640]{1,0:T(8,128)(2,1)S(1)} %get-tuple-element.99.refs_1_.refs_0_), channel_id=1, source_target_pairs={{0,224},{32,0},{64,32},{96,64},{128,96},{160,128},{192,160},{224,1... | collective-permute-start | bytes 491528 | tf_op jit(solution)/shard_map/ppermute | solution.py:29
  23.8 0.0 collective-permute-start
  23.8 2.8 %collective-permute-done.1.refs_2_.refs_1_ = bf16[128,640]{1,0:T(8,128)(2,1)S(1)} collective-permute-done((bf16[128,640]{1,0:T(8,128)(2,1)S(1)}, bf16[128,640]{1,0:T(8,128)(2,1)S(1)}, u32[]{:S(2)}, u32[]{:S(2)}) %collective-permute-start.1) | collective-permute-done | bytes 163872 | tf_op jit(solution)/shard_map/ppermute | solution.py:29
  26.6 3.7 %collective-permute-done.refs_3_.refs_8_.refs_2_ = bf16[128,640]{1,0:T(8,128)(2,1)S(1)} collective-permute-done((bf16[128,640]{1,0:T(8,128)(2,1)S(1)}, bf16[128,640]{1,0:T(8,128)(2,1)S(1)}, u32[]{:S(2)}, u32[]{:S(2)}) %collective-permute-start) | collective-permute-done | bytes 163872 | tf_op jit(solution)/shard_map/ppermute | solution.py:29
  30.3 0.0 all-to-all-done.1.kv
  30.3 5.6 %all-to-all-start.2 = ((bf16[8,2,3,128,128]{4,3,2,1,0:T(8,128)(2,1)}), bf16[8,2,3,128,128]{4,3,2,1,0:T(8,128)(2,1)S(1)}, u32[]{:S(2)}, u32[]{:S(2)}) async-start(bf16[8,2,3,128,128]{4,3,2,1,0:T(8,128)(2,1)} %get-tuple-element.77), calls=%async_computation.2 | async-start | bytes 3145728 | tf_op jit(solution)/shard_map/all_to_all | solution.py:476
  35.9 0.2 collective-permute-start.3
  36.2 1.8 %collective-permute-start.2 = (bf16[128,640]{1,0:T(8,128)(2,1)S(1)}, bf16[128,640]{1,0:T(8,128)(2,1)S(1)}, u32[]{:S(2)}, u32[]{:S(2)}) collective-permute-start(bf16[128,640]{1,0:T(8,128)(2,1)S(1)} %collective-permute-done.refs_3_.refs_8_.refs_2_), channel_id=1, source_target_pairs={{0,32},{32,64},{64,96},{96,128},{128,160},{160,192},{192,224},{224... | collective-permute-start | bytes 491528 | tf_op jit(solution)/shard_map/ppermute | solution.py:29
  37.9 0.1 pad_add_fusion.place.refs_0_
  38.0 0.8 prepare.2
  38.8 2.6 %attend.8.refs_2_.refs_3_.refs_5_ = bf16[3,144,512]{2,1,0:T(8,128)(2,1)S(1)} custom-call(s32[2]{0:T(128)S(1)} %pad_add_fusion.place.refs_0_, bf16[128,640]{1,0:T(8,128)(2,1)S(1)} %get-tuple-element.99.refs_1_.refs_0_, bf16[128,640]{1,0:T(8,128)(2,1)S(1)} %collective-permute-done.1.refs_2_.refs_1_, ...), custom_call_target="tpu_custom_call" | custom-call | flops 1610612736 | bytes 3145728 | tf_op jit(solution)/shard_map/attend/pallas_call | solution.py:302
  41.4 0.0 copy-start.6
  41.4 0.8 copy-done.6
  42.2 0.0 collective-permute-done.3.refs_1_.refs_2_
  42.2 0.5 collective-permute-done.2.refs_2_.refs_7_
  42.7 0.9 collective-permute-start.4
  43.6 1.1 %collective-permute-start.7 = (bf16[128,640]{1,0:T(8,128)(2,1)S(1)}, bf16[128,640]{1,0:T(8,128)(2,1)S(1)}, u32[]{:S(2)}, u32[]{:S(2)}) collective-permute-start(bf16[128,640]{1,0:T(8,128)(2,1)S(1)} %collective-permute-done.2.refs_2_.refs_7_), channel_id=1, source_target_pairs={{0,32},{32,64},{64,96},{96,128},{128,160},{160,192},{192,224},{224... | collective-permute-start | bytes 491528 | tf_op jit(solution)/shard_map/ppermute | solution.py:29
  44.7 0.4 collective-permute-start.5
  45.2 3.8 %collective-permute-start.6 = (bf16[64,640]{1,0:T(8,128)(2,1)S(1)}, bf16[64,640]{1,0:T(8,128)(2,1)S(1)}, u32[]{:S(2)}, u32[]{:S(2)}) collective-permute-start(bf16[64,640]{1,0:T(8,128)(2,1)S(1)} %slice.7), channel_id=1, source_target_pairs={{0,192},{32,224},{64,0},{96,32},{128,64},{160,96},{192,128},{224,1... | collective-permute-start | bytes 245768 | tf_op jit(solution)/shard_map/ppermute | solution.py:29
  49.0 1.9 %attend.9.refs_3_.refs_5_ = bf16[2,144,512]{2,1,0:T(8,128)(2,1)S(1)} custom-call(s32[2]{0:T(128)S(1)} %pad_add_fusion.place.refs_0_, bf16[128,640]{1,0:T(8,128)(2,1)S(1)} %collective-permute-done.3.refs_1_.refs_2_, bf16[128,640]{1,0:T(8,128)(2,1)S(1)} %collective-permute-done.2.refs_2_.refs_7_, ...), custom_call_target="tpu_custom_call" | custom-call | flops 1073741824 | bytes 3145728 | tf_op jit(solution)/shard_map/attend/pallas_call | solution.py:302
  50.9 0.7 copy-done.4
  51.6 0.6 collective-permute-done.5.refs_1_.refs_4_
  52.2 0.0 collective-permute-done.6.refs_2_.refs_5_
  52.2 0.0 collective-permute-done.4.refs_3_.refs_1_
  52.3 0.0 collective-permute-done.7.refs_4_.refs_2_.refs_6_
  52.3 2.6 %attend.10.refs_3_.refs_4_ = bf16[3,144,512]{2,1,0:T(8,128)(2,1)S(1)} custom-call(s32[2]{0:T(128)S(1)} %pad_add_fusion.place.refs_0_, bf16[64,640]{1,0:T(8,128)(2,1)S(1)} %collective-permute-done.5.refs_1_.refs_4_, bf16[64,640]{1,0:T(8,128)(2,1)S(1)} %collective-permute-done.6.refs_2_.refs_5_, bf16[128,640]{1,0:T(8,128)(2,1)S(1)} %collective-permute-done.4.refs_3_.refs_1_, ...), custom_call_target="tpu_custom_call" | custom-call | flops 1610612736 | bytes 3145728 | tf_op jit(solution)/shard_map/attend/pallas_call | solution.py:302
  54.9 0.0 copy-start.8
  54.9 0.8 copy-done.8
  55.6 0.0 all-to-all-done.2.kv
  55.6 1.0 prepare.3
  56.7 3.0 %attend.11 = bf16[144,512]{1,0:T(8,128)(2,1)S(1)} custom-call(s32[2]{0:T(128)S(1)} %pad_add_fusion.place.refs_0_, bf16[64,640]{1,0:T(8,128)(2,1)S(1)} %collective-permute-done.5.refs_1_.refs_4_, bf16[64,640]{1,0:T(8,128)(2,1)S(1)} %collective-permute-done.6.refs_2_.refs_5_, bf16[3,144,512]{2,1,0:T(8,128)(2,1)S(1)} %copy-done.9, ...), custom_call_target="tpu_custom_call" | custom-call | flops 1644167168 | bytes 3145728 | tf_op jit(solution)/shard_map/attend/pallas_call | solution.py:302
  59.7 1.5 %collective-permute-start.8 = (bf16[144,512]{1,0:T(8,128)(2,1)S(1)}, bf16[144,512]{1,0:T(8,128)(2,1)S(1)}, u32[]{:S(2)}, u32[]{:S(2)}) collective-permute-start(bf16[144,512]{1,0:T(8,128)(2,1)S(1)} %attend.11), channel_id=1, source_target_pairs={{0,64},{32,96},{64,128},{96,160},{128,192},{160,224},{192,0},{224,... | collective-permute-start | bytes 442376 | tf_op jit(solution)/shard_map/ppermute | solution.py:29
  61.2 4.7 %attend.12 = (bf16[144,512]{1,0:T(8,128)(2,1)S(1)}, bf16[144,512]{1,0:T(8,128)(2,1)S(1)}) custom-call(s32[2]{0:T(128)S(1)} %pad_add_fusion.place.refs_0_, bf16[128,640]{1,0:T(8,128)(2,1)S(1)} %collective-permute-done.4.refs_3_.refs_1_, bf16[128,640]{1,0:T(8,128)(2,1)S(1)} %collective-permute-done.7.refs_4_.refs_2_.refs_6_, ...), custom_call_target="tpu_custom_call" | custom-call | flops 3288334336 | bytes 3145728 | tf_op jit(solution)/shard_map/attend/pallas_call | solution.py:302
  65.9 2.8 %collective-permute-start.12 = (bf16[144,512]{1,0:T(8,128)(2,1)S(1)}, bf16[144,512]{1,0:T(8,128)(2,1)S(1)}, u32[]{:S(2)}, u32[]{:S(2)}) collective-permute-start(bf16[144,512]{1,0:T(8,128)(2,1)S(1)} %get-tuple-element.85), channel_id=1, source_target_pairs={{0,192},{32,224},{64,0},{96,32},{128,64},{160,96},{192,128},{224,1... | collective-permute-start | bytes 442376 | tf_op jit(solution)/shard_map/ppermute | solution.py:29
  68.7 0.2 collective-permute-start.11
  68.9 1.5 %collective-permute-done.8.refs_4_ = bf16[144,512]{1,0:T(8,128)(2,1)S(1)} collective-permute-done((bf16[144,512]{1,0:T(8,128)(2,1)S(1)}, bf16[144,512]{1,0:T(8,128)(2,1)S(1)}, u32[]{:S(2)}, u32[]{:S(2)}) %collective-permute-start.8) | collective-permute-done | bytes 147488 | tf_op jit(solution)/shard_map/ppermute | solution.py:29
  70.4 4.7 %attend.13 = (bf16[144,512]{1,0:T(8,128)(2,1)S(1)}, bf16[144,512]{1,0:T(8,128)(2,1)S(1)}) custom-call(s32[2]{0:T(128)S(1)} %pad_add_fusion.place.refs_0_, bf16[128,640]{1,0:T(8,128)(2,1)S(1)} %collective-permute-done.3.refs_1_.refs_2_, bf16[128,640]{1,0:T(8,128)(2,1)S(1)} %collective-permute-done.2.refs_2_.refs_7_, bf16[2,144,512]{2,1,0:T(8,128)(2,1)S(1)} %copy-done.5, ...), custom_call_target="tpu_custom_call" | custom-call | flops 3288334336 | bytes 3145728 | tf_op jit(solution)/shard_map/attend/pallas_call | solution.py:302
  75.1 1.6 %collective-permute-start.9 = (bf16[144,512]{1,0:T(8,128)(2,1)S(1)}, bf16[144,512]{1,0:T(8,128)(2,1)S(1)}, u32[]{:S(2)}, u32[]{:S(2)}) collective-permute-start(bf16[144,512]{1,0:T(8,128)(2,1)S(1)} %get-tuple-element.88), channel_id=1, source_target_pairs={{0,64},{32,96},{64,128},{96,160},{128,192},{160,224},{192,0},{224,... | collective-permute-start | bytes 442376 | tf_op jit(solution)/shard_map/ppermute | solution.py:29
  76.7 2.6 %collective-permute-start.10 = (bf16[144,512]{1,0:T(8,128)(2,1)S(1)}, bf16[144,512]{1,0:T(8,128)(2,1)S(1)}, u32[]{:S(2)}, u32[]{:S(2)}) collective-permute-start(bf16[144,512]{1,0:T(8,128)(2,1)S(1)} %get-tuple-element.89), channel_id=1, source_target_pairs={{0,192},{32,224},{64,0},{96,32},{128,64},{160,96},{192,128},{224,1... | collective-permute-start | bytes 442376 | tf_op jit(solution)/shard_map/ppermute | solution.py:29
  79.3 0.0 collective-permute-done.11.refs_4_
  79.3 0.0 collective-permute-done.12.refs_6_
  79.3 0.0 copy-done.7
  79.4 4.7 %attend.15 = (bf16[144,512]{1,0:T(8,128)(2,1)S(1)}, bf16[144,512]{1,0:T(8,128)(2,1)S(1)}) custom-call(s32[2]{0:T(128)S(1)} %pad_add_fusion.place.refs_0_, bf16[128,640]{1,0:T(8,128)(2,1)S(1)} %collective-permute-done.1.refs_2_.refs_1_, bf16[128,640]{1,0:T(8,128)(2,1)S(1)} %collective-permute-done.refs_3_.refs_8_.refs_2_, bf16[3,144,512]{2,1,0:T(8,128)(2,1)S(1)} %copy-done.7, ...), custom_call_target="tpu_custom_call" | custom-call | flops 3288334336 | bytes 3145728 | tf_op jit(solution)/shard_map/attend/pallas_call | solution.py:302
  84.0 1.5 %collective-permute-start.13 = (bf16[144,512]{1,0:T(8,128)(2,1)S(1)}, bf16[144,512]{1,0:T(8,128)(2,1)S(1)}, u32[]{:S(2)}, u32[]{:S(2)}) collective-permute-start(bf16[144,512]{1,0:T(8,128)(2,1)S(1)} %get-tuple-element.105), channel_id=1, source_target_pairs={{0,32},{32,64},{64,96},{96,128},{128,160},{160,192},{192,224},{224... | collective-permute-start | bytes 442376 | tf_op jit(solution)/shard_map/ppermute | solution.py:29
  85.5 1.8 %collective-permute-start.14 = (bf16[144,512]{1,0:T(8,128)(2,1)S(1)}, bf16[144,512]{1,0:T(8,128)(2,1)S(1)}, u32[]{:S(2)}, u32[]{:S(2)}) collective-permute-start(bf16[144,512]{1,0:T(8,128)(2,1)S(1)} %get-tuple-element.106), channel_id=1, source_target_pairs={{0,224},{32,0},{64,32},{96,64},{128,96},{160,128},{192,160},{224,1... | collective-permute-start | bytes 442376 | tf_op jit(solution)/shard_map/ppermute | solution.py:29
  87.3 0.0 collective-permute-done.10.refs_2_
  87.3 0.0 collective-permute-done.9.refs_1_
  87.3 0.9 windows.1.refs_5_
  88.3 3.0 %attend.14.refs_0_ = bf16[144,512]{1,0:T(8,128)(2,1)S(1)} custom-call(s32[2]{0:T(128)S(1)} %pad_add_fusion.place.refs_0_, bf16[128,640]{1,0:T(8,128)(2,1)S(1)} %get-tuple-element.99.refs_1_.refs_0_, bf16[3,144,512]{2,1,0:T(8,128)(2,1)S(1)} %copy-done.7, bf16[3136,128]{1,0:T(8,128)(2,1)S(1)} %get-tuple-element.81.refs_4_.refs_5_.refs_6_.refs_3_.refs_7_, ...), custom_call_target="tpu_custom_call" | custom-call | flops 1644167168 | bytes 3145728 | tf_op jit(solution)/shard_map/attend/pallas_call | solution.py:302
  91.3 0.0 copy-start
  91.3 0.0 copy-start.1
  91.3 0.0 collective-permute-done.13.refs_3_
  91.3 0.0 collective-permute-done.14.refs_4_
  91.3 0.2 merge.1
  91.6 14.5 %all_to_all.20.new_ref = bf16[8,320,128]{2,1,0:T(8,128)(2,1)S(1)} all-to-all(bf16[8,320,128]{2,1,0:T(8,128)(2,1)S(1)} %merge.1), channel_id=1, replica_groups=mesh['z'=8,'b'=8,'head'=2,'conv'=2] {'b'}, dimensions={0} | all-to-all | bytes 1310720 | tf_op jit(solution)/shard_map/all_to_all | solution.py:503
  106.1 2.0 %finish.1 = (bf16[2,8,4096]{2,1,0:T(8,128)(2,1)}, bf16[2,4,128,512]{3,2,1,0:T(8,128)(2,1)}, bf16[2,4,128,512]{3,2,1,0:T(8,128)(2,1)}) custom-call(s32[2]{0:T(128)S(1)} %pad_add_fusion.place.refs_0_, s32[2]{0:T(128)S(1)} %copy-done.3, s32[2,256]{1,0:T(2,128)S(1)} %copy-done.2, bf16[8,320,128]{2,1,0:T(8,128)(2,1)S(1)} %all_to_all.20.new_ref, ...), custom_call_target="tpu_custom_call" | custom-call | bytes 5242880 | tf_op jit(solution)/shard_map/finish/pallas_call | solution.py:436
  (12 shorter events, 0.0 us)
Async XLA Ops:
  2.3 11.9 %all-to-all-start = ((bf16[8,80,128]{2,1,0:T(8,128)(2,1)}), bf16[8,80,128]{2,1,0:T(8,128)(2,1)S(1)}, u32[]{:S(2)}, u32[]{:S(2)}) async-start(bf16[8,80,128]{2,1,0:T(8,128)(2,1)} %pack_turn.1), calls=%async_computation | async-start | bytes 327680 | tf_op jit(solution)/shard_map/all_to_all | solution.py:456
  14.2 16.1 %all-to-all-start.1 = ((bf16[8,2,1,128,128]{4,3,2,1,0:T(8,128)(2,1)}), bf16[8,2,1,128,128]{4,3,2,1,0:T(8,128)(2,1)S(1)}, u32[]{:S(2)}, u32[]{:S(2)}) async-start(bf16[8,2,1,128,128]{4,3,2,1,0:T(8,128)(2,1)} %get-tuple-element.65), calls=%async_computation.1 | async-start | bytes 1048576 | tf_op jit(solution)/shard_map/all_to_all | solution.py:459
  17.8 20.2 %copy-start.2 = (s32[2,256]{1,0:T(2,128)S(1)}, s32[2,256]{1,0:T(2,128)}, u32[]{:S(2)}) copy-start(s32[2,256]{1,0:T(2,128)} %slots_ref.7) | copy-start | bytes 6148
  17.8 20.2 %copy-start.3 = (s32[2]{0:T(128)S(1)}, s32[2]{0:T(128)}, u32[]{:S(2)}) copy-start(s32[2]{0:T(128)} %lengths.7) | copy-start | bytes 28
  17.8 8.8 %collective-permute-start.1 = (bf16[128,640]{1,0:T(8,128)(2,1)S(1)}, bf16[128,640]{1,0:T(8,128)(2,1)S(1)}, u32[]{:S(2)}, u32[]{:S(2)}) collective-permute-start(bf16[128,640]{1,0:T(8,128)(2,1)S(1)} %get-tuple-element.99.refs_1_.refs_0_), channel_id=1, source_target_pairs={{0,224},{32,0},{64,32},{96,64},{128,96},{160,128},{192,160},{224,1... | collective-permute-start | bytes 491528 | tf_op jit(solution)/shard_map/ppermute | solution.py:29
  23.8 6.5 %collective-permute-start = (bf16[128,640]{1,0:T(8,128)(2,1)S(1)}, bf16[128,640]{1,0:T(8,128)(2,1)S(1)}, u32[]{:S(2)}, u32[]{:S(2)}) collective-permute-start(bf16[128,640]{1,0:T(8,128)(2,1)S(1)} %get-tuple-element.99.refs_1_.refs_0_), channel_id=1, source_target_pairs={{0,32},{32,64},{64,96},{96,128},{128,160},{160,192},{192,224},{224... | collective-permute-start | bytes 491528 | tf_op jit(solution)/shard_map/ppermute | solution.py:29
  30.3 25.3 %all-to-all-start.2 = ((bf16[8,2,3,128,128]{4,3,2,1,0:T(8,128)(2,1)}), bf16[8,2,3,128,128]{4,3,2,1,0:T(8,128)(2,1)S(1)}, u32[]{:S(2)}, u32[]{:S(2)}) async-start(bf16[8,2,3,128,128]{4,3,2,1,0:T(8,128)(2,1)} %get-tuple-element.77), calls=%async_computation.2 | async-start | bytes 3145728 | tf_op jit(solution)/shard_map/all_to_all | solution.py:476
  35.9 6.2 %collective-permute-start.3 = (bf16[128,640]{1,0:T(8,128)(2,1)S(1)}, bf16[128,640]{1,0:T(8,128)(2,1)S(1)}, u32[]{:S(2)}, u32[]{:S(2)}) collective-permute-start(bf16[128,640]{1,0:T(8,128)(2,1)S(1)} %collective-permute-done.1.refs_2_.refs_1_), channel_id=1, source_target_pairs={{0,224},{32,0},{64,32},{96,64},{128,96},{160,128},{192,160},{224,1... | collective-permute-start | bytes 491528 | tf_op jit(solution)/shard_map/ppermute | solution.py:29
  36.2 6.5 %collective-permute-start.2 = (bf16[128,640]{1,0:T(8,128)(2,1)S(1)}, bf16[128,640]{1,0:T(8,128)(2,1)S(1)}, u32[]{:S(2)}, u32[]{:S(2)}) collective-permute-start(bf16[128,640]{1,0:T(8,128)(2,1)S(1)} %collective-permute-done.refs_3_.refs_8_.refs_2_), channel_id=1, source_target_pairs={{0,32},{32,64},{64,96},{96,128},{128,160},{160,192},{192,224},{224... | collective-permute-start | bytes 491528 | tf_op jit(solution)/shard_map/ppermute | solution.py:29
  41.4 0.8 copy-start.6
  42.7 9.6 %collective-permute-start.4 = (bf16[128,640]{1,0:T(8,128)(2,1)S(1)}, bf16[128,640]{1,0:T(8,128)(2,1)S(1)}, u32[]{:S(2)}, u32[]{:S(2)}) collective-permute-start(bf16[128,640]{1,0:T(8,128)(2,1)S(1)} %collective-permute-done.3.refs_1_.refs_2_), channel_id=1, source_target_pairs={{0,224},{32,0},{64,32},{96,64},{128,96},{160,128},{192,160},{224,1... | collective-permute-start | bytes 491528 | tf_op jit(solution)/shard_map/ppermute | solution.py:29
  43.6 8.6 %collective-permute-start.7 = (bf16[128,640]{1,0:T(8,128)(2,1)S(1)}, bf16[128,640]{1,0:T(8,128)(2,1)S(1)}, u32[]{:S(2)}, u32[]{:S(2)}) collective-permute-start(bf16[128,640]{1,0:T(8,128)(2,1)S(1)} %collective-permute-done.2.refs_2_.refs_7_), channel_id=1, source_target_pairs={{0,32},{32,64},{64,96},{96,128},{128,160},{160,192},{192,224},{224... | collective-permute-start | bytes 491528 | tf_op jit(solution)/shard_map/ppermute | solution.py:29
  44.7 7.5 %collective-permute-start.5 = (bf16[64,640]{1,0:T(8,128)(2,1)S(1)}, bf16[64,640]{1,0:T(8,128)(2,1)S(1)}, u32[]{:S(2)}, u32[]{:S(2)}) collective-permute-start(bf16[64,640]{1,0:T(8,128)(2,1)S(1)} %slice.6), channel_id=1, source_target_pairs={{0,64},{32,96},{64,128},{96,160},{128,192},{160,224},{192,0},{224,... | collective-permute-start | bytes 245768 | tf_op jit(solution)/shard_map/ppermute | solution.py:29
  45.2 7.1 %collective-permute-start.6 = (bf16[64,640]{1,0:T(8,128)(2,1)S(1)}, bf16[64,640]{1,0:T(8,128)(2,1)S(1)}, u32[]{:S(2)}, u32[]{:S(2)}) collective-permute-start(bf16[64,640]{1,0:T(8,128)(2,1)S(1)} %slice.7), channel_id=1, source_target_pairs={{0,192},{32,224},{64,0},{96,32},{128,64},{160,96},{192,128},{224,1... | collective-permute-start | bytes 245768 | tf_op jit(solution)/shard_map/ppermute | solution.py:29
  50.9 0.7 copy-start.4
  54.9 0.8 copy-start.8
  55.6 1.0 copy-start.9
  59.7 10.7 %copy-start.5 = (bf16[2,144,512]{2,1,0:T(8,128)(2,1)S(1)}, bf16[2,144,512]{2,1,0:T(8,128)(2,1)}, u32[]{:S(2)}) copy-start(bf16[2,144,512]{2,1,0:T(8,128)(2,1)} %copy-done.4) | copy-start | bytes 884740
  59.7 10.7 %collective-permute-start.8 = (bf16[144,512]{1,0:T(8,128)(2,1)S(1)}, bf16[144,512]{1,0:T(8,128)(2,1)S(1)}, u32[]{:S(2)}, u32[]{:S(2)}) collective-permute-start(bf16[144,512]{1,0:T(8,128)(2,1)S(1)} %attend.11), channel_id=1, source_target_pairs={{0,64},{32,96},{64,128},{96,160},{128,192},{160,224},{192,0},{224,... | collective-permute-start | bytes 442376 | tf_op jit(solution)/shard_map/ppermute | solution.py:29
  65.9 13.5 %collective-permute-start.12 = (bf16[144,512]{1,0:T(8,128)(2,1)S(1)}, bf16[144,512]{1,0:T(8,128)(2,1)S(1)}, u32[]{:S(2)}, u32[]{:S(2)}) collective-permute-start(bf16[144,512]{1,0:T(8,128)(2,1)S(1)} %get-tuple-element.85), channel_id=1, source_target_pairs={{0,192},{32,224},{64,0},{96,32},{128,64},{160,96},{192,128},{224,1... | collective-permute-start | bytes 442376 | tf_op jit(solution)/shard_map/ppermute | solution.py:29
  68.7 10.7 %copy-start.7 = (bf16[3,144,512]{2,1,0:T(8,128)(2,1)S(1)}, bf16[3,144,512]{2,1,0:T(8,128)(2,1)}, u32[]{:S(2)}) copy-start(bf16[3,144,512]{2,1,0:T(8,128)(2,1)} %copy-done.6) | copy-start | bytes 1327108
  68.7 10.7 %collective-permute-start.11 = (bf16[144,512]{1,0:T(8,128)(2,1)S(1)}, bf16[144,512]{1,0:T(8,128)(2,1)S(1)}, u32[]{:S(2)}, u32[]{:S(2)}) collective-permute-start(bf16[144,512]{1,0:T(8,128)(2,1)S(1)} %get-tuple-element.104), channel_id=1, source_target_pairs={{0,64},{32,96},{64,128},{96,160},{128,192},{160,224},{192,0},{224,... | collective-permute-start | bytes 442376 | tf_op jit(solution)/shard_map/ppermute | solution.py:29
  75.1 12.2 %collective-permute-start.9 = (bf16[144,512]{1,0:T(8,128)(2,1)S(1)}, bf16[144,512]{1,0:T(8,128)(2,1)S(1)}, u32[]{:S(2)}, u32[]{:S(2)}) collective-permute-start(bf16[144,512]{1,0:T(8,128)(2,1)S(1)} %get-tuple-element.88), channel_id=1, source_target_pairs={{0,64},{32,96},{64,128},{96,160},{128,192},{160,224},{192,0},{224,... | collective-permute-start | bytes 442376 | tf_op jit(solution)/shard_map/ppermute | solution.py:29
  76.7 10.7 %collective-permute-start.10 = (bf16[144,512]{1,0:T(8,128)(2,1)S(1)}, bf16[144,512]{1,0:T(8,128)(2,1)S(1)}, u32[]{:S(2)}, u32[]{:S(2)}) collective-permute-start(bf16[144,512]{1,0:T(8,128)(2,1)S(1)} %get-tuple-element.89), channel_id=1, source_target_pairs={{0,192},{32,224},{64,0},{96,32},{128,64},{160,96},{192,128},{224,1... | collective-permute-start | bytes 442376 | tf_op jit(solution)/shard_map/ppermute | solution.py:29
  84.0 7.3 %collective-permute-start.13 = (bf16[144,512]{1,0:T(8,128)(2,1)S(1)}, bf16[144,512]{1,0:T(8,128)(2,1)S(1)}, u32[]{:S(2)}, u32[]{:S(2)}) collective-permute-start(bf16[144,512]{1,0:T(8,128)(2,1)S(1)} %get-tuple-element.105), channel_id=1, source_target_pairs={{0,32},{32,64},{64,96},{96,128},{128,160},{160,192},{192,224},{224... | collective-permute-start | bytes 442376 | tf_op jit(solution)/shard_map/ppermute | solution.py:29
  85.5 5.8 %collective-permute-start.14 = (bf16[144,512]{1,0:T(8,128)(2,1)S(1)}, bf16[144,512]{1,0:T(8,128)(2,1)S(1)}, u32[]{:S(2)}, u32[]{:S(2)}) collective-permute-start(bf16[144,512]{1,0:T(8,128)(2,1)S(1)} %get-tuple-element.106), channel_id=1, source_target_pairs={{0,224},{32,0},{64,32},{96,64},{128,96},{160,128},{192,160},{224,1... | collective-permute-start | bytes 442376 | tf_op jit(solution)/shard_map/ppermute | solution.py:29
  91.3 14.8 %copy-start = (bf16[2,4,128,512]{3,2,1,0:T(8,128)(2,1)S(1)}, bf16[2,4,128,512]{3,2,1,0:T(8,128)(2,1)}, u32[]{:S(2)}) copy-start(bf16[2,4,128,512]{3,2,1,0:T(8,128)(2,1)} %k_ref.1) | copy-start | bytes 3145732
  91.3 14.8 %copy-start.1 = (bf16[2,4,128,512]{3,2,1,0:T(8,128)(2,1)S(1)}, bf16[2,4,128,512]{3,2,1,0:T(8,128)(2,1)}, u32[]{:S(2)}) copy-start(bf16[2,4,128,512]{3,2,1,0:T(8,128)(2,1)} %v_ref.1) | copy-start | bytes 3145732
